TPU v7x, 32 devices: a whole 2x2x4 slice. The times are simulated.
32 devices in a mesh: groups: 2 (over x), dp: 2 (over core), tensor: 8 (over z, y).
Axes of the slice: x: 2, y: 2, z: 4, core: 2. Of those that a mesh axis runs over, the one named last changes fastest.
Arguments:
- tokens: bfloat16 [256, 8192], P(('groups', 'dp', 'tensor')), parts along dimension 0, may hold values from -6 to 6
- norm_gain: float32 [8192], replicated, may hold values from 0.25 to 1.75
- gate_weight: bfloat16 [8192, 14336], P(None, ('dp', 'tensor')), may hold values from -0.0625 to 0.0625
- up_weight: bfloat16 [8192, 14336], P(None, ('dp', 'tensor')), may hold values from -0.0625 to 0.0625
- down_weight: bfloat16 [14336, 8192], P(('dp', 'tensor')), may hold values from -0.046875 to 0.046875
Outputs:
- layer_out: bfloat16 [256, 8192], P(('groups', 'dp', 'tensor')), parts along dimension 0
There are 2 independent parts, one for each index of `groups`. A program takes and returns all parts, laid end to end along the dimension named above; an argument that names none is the same for every part. Nothing has to cross between parts.
All inputs are finite; a program needn't handle non-finite values.
Results may differ from a plain program's by a relative error of at most 0.0049.
Values may be sent and summed in bfloat16 or wider, within the bound.
No kernel may reach another device: no remote copies, remote signals or barrier semaphores. Data moves between devices by JAX's collectives and lax.ppermute only.
A program may use at most 128 MiB of HBM per device.

v0:
```python
import jax
import jax.numpy as jnp
from jax import lax
from jax.sharding import PartitionSpec as P


def make_project(gate_slab, up_slab):

    def project(block_rows, offset):
        gate_out = jnp.dot(block_rows, gate_slab, preferred_element_type=jnp.float32)
        up_out = jnp.dot(block_rows, up_slab, preferred_element_type=jnp.float32)
        return (jax.nn.silu(gate_out) * up_out).astype(jnp.bfloat16)

    return project


def make_partial(hidden, down_slab):
    return jnp.dot(hidden, down_slab, preferred_element_type=jnp.float32)


def per_device(tokens, norm_gain, gate_weight, up_weight, down_weight):
    widened = tokens.astype(jnp.float32)
    inv_rms = lax.rsqrt(jnp.mean(widened * widened, axis=-1, keepdims=True) + 1e-05)
    normed = (widened * inv_rms * norm_gain).astype(jnp.bfloat16)
    project = make_project(gate_weight, up_weight)
    hidden = project(lax.all_gather(normed, ("dp", "tensor"), axis=0, tiled=True), jnp.int32(0))
    summed = lax.psum_scatter(
        make_partial(hidden, down_weight), ("dp", "tensor"), scatter_dimension=0, tiled=True
    )
    return (widened + summed).astype(jnp.bfloat16)


def solution(mesh):
    in_specs = (
        P(("groups", "dp", "tensor"), None),
        P(),
        P(None, ("dp", "tensor")),
        P(None, ("dp", "tensor")),
        P(("dp", "tensor"), None),
    )
    out_specs = P(("groups", "dp", "tensor"), None)
    return jax.shard_map(
        per_device, mesh=mesh, in_specs=in_specs, out_specs=out_specs, check_vma=False
    )
```

profile of v0, /device:TPU:0, one launch (start us, length us, event | category | flops | bytes accessed | tf_op | source)
XLA Modules:
  0.0 157.7 jit_solution(14260443349741529989)
XLA Ops:
  6.5 0.0 all-gather.2.cloned.1.call-start
  6.5 1.1 fusion.7
  7.6 1.7 %fusion.9 = bf16[8,8192]{1,0:T(8,128)(2,1)} fusion(bf16[8,8192]{1,0:T(8,128)(2,1)} %param.5, f32[8192]{0:T(1024)} %param.6, f32[8]{0:T(128)S(1)} %add_rsqrt_fusion), kind=kLoop, calls=%fused_computation.13 | loop fusion | flops 262144 | bytes 294944 | tf_op jit(solution)/shard_map/convert_element_type | solution.py:24
  9.3 0.0 all-gather.2.cloned.1.call-update
  9.3 0.0 reduce-scatter.2.cloned.1.call-start
  9.4 44.3 %all-gather.2.cloned.1.call-done = bf16[128,8192]{1,0:T(8,128)(2,1)} async-done(((bf16[8,8192]{1,0:T(8,128)(2,1)}), bf16[128,8192]{1,0:T(8,128)(2,1)}) %all-gather.2.cloned.1.call-update) | async-done | bytes 2097168 | tf_op jit(solution)/shard_map/all_gather | solution.py:26
  53.7 0.0 copy-start
  53.7 8.3 %fusion.13 = f32[128,896]{1,0:T(8,128)S(1)} fusion(bf16[128,8192]{1,0:T(8,128)(2,1)} %all-gather.2.cloned.1.call-done, bf16[8192,896]{1,0:T(8,128)(2,1)} %param.7), kind=kOutput, calls=%fused_computation.18 | convolution fusion | flops 1879048192 | bytes 17235968 | tf_op jit(solution)/shard_map/dot_general | solution.py:10
  62.0 0.0 copy-done
  62.0 0.0 copy-start.1
  62.0 15.9 %fusion.1 = f32[128,8192]{1,0:T(8,128)} fusion(bf16[896,8192]{1,0:T(8,128)(2,1)} %param.9, bf16[128,8192]{1,0:T(8,128)(2,1)S(1)} %copy-done, bf16[8192,896]{1,0:T(8,128)(2,1)} %param.8, f32[128,896]{1,0:T(8,128)S(1)} %fusion.13), kind=kOutput, calls=%fused_computation.2 | convolution fusion | flops 3758784512 | bytes 36110336 | tf_op jit(solution)/shard_map/dot_general | solution.py:18
  77.9 0.0 reduce-scatter.2.cloned.1.call-update
  78.0 71.3 %reduce-scatter.2.cloned.1.call-done = f32[8,8192]{1,0:T(8,128)} async-done(((f32[128,8192]{1,0:T(8,128)}), f32[8,8192]{1,0:T(8,128)}) %reduce-scatter.2.cloned.1.call-update) | async-done | bytes 262160 | tf_op jit(solution)/shard_map/reduce_scatter | solution.py:27
  149.2 0.0 copy-done.1
  149.3 1.6 %fusion.10 = bf16[8,8192]{1,0:T(8,128)(2,1)} fusion(f32[8,8192]{1,0:T(8,128)} %reduce-scatter.2.cloned.1.call-done, bf16[8,8192]{1,0:T(8,128)(2,1)S(1)} %copy-done.1), kind=kLoop, calls=%fused_computation.14 | loop fusion | flops 196608 | bytes 524288 | tf_op jit(solution)/shard_map/convert_element_type | solution.py:30
  (1 shorter events, 0.0 us)
Async XLA Ops:
  6.5 47.2 %all-gather.2.cloned.1.call-start = ((), (), s32[]{:S(2)}) async-start(), calls=%async_computation.1 | async-start | bytes 2228224 | tf_op jit(solution)/shard_map/all_gather | solution.py:26
  9.3 139.9 %reduce-scatter.2.cloned.1.call-start = ((), (), s32[]{:S(2)}) async-start(), calls=%async_computation.2 | async-start | bytes 4456448 | tf_op jit(solution)/shard_map/reduce_scatter | solution.py:27
  53.7 8.3 %copy-start = (bf16[128,8192]{1,0:T(8,128)(2,1)S(1)}, bf16[128,8192]{1,0:T(8,128)(2,1)}, u32[]{:S(2)}) copy-start(bf16[128,8192]{1,0:T(8,128)(2,1)} %all-gather.2.cloned.1.call-done) | copy-start | bytes 6291460
  62.0 87.2 %copy-start.1 = (bf16[8,8192]{1,0:T(8,128)(2,1)S(1)}, bf16[8,8192]{1,0:T(8,128)(2,1)}, u32[]{:S(2)}) copy-start(bf16[8,8192]{1,0:T(8,128)(2,1)} %param.5) | copy-start | bytes 393220
Sparse Core Ops, SparseCore 0:
  9.6 44.0 all-gather.1
  78.1 71.1 reduce-scatter.1
where the time goes:
time: 158 us
  waiting for transfers between devices  116 us (73%)
  matrix products  24.2 us (15%)
  between operations  13.4 us (8%)
  other arithmetic  4.39 us (3%)
    reduce_scatter x1, waiting for transfers between devices, per_device(): lax.psum_scatter(make_partial(hidden, down_weight), ('dp', 'tensor'), sca...  71.3 us
    all_gather x1, waiting for transfers between devices, per_device(): lax.all_gather(normed, ('dp', 'tensor'), axis=0, tiled=True)  44.3 us
    dot_general x1, matrix products, make_partial(): return jnp.dot(hidden, down_slab, preferred_element_type=jnp.float32)  15.9 us
    dot_general x1, matrix products, project(): jnp.dot(block_rows, gate_slab, preferred_element_type=jnp.float32)  8.3 us
  transfers between devices with their start and end apart: 2, of which 2 were waited for; matrix products, arithmetic and copies ran while one was open for 0% of the time, Pallas kernels for 0%

commit v1 on v0

v1 whole, which is shorter than its diff:
```python
import functools

import jax
import jax.numpy as jnp
from jax import lax
from jax.experimental import pallas as pl
from jax.experimental.pallas import tpu as pltpu
from jax.sharding import PartitionSpec as P

BF = jnp.bfloat16
F32 = jnp.float32
N_CHUNKS = 2
PARTS = 4
HELD = 2


def flip(x, axis, size, mask):
    return lax.ppermute(x, axis, [(i, i ^ mask) for i in range(size)])


def norm_rows(tokens, norm_gain):
    widened = tokens.astype(F32)
    inv_rms = lax.rsqrt(jnp.mean(widened * widened, axis=-1, keepdims=True) + 1e-05)
    return (widened * inv_rms * norm_gain).astype(BF)


def vmem_specs(count):
    return [pl.BlockSpec(memory_space=pltpu.VMEM)] * count


def norm_kernel(tokens, gain, out):
    out[...] = norm_rows(tokens[...], gain[...])


def fetch_kernel(part, parts, gate, up, gate_out, up_out, mark, sems):
    depth = gate_out.shape[0]
    copies = [
        pltpu.make_async_copy(src.at[pl.ds(part * depth, depth)], dst, sems.at[i])
        for i, (src, dst) in enumerate([(gate, gate_out), (up, up_out)])
    ]
    for copy in copies:
        copy.start()
    mark[...] = jnp.zeros_like(mark)
    for copy in copies:
        copy.wait()


def fetch(gate, up, part, parts):
    depth, units = gate.shape[0] // parts, gate.shape[1]
    return pl.pallas_call(
        functools.partial(fetch_kernel, part, parts),
        out_shape=[pltpu.VMEM((depth, units), BF)] * 2 + [jax.ShapeDtypeStruct((16, 128), BF)],
        in_specs=[pl.BlockSpec(memory_space=pltpu.HBM)] * 2,
        out_specs=vmem_specs(3),
        scratch_shapes=[pltpu.SemaphoreType.DMA((2,))],
        compiler_params=pltpu.CompilerParams(vmem_limit_bytes=1 * 2**20),
        cost_estimate=pl.CostEstimate(flops=0, bytes_accessed=4 * depth * units, transcendentals=0),
        name=f"fetch_{part}",
    )(hbm(gate), hbm(up))


def hidden_kernel(held, parts, *refs):
    pieces, rest = refs[:16], refs[16:]
    gates, ups, (gate, up, out, gate_late, up_late, sems) = rest[:held], rest[held : 2 * held], rest[2 * held :]
    depth = gate.shape[0] // parts
    copies = []
    for k in range(held, parts):
        for i, (src, dst) in enumerate([(gate, gate_late), (up, up_late)]):
            copies.append(pltpu.make_async_copy(src.at[pl.ds(k * depth, depth)], dst.at[k - held], sems.at[k - held, i]))
            copies[-1].start()
    gate_out = up_out = 0.0
    for k in range(parts):
        rows = jnp.concatenate([p[:, k * depth : (k + 1) * depth] for p in pieces], axis=0)
        if k >= held:
            copies[2 * (k - held)].wait()
            copies[2 * (k - held) + 1].wait()
        gate_block = gates[k][...] if k < held else gate_late[k - held]
        up_block = ups[k][...] if k < held else up_late[k - held]
        gate_out += jnp.dot(rows, gate_block, preferred_element_type=F32)
        up_out += jnp.dot(rows, up_block, preferred_element_type=F32)
    out[...] = (jax.nn.silu(gate_out) * up_out).astype(BF)


def down_kernel(hidden, down, own, other):
    half = own.shape[0]
    part = jnp.dot(hidden[...], down[...], preferred_element_type=F32)
    own[...] = part[:half]
    other[...] = part[half:].astype(BF)


def pair_kernel(chunks, depth, *refs):
    owns, recvs, keeps, sends = refs[:chunks], refs[chunks : 2 * chunks], refs[2 * chunks : 2 * chunks + depth], refs[2 * chunks + depth :]
    rows = keeps[0].shape[0]
    for c in range(chunks):
        step = owns[c].shape[1]
        cols = slice(c * step, (c + 1) * step)
        total = owns[c][...] + recvs[c][...].astype(F32)
        for d in range(depth):
            keeps[d][:, cols] = total[d * rows : (d + 1) * rows]
            sends[d][:, cols] = total[(depth + d) * rows : (depth + d + 1) * rows].astype(BF)


def hbm(x):
    return pltpu.with_memory_space_constraint(x, pltpu.HBM)


def tie(x, mark):
    return x + mark[0, 0]


def pin(x):
    return pltpu.with_memory_space_constraint(x, pltpu.VMEM)


def per_device(tokens, norm_gain, gate_weight, up_weight, down_weight):
    rows, width = tokens.shape
    units = gate_weight.shape[1]
    depth = 4
    normed = pl.pallas_call(
        norm_kernel,
        out_shape=jax.ShapeDtypeStruct((rows, width), BF),
        in_specs=vmem_specs(2),
        out_specs=vmem_specs(1)[0],
        name="norm",
    )(tokens, norm_gain.reshape(1, width))
    z_pieces = [normed] + [flip(normed, "tensor", 8, 2 * d) for d in range(1, depth)]
    fetched = [fetch(gate_weight, up_weight, i, PARTS) for i in range(PARTS)]
    fetched = [fetch(gate_weight, up_weight, i, PARTS) for i in range(HELD)]
    y_pieces = [flip(normed, "tensor", 8, 1)]
    for d in range(1, depth):
        y_pieces.append(flip(tie(z_pieces[d], fetched[min(d, HELD) - 1][2]), "tensor", 8, 1))
    mine = z_pieces + y_pieces
    pieces = mine + [flip(p, "dp", 2, 1) for p in mine]
    late = (PARTS - HELD, width // PARTS, units)
    hidden = pl.pallas_call(
        functools.partial(hidden_kernel, HELD, PARTS),
        out_shape=jax.ShapeDtypeStruct((16 * rows, units), BF),
        in_specs=vmem_specs(16 + 2 * HELD) + [pl.BlockSpec(memory_space=pltpu.HBM)] * 2,
        out_specs=vmem_specs(1)[0],
        scratch_shapes=[pltpu.VMEM(late, BF), pltpu.VMEM(late, BF), pltpu.SemaphoreType.DMA((PARTS - HELD, 2))],
        compiler_params=pltpu.CompilerParams(vmem_limit_bytes=24 * 2**20),
        name="hidden",
    )(*pieces, *[pin(f[0]) for f in fetched], *[pin(f[1]) for f in fetched], hbm(gate_weight), hbm(up_weight))
    step = width // N_CHUNKS
    owns, recvs = [], []
    for c in range(N_CHUNKS):
        own, other = pl.pallas_call(
            down_kernel,
            out_shape=(jax.ShapeDtypeStruct((8 * rows, step), F32), jax.ShapeDtypeStruct((8 * rows, step), BF)),
            grid=(1,),
            in_specs=[pl.BlockSpec((16 * rows, units), lambda i: (0, 0)), pl.BlockSpec((units, step), functools.partial(lambda c, i: (0, c), c))],
            out_specs=(pl.BlockSpec((8 * rows, step), lambda i: (0, 0)),) * 2,
            compiler_params=pltpu.CompilerParams(vmem_limit_bytes=16 * 2**20),
            name="down",
        )(hidden, down_weight)
        owns.append(own)
        recvs.append(flip(other, "dp", 2, 1))
    pairs = pl.pallas_call(
        functools.partial(pair_kernel, N_CHUNKS, depth),
        out_shape=[jax.ShapeDtypeStruct((rows, width), F32)] * depth + [jax.ShapeDtypeStruct((rows, width), BF)] * depth,
        in_specs=vmem_specs(2 * N_CHUNKS),
        out_specs=vmem_specs(2 * depth),
        compiler_params=pltpu.CompilerParams(vmem_limit_bytes=16 * 2**20),
        name="pair",
    )(*owns, *recvs)
    keeps, sends = pairs[:depth], pairs[depth:]
    total = tokens.astype(F32)
    sums = {}
    for d in reversed(range(depth)):
        sums[d] = keeps[d] + flip(sends[d], "tensor", 8, 1).astype(F32)
        if d:
            sums[d] = flip(sums[d].astype(BF), "tensor", 8, 2 * d).astype(F32)
    for d in range(depth):
        total = total + sums[d]
    return total.astype(BF)


def generic_device(tokens, norm_gain, gate_weight, up_weight, down_weight):
    normed = norm_rows(tokens, norm_gain)
    gathered = lax.all_gather(normed, ("dp", "tensor"), axis=0, tiled=True)
    gate_out = jnp.dot(gathered, gate_weight, preferred_element_type=F32)
    up_out = jnp.dot(gathered, up_weight, preferred_element_type=F32)
    hidden = (jax.nn.silu(gate_out) * up_out).astype(BF)
    partial = jnp.dot(hidden, down_weight, preferred_element_type=F32)
    summed = lax.psum_scatter(partial, ("dp", "tensor"), scatter_dimension=0, tiled=True)
    return (tokens.astype(F32) + summed).astype(BF)


def solution(mesh):
    tuned = mesh.shape["dp"] == 2 and mesh.shape["tensor"] == 8
    in_specs = (
        P(("groups", "dp", "tensor"), None),
        P(),
        P(None, ("dp", "tensor")),
        P(None, ("dp", "tensor")),
        P(("dp", "tensor"), None),
    )
    out_specs = P(("groups", "dp", "tensor"), None)
    return jax.shard_map(
        per_device if tuned else generic_device, mesh=mesh, in_specs=in_specs, out_specs=out_specs, check_vma=False
    )
```

time: 158 us -> 69.9 us (0.44)
  waiting for transfers between devices: 116 us -> 26.7 us
  matrix products: 24.2 us -> 0 us
  Pallas kernels: 0 us -> 19.7 us
  starting transfers between devices: 0.04 us -> 19.1 us
  between operations: 13.4 us -> 0.22 us
    reduce_scatter x1 -> x0, waiting for transfers between devices: 71.3 us -> none  [per_device(): lax.psum_scatter(make_partial(hidden, down_weight), ('dp', 'tensor'), sca...]
    all_gather x1 -> x0, waiting for transfers between devices: 44.3 us -> none  [per_device(): lax.all_gather(normed, ('dp', 'tensor'), axis=0, tiled=True)]
    ppermute x0 -> x24, waiting for transfers between devices: none -> 26.7 us  [flip(): return lax.ppermute(x, axis, [(i, i ^ mask) for i in range(size)])]
    dot_general x2 -> x0, matrix products: 24.2 us -> none  [the longest x1 15.9 us: make_partial(): return jnp.dot(hidden, down_slab, preferred_element_type=jnp.float32)]
    pallas_call x0 -> x7, Pallas kernels: none -> 19.7 us  [the longest x1 8.79 us: per_device(): pl.pallas_call(functools.partial(hidden_kernel, HELD, PARTS), out_shape=j...]
    ppermute x0 -> x24, starting transfers between devices: none -> 19.1 us  [flip(): return lax.ppermute(x, axis, [(i, i ^ mask) for i in range(size)])]
    convert_element_type x2 -> x4, other arithmetic: 3.29 us -> 0.82 us  [the longest x1 0.75 us: per_device(): return total.astype(BF)]
    add x0 -> x3, other arithmetic: none -> 2.12 us  [tie(): return x + mark[0, 0]]
  transfers between devices with their start and end apart: 2 -> 24, of which waited for: 2 -> 10; matrix products, arithmetic and copies ran while one was open for 0% -> 5% of each run, Pallas kernels for 0% -> 9%
where the time goes in v1:
time: 69.9 us; the launch traced here: 69.8 us
  waiting for transfers between devices  26.7 us (38%)
  Pallas kernels  19.7 us (28%)
  starting transfers between devices  19.1 us (27%)
  other arithmetic  2.95 us (4%)
  local copies, waits for them, and re-layouts  1.06 us (2%)
    ppermute x24, waiting for transfers between devices, flip(): return lax.ppermute(x, axis, [(i, i ^ mask) for i in range(size)])  26.7 us
    ppermute x24, starting transfers between devices, flip(): return lax.ppermute(x, axis, [(i, i ^ mask) for i in range(size)])  19.1 us
    pallas_call x1, Pallas kernels, per_device(): pl.pallas_call(functools.partial(hidden_kernel, HELD, PARTS), out_shape=j...  8.79 us
    pallas_call x2, Pallas kernels, fetch(): pl.pallas_call(functools.partial(fetch_kernel, part, parts), out_shape=[p...  6.49 us
    pallas_call x2, Pallas kernels, per_device(): pl.pallas_call(down_kernel, out_shape=(jax.ShapeDtypeStruct((8 * rows, st...  2.53 us
    add x3, other arithmetic, tie(): return x + mark[0, 0]  2.12 us
    pallas_call x1, Pallas kernels, per_device(): pl.pallas_call(norm_kernel, out_shape=jax.ShapeDtypeStruct((rows, width),...  1.75 us
  transfers between devices with their start and end apart: 24, of which 10 were waited for; matrix products, arithmetic and copies ran while one was open for 5% of the time, Pallas kernels for 9%

profile of v1, /device:TPU:0, one launch (start us, length us, event | category | flops | bytes accessed | tf_op | source)
XLA Modules:
  0.0 69.8 jit_solution(6623035138449128016)
XLA Ops:
  0.0 1.7 %norm.1.refs_0_ = bf16[8,8192]{1,0:T(8,128)(2,1)} custom-call(bf16[8,8192]{1,0:T(8,128)(2,1)} %tokens.1, f32[1,8192]{1,0:T(1,128)} %bitcast.5), custom_call_target="tpu_custom_call" | custom-call | tf_op jit(solution)/shard_map/norm/pallas_call | solution.py:119
  1.8 3.0 %collective-permute-start = (bf16[8,8192]{1,0:T(8,128)(2,1)}, bf16[8,8192]{1,0:T(8,128)(2,1)S(1)}, u32[]{:S(2)}, u32[]{:S(2)}) collective-permute-start(bf16[8,8192]{1,0:T(8,128)(2,1)} %norm.1.refs_0_), channel_id=1, source_target_pairs={{0,2},{1,3},{2,0},{3,1},{4,6},{5,7},{6,4},{7,5},{8,10},{9,11},{10,... | collective-permute-start | bytes 393224 | tf_op jit(solution)/shard_map/ppermute | solution.py:18
  4.8 0.0 collective-permute-start.7
  4.8 1.5 %collective-permute-start.3 = (bf16[8,8192]{1,0:T(8,128)(2,1)}, bf16[8,8192]{1,0:T(8,128)(2,1)S(1)}, u32[]{:S(2)}, u32[]{:S(2)}) collective-permute-start(bf16[8,8192]{1,0:T(8,128)(2,1)} %norm.1.refs_0_), channel_id=1, source_target_pairs={{0,1},{1,0},{2,3},{3,2},{4,5},{5,4},{6,7},{7,6},{8,9},{9,8},{10,11... | collective-permute-start | bytes 393224 | tf_op jit(solution)/shard_map/ppermute | solution.py:18
  6.3 2.5 %collective-permute-start.2 = (bf16[8,8192]{1,0:T(8,128)(2,1)}, bf16[8,8192]{1,0:T(8,128)(2,1)S(1)}, u32[]{:S(2)}, u32[]{:S(2)}) collective-permute-start(bf16[8,8192]{1,0:T(8,128)(2,1)} %norm.1.refs_0_), channel_id=1, source_target_pairs={{0,6},{1,7},{2,4},{3,5},{4,2},{5,3},{6,0},{7,1},{8,14},{9,15},{10,... | collective-permute-start | bytes 393224 | tf_op jit(solution)/shard_map/ppermute | solution.py:18
  8.8 0.1 collective-permute-start.1
  8.9 3.2 %fetch_0.1 = (bf16[2048,896]{1,0:T(8,128)(2,1)S(1)}, bf16[2048,896]{1,0:T(8,128)(2,1)S(1)}, bf16[16,128]{1,0:T(8,128)(2,1)S(1)}) custom-call(bf16[8192,896]{1,0:T(8,128)(2,1)} %refs_20_.1, bf16[8192,896]{1,0:T(8,128)(2,1)} %refs_21_.1), custom_call_target="tpu_custom_call" | custom-call | bytes 7340032 | tf_op jit(solution)/shard_map/fetch_0/pallas_call | solution.py:50
  12.1 0.0 copy-start
  12.1 0.0 slice-start
  12.1 0.0 slice-start.1
  12.1 3.3 %fetch_1.1 = (bf16[2048,896]{1,0:T(8,128)(2,1)S(1)}, bf16[2048,896]{1,0:T(8,128)(2,1)S(1)}, bf16[16,128]{1,0:T(8,128)(2,1)S(1)}) custom-call(bf16[8192,896]{1,0:T(8,128)(2,1)} %refs_20_.1, bf16[8192,896]{1,0:T(8,128)(2,1)} %refs_21_.1), custom_call_target="tpu_custom_call" | custom-call | bytes 7340032 | tf_op jit(solution)/shard_map/fetch_1/pallas_call | solution.py:50
  15.4 0.5 slice.7
  15.9 0.5 slice.8
  16.5 0.0 collective-permute-done.refs_1_
  16.5 0.9 %broadcast_add_fusion.2 = bf16[8,8192]{1,0:T(8,128)(2,1)S(1)} fusion(bf16[8,8192]{1,0:T(8,128)(2,1)S(1)} %collective-permute-done.refs_1_, bf16[]{:T(256)} %bitcast.1), kind=kLoop, calls=%fused_computation.6 | loop fusion | flops 65536 | bytes 262146 | tf_op jit(solution)/shard_map/add | solution.py:108
  17.3 0.6 collective-permute-start.4
  17.9 3.5 %collective-permute-done.1.refs_2_ = bf16[8,8192]{1,0:T(8,128)(2,1)S(1)} collective-permute-done((bf16[8,8192]{1,0:T(8,128)(2,1)}, bf16[8,8192]{1,0:T(8,128)(2,1)S(1)}, u32[]{:S(2)}, u32[]{:S(2)}) %collective-permute-start.1) | collective-permute-done | bytes 131104 | tf_op jit(solution)/shard_map/ppermute | solution.py:18
  21.4 0.6 broadcast_add_fusion.1
  22.1 0.6 collective-permute-start.5
  22.7 0.0 collective-permute-done.3.refs_4_
  22.7 0.0 collective-permute-start.11
  22.7 0.0 collective-permute-done.2.refs_3_
  22.7 0.5 collective-permute-start.10
  23.2 0.6 broadcast_add_fusion
  23.8 0.0 collective-permute-done.7.refs_8_
  23.8 1.6 %collective-permute-start.6 = (bf16[8,8192]{1,0:T(8,128)(2,1)S(1)}, bf16[8,8192]{1,0:T(8,128)(2,1)S(1)}, u32[]{:S(2)}, u32[]{:S(2)}) collective-permute-start(bf16[8,8192]{1,0:T(8,128)(2,1)S(1)} %broadcast_add_fusion), channel_id=1, source_target_pairs={{0,1},{1,0},{2,3},{3,2},{4,5},{5,4},{6,7},{7,6},{8,9},{9,8},{10,11... | collective-permute-start | bytes 393224 | tf_op jit(solution)/shard_map/ppermute | solution.py:18
  25.4 0.0 collective-permute-done.11.refs_12_
  25.4 0.0 collective-permute-start.9
  25.4 0.0 collective-permute-done.10.refs_11_
  25.4 0.5 collective-permute-start.8
  25.9 0.0 collective-permute-done.4.refs_5_
  25.9 0.1 collective-permute-start.12
  26.0 2.0 %collective-permute-done.5.refs_6_ = bf16[8,8192]{1,0:T(8,128)(2,1)S(1)} collective-permute-done((bf16[8,8192]{1,0:T(8,128)(2,1)S(1)}, bf16[8,8192]{1,0:T(8,128)(2,1)S(1)}, u32[]{:S(2)}, u32[]{:S(2)}) %collective-permute-start.5) | collective-permute-done | bytes 131104 | tf_op jit(solution)/shard_map/ppermute | solution.py:18
  28.0 0.0 collective-permute-start.13
  28.0 2.1 %collective-permute-done.6.refs_7_ = bf16[8,8192]{1,0:T(8,128)(2,1)S(1)} collective-permute-done((bf16[8,8192]{1,0:T(8,128)(2,1)S(1)}, bf16[8,8192]{1,0:T(8,128)(2,1)S(1)}, u32[]{:S(2)}, u32[]{:S(2)}) %collective-permute-start.6) | collective-permute-done | bytes 131104 | tf_op jit(solution)/shard_map/ppermute | solution.py:18
  30.1 0.0 collective-permute-start.14
  30.1 0.0 collective-permute-done.9.refs_10_
  30.1 0.0 collective-permute-done.8.refs_9_
  30.1 0.0 collective-permute-done.12.refs_13_
  30.1 0.0 collective-permute-done.13.refs_14_
  30.1 1.3 %collective-permute-done.14.refs_15_ = bf16[8,8192]{1,0:T(8,128)(2,1)S(1)} collective-permute-done((bf16[8,8192]{1,0:T(8,128)(2,1)S(1)}, bf16[8,8192]{1,0:T(8,128)(2,1)S(1)}, u32[]{:S(2)}, u32[]{:S(2)}) %collective-permute-start.14) | collective-permute-done | bytes 131104 | tf_op jit(solution)/shard_map/ppermute | solution.py:18
  31.4 8.8 %hidden.1 = bf16[128,896]{1,0:T(8,128)(2,1)S(1)} custom-call(bf16[8,8192]{1,0:T(8,128)(2,1)S(1)} %copy-done, bf16[8,8192]{1,0:T(8,128)(2,1)S(1)} %collective-permute-done.refs_1_, bf16[8,8192]{1,0:T(8,128)(2,1)S(1)} %collective-permute-done.1.refs_2_, bf16[8,8192]{1,0:T(8,128)(2,1)S(1)} %collective-permute-done.2.refs_3_, ...), custom_call_target="tpu_custom_call" | custom-call | tf_op jit(solution)/shard_map/hidden/pallas_call | solution.py:135
  40.3 1.3 %down.6 = (f32[64,4096]{1,0:T(8,128)S(1)}, bf16[64,4096]{1,0:T(8,128)(2,1)S(1)}) custom-call(bf16[128,896]{1,0:T(8,128)(2,1)S(1)} %hidden.1, bf16[896,8192]{1,0:T(8,128)(2,1)S(1)} %bitcast.4), custom_call_target="tpu_custom_call" | custom-call | tf_op jit(solution)/shard_map/down/pallas_call | solution.py:147
  41.6 1.3 %down.4 = (f32[64,4096]{1,0:T(8,128)S(1)}, bf16[64,4096]{1,0:T(8,128)(2,1)S(1)}) custom-call(bf16[128,896]{1,0:T(8,128)(2,1)S(1)} %hidden.1, bf16[896,8192]{1,0:T(8,128)(2,1)S(1)} %bitcast.4), custom_call_target="tpu_custom_call" | custom-call | tf_op jit(solution)/shard_map/down/pallas_call | solution.py:147
  42.8 0.0 copy-start.1
  42.8 0.2 collective-permute-start.16
  43.1 0.4 collective-permute-start.15
  43.4 1.4 %collective-permute-done.16.refs_3_ = bf16[64,4096]{1,0:T(8,128)(2,1)S(1)} collective-permute-done((bf16[64,4096]{1,0:T(8,128)(2,1)S(1)}, bf16[64,4096]{1,0:T(8,128)(2,1)S(1)}, u32[]{:S(2)}, u32[]{:S(2)}) %collective-permute-start.16) | collective-permute-done | bytes 524320 | tf_op jit(solution)/shard_map/ppermute | solution.py:18
  44.8 0.7 %collective-permute-done.15.refs_2_ = bf16[64,4096]{1,0:T(8,128)(2,1)S(1)} collective-permute-done((bf16[64,4096]{1,0:T(8,128)(2,1)S(1)}, bf16[64,4096]{1,0:T(8,128)(2,1)S(1)}, u32[]{:S(2)}, u32[]{:S(2)}) %collective-permute-start.15) | collective-permute-done | bytes 524320 | tf_op jit(solution)/shard_map/ppermute | solution.py:18
  45.6 0.2 pair.1
  45.7 0.9 %collective-permute-start.18 = (bf16[8,8192]{1,0:T(8,128)(2,1)S(1)}, bf16[8,8192]{1,0:T(8,128)(2,1)S(1)}, u32[]{:S(2)}, u32[]{:S(2)}) collective-permute-start(bf16[8,8192]{1,0:T(8,128)(2,1)S(1)} %get-tuple-element.36), channel_id=1, source_target_pairs={{0,1},{1,0},{2,3},{3,2},{4,5},{5,4},{6,7},{7,6},{8,9},{9,8},{10,11... | collective-permute-start | bytes 393224 | tf_op jit(solution)/shard_map/ppermute | solution.py:18
  46.6 1.3 %collective-permute-start.17 = (bf16[8,8192]{1,0:T(8,128)(2,1)S(1)}, bf16[8,8192]{1,0:T(8,128)(2,1)S(1)}, u32[]{:S(2)}, u32[]{:S(2)}) collective-permute-start(bf16[8,8192]{1,0:T(8,128)(2,1)S(1)} %get-tuple-element.34), channel_id=1, source_target_pairs={{0,1},{1,0},{2,3},{3,2},{4,5},{5,4},{6,7},{7,6},{8,9},{9,8},{10,11... | collective-permute-start | bytes 393224 | tf_op jit(solution)/shard_map/ppermute | solution.py:18
  47.8 0.8 %collective-permute-start.20 = (bf16[8,8192]{1,0:T(8,128)(2,1)S(1)}, bf16[8,8192]{1,0:T(8,128)(2,1)S(1)}, u32[]{:S(2)}, u32[]{:S(2)}) collective-permute-start(bf16[8,8192]{1,0:T(8,128)(2,1)S(1)} %get-tuple-element.38), channel_id=1, source_target_pairs={{0,1},{1,0},{2,3},{3,2},{4,5},{5,4},{6,7},{7,6},{8,9},{9,8},{10,11... | collective-permute-start | bytes 393224 | tf_op jit(solution)/shard_map/ppermute | solution.py:18
  48.6 1.3 %collective-permute-start.22 = (bf16[8,8192]{1,0:T(8,128)(2,1)S(1)}, bf16[8,8192]{1,0:T(8,128)(2,1)S(1)}, u32[]{:S(2)}, u32[]{:S(2)}) collective-permute-start(bf16[8,8192]{1,0:T(8,128)(2,1)S(1)} %get-tuple-element.40), channel_id=1, source_target_pairs={{0,1},{1,0},{2,3},{3,2},{4,5},{5,4},{6,7},{7,6},{8,9},{9,8},{10,11... | collective-permute-start | bytes 393224 | tf_op jit(solution)/shard_map/ppermute | solution.py:18
  49.9 2.3 %collective-permute-done.18 = bf16[8,8192]{1,0:T(8,128)(2,1)S(1)} collective-permute-done((bf16[8,8192]{1,0:T(8,128)(2,1)S(1)}, bf16[8,8192]{1,0:T(8,128)(2,1)S(1)}, u32[]{:S(2)}, u32[]{:S(2)}) %collective-permute-start.18) | collective-permute-done | bytes 131104 | tf_op jit(solution)/shard_map/ppermute | solution.py:18
  52.2 0.1 collective-permute-start.19
  52.2 5.5 %collective-permute-done.20 = bf16[8,8192]{1,0:T(8,128)(2,1)S(1)} collective-permute-done((bf16[8,8192]{1,0:T(8,128)(2,1)S(1)}, bf16[8,8192]{1,0:T(8,128)(2,1)S(1)}, u32[]{:S(2)}, u32[]{:S(2)}) %collective-permute-start.20) | collective-permute-done | bytes 131104 | tf_op jit(solution)/shard_map/ppermute | solution.py:18
  57.8 0.9 %collective-permute-start.21 = (bf16[8,8192]{1,0:T(8,128)(2,1)S(1)}, bf16[8,8192]{1,0:T(8,128)(2,1)S(1)}, u32[]{:S(2)}, u32[]{:S(2)}) collective-permute-start(bf16[8,8192]{1,0:T(8,128)(2,1)S(1)} %add_convert_fusion.2), channel_id=1, source_target_pairs={{0,4},{1,5},{2,6},{3,7},{4,0},{5,1},{6,2},{7,3},{8,12},{9,13},{10,... | collective-permute-start | bytes 393224 | tf_op jit(solution)/shard_map/ppermute | solution.py:18
  58.7 1.1 %collective-permute-done.22 = bf16[8,8192]{1,0:T(8,128)(2,1)S(1)} collective-permute-done((bf16[8,8192]{1,0:T(8,128)(2,1)S(1)}, bf16[8,8192]{1,0:T(8,128)(2,1)S(1)}, u32[]{:S(2)}, u32[]{:S(2)}) %collective-permute-start.22) | collective-permute-done | bytes 131104 | tf_op jit(solution)/shard_map/ppermute | solution.py:18
  59.8 2.5 %collective-permute-start.23 = (bf16[8,8192]{1,0:T(8,128)(2,1)S(1)}, bf16[8,8192]{1,0:T(8,128)(2,1)S(1)}, u32[]{:S(2)}, u32[]{:S(2)}) collective-permute-start(bf16[8,8192]{1,0:T(8,128)(2,1)S(1)} %add_convert_fusion.1), channel_id=1, source_target_pairs={{0,6},{1,7},{2,4},{3,5},{4,2},{5,3},{6,0},{7,1},{8,14},{9,15},{10,... | collective-permute-start | bytes 393224 | tf_op jit(solution)/shard_map/ppermute | solution.py:18
  62.3 0.0 collective-permute-done.17
  62.3 6.7 %collective-permute-done.21 = bf16[8,8192]{1,0:T(8,128)(2,1)S(1)} collective-permute-done((bf16[8,8192]{1,0:T(8,128)(2,1)S(1)}, bf16[8,8192]{1,0:T(8,128)(2,1)S(1)}, u32[]{:S(2)}, u32[]{:S(2)}) %collective-permute-start.21) | collective-permute-done | bytes 131104 | tf_op jit(solution)/shard_map/ppermute | solution.py:18
  69.0 0.0 collective-permute-done.23
  69.0 0.8 %add_convert_fusion = bf16[8,8192]{1,0:T(8,128)(2,1)} fusion(bf16[8,8192]{1,0:T(8,128)(2,1)S(1)} %collective-permute-done.23, bf16[8,8192]{1,0:T(8,128)(2,1)S(1)} %collective-permute-done.21, bf16[8,8192]{1,0:T(8,128)(2,1)S(1)} %collective-permute-done.19, f32[8,8192]{1,0:T(8,128)S(1)} %get-tuple-element.33, bf16[8,8192]{1,0:T(8,128)(2,1)S(1)} %collective-permute-done.17, ...), kind=kLoop, calls=%fused_computation | loop fusion | flops 720896 | bytes 1048576 | tf_op jit(solution)/shard_map/convert_element_type | solution.py:175
  (13 shorter events, 0.1 us)
Async XLA Ops:
  1.8 14.7 %collective-permute-start = (bf16[8,8192]{1,0:T(8,128)(2,1)}, bf16[8,8192]{1,0:T(8,128)(2,1)S(1)}, u32[]{:S(2)}, u32[]{:S(2)}) collective-permute-start(bf16[8,8192]{1,0:T(8,128)(2,1)} %norm.1.refs_0_), channel_id=1, source_target_pairs={{0,2},{1,3},{2,0},{3,1},{4,6},{5,7},{6,4},{7,5},{8,10},{9,11},{10,... | collective-permute-start | bytes 393224 | tf_op jit(solution)/shard_map/ppermute | solution.py:18
  4.8 19.0 %collective-permute-start.7 = (bf16[8,8192]{1,0:T(8,128)(2,1)}, bf16[8,8192]{1,0:T(8,128)(2,1)S(1)}, u32[]{:S(2)}, u32[]{:S(2)}) collective-permute-start(bf16[8,8192]{1,0:T(8,128)(2,1)} %norm.1.refs_0_), channel_id=1, source_target_pairs={{0,8},{8,0},{1,9},{9,1},{2,10},{10,2},{3,11},{11,3},{4,12},{12,4},... | collective-permute-start | bytes 393224 | tf_op jit(solution)/shard_map/ppermute | solution.py:18
  4.8 17.9 %collective-permute-start.3 = (bf16[8,8192]{1,0:T(8,128)(2,1)}, bf16[8,8192]{1,0:T(8,128)(2,1)S(1)}, u32[]{:S(2)}, u32[]{:S(2)}) collective-permute-start(bf16[8,8192]{1,0:T(8,128)(2,1)} %norm.1.refs_0_), channel_id=1, source_target_pairs={{0,1},{1,0},{2,3},{3,2},{4,5},{5,4},{6,7},{7,6},{8,9},{9,8},{10,11... | collective-permute-start | bytes 393224 | tf_op jit(solution)/shard_map/ppermute | solution.py:18
  6.3 16.4 %collective-permute-start.2 = (bf16[8,8192]{1,0:T(8,128)(2,1)}, bf16[8,8192]{1,0:T(8,128)(2,1)S(1)}, u32[]{:S(2)}, u32[]{:S(2)}) collective-permute-start(bf16[8,8192]{1,0:T(8,128)(2,1)} %norm.1.refs_0_), channel_id=1, source_target_pairs={{0,6},{1,7},{2,4},{3,5},{4,2},{5,3},{6,0},{7,1},{8,14},{9,15},{10,... | collective-permute-start | bytes 393224 | tf_op jit(solution)/shard_map/ppermute | solution.py:18
  8.8 12.7 %collective-permute-start.1 = (bf16[8,8192]{1,0:T(8,128)(2,1)}, bf16[8,8192]{1,0:T(8,128)(2,1)S(1)}, u32[]{:S(2)}, u32[]{:S(2)}) collective-permute-start(bf16[8,8192]{1,0:T(8,128)(2,1)} %norm.1.refs_0_), channel_id=1, source_target_pairs={{0,4},{1,5},{2,6},{3,7},{4,0},{5,1},{6,2},{7,3},{8,12},{9,13},{10,... | collective-permute-start | bytes 393224 | tf_op jit(solution)/shard_map/ppermute | solution.py:18
  12.1 19.4 %copy-start = (bf16[8,8192]{1,0:T(8,128)(2,1)S(1)}, bf16[8,8192]{1,0:T(8,128)(2,1)}, u32[]{:S(2)}) copy-start(bf16[8,8192]{1,0:T(8,128)(2,1)} %norm.1.refs_0_) | copy-start | bytes 393220
  12.1 28.2 %slice-start = ((s8[14680064]{0:T(1024)(128)(4,1)}), s8[4194304]{0:T(1024)(128)(4,1)S(1)}, s32[]{:S(2)}) async-start(s8[14680064]{0:T(1024)(128)(4,1)} %bitcast.3), calls=%async_computation | async-start | bytes 8388608
  12.1 28.2 %slice-start.1 = ((s8[14680064]{0:T(1024)(128)(4,1)}), s8[4194304]{0:T(1024)(128)(4,1)S(1)}, s32[]{:S(2)}) async-start(s8[14680064]{0:T(1024)(128)(4,1)} %bitcast.3), calls=%async_computation.1 | async-start | bytes 8388608
  17.3 8.6 %collective-permute-start.4 = (bf16[8,8192]{1,0:T(8,128)(2,1)S(1)}, bf16[8,8192]{1,0:T(8,128)(2,1)S(1)}, u32[]{:S(2)}, u32[]{:S(2)}) collective-permute-start(bf16[8,8192]{1,0:T(8,128)(2,1)S(1)} %broadcast_add_fusion.2), channel_id=1, source_target_pairs={{0,1},{1,0},{2,3},{3,2},{4,5},{5,4},{6,7},{7,6},{8,9},{9,8},{10,11... | collective-permute-start | bytes 393224 | tf_op jit(solution)/shard_map/ppermute | solution.py:18
  22.1 5.9 %collective-permute-start.5 = (bf16[8,8192]{1,0:T(8,128)(2,1)S(1)}, bf16[8,8192]{1,0:T(8,128)(2,1)S(1)}, u32[]{:S(2)}, u32[]{:S(2)}) collective-permute-start(bf16[8,8192]{1,0:T(8,128)(2,1)S(1)} %broadcast_add_fusion.1), channel_id=1, source_target_pairs={{0,1},{1,0},{2,3},{3,2},{4,5},{5,4},{6,7},{7,6},{8,9},{9,8},{10,11... | collective-permute-start | bytes 393224 | tf_op jit(solution)/shard_map/ppermute | solution.py:18
  22.7 2.8 %collective-permute-start.11 = (bf16[8,8192]{1,0:T(8,128)(2,1)S(1)}, bf16[8,8192]{1,0:T(8,128)(2,1)S(1)}, u32[]{:S(2)}, u32[]{:S(2)}) collective-permute-start(bf16[8,8192]{1,0:T(8,128)(2,1)S(1)} %collective-permute-done.3.refs_4_), channel_id=1, source_target_pairs={{0,8},{8,0},{1,9},{9,1},{2,10},{10,2},{3,11},{11,3},{4,12},{12,4},... | collective-permute-start | bytes 393224 | tf_op jit(solution)/shard_map/ppermute | solution.py:18
  22.7 2.8 %collective-permute-start.10 = (bf16[8,8192]{1,0:T(8,128)(2,1)S(1)}, bf16[8,8192]{1,0:T(8,128)(2,1)S(1)}, u32[]{:S(2)}, u32[]{:S(2)}) collective-permute-start(bf16[8,8192]{1,0:T(8,128)(2,1)S(1)} %collective-permute-done.2.refs_3_), channel_id=1, source_target_pairs={{0,8},{8,0},{1,9},{9,1},{2,10},{10,2},{3,11},{11,3},{4,12},{12,4},... | collective-permute-start | bytes 393224 | tf_op jit(solution)/shard_map/ppermute | solution.py:18
  23.8 6.3 %collective-permute-start.6 = (bf16[8,8192]{1,0:T(8,128)(2,1)S(1)}, bf16[8,8192]{1,0:T(8,128)(2,1)S(1)}, u32[]{:S(2)}, u32[]{:S(2)}) collective-permute-start(bf16[8,8192]{1,0:T(8,128)(2,1)S(1)} %broadcast_add_fusion), channel_id=1, source_target_pairs={{0,1},{1,0},{2,3},{3,2},{4,5},{5,4},{6,7},{7,6},{8,9},{9,8},{10,11... | collective-permute-start | bytes 393224 | tf_op jit(solution)/shard_map/ppermute | solution.py:18
  25.4 4.7 %collective-permute-start.9 = (bf16[8,8192]{1,0:T(8,128)(2,1)S(1)}, bf16[8,8192]{1,0:T(8,128)(2,1)S(1)}, u32[]{:S(2)}, u32[]{:S(2)}) collective-permute-start(bf16[8,8192]{1,0:T(8,128)(2,1)S(1)} %collective-permute-done.1.refs_2_), channel_id=1, source_target_pairs={{0,8},{8,0},{1,9},{9,1},{2,10},{10,2},{3,11},{11,3},{4,12},{12,4},... | collective-permute-start | bytes 393224 | tf_op jit(solution)/shard_map/ppermute | solution.py:18
  25.4 4.7 %collective-permute-start.8 = (bf16[8,8192]{1,0:T(8,128)(2,1)S(1)}, bf16[8,8192]{1,0:T(8,128)(2,1)S(1)}, u32[]{:S(2)}, u32[]{:S(2)}) collective-permute-start(bf16[8,8192]{1,0:T(8,128)(2,1)S(1)} %collective-permute-done.refs_1_), channel_id=1, source_target_pairs={{0,8},{8,0},{1,9},{9,1},{2,10},{10,2},{3,11},{11,3},{4,12},{12,4},... | collective-permute-start | bytes 393224 | tf_op jit(solution)/shard_map/ppermute | solution.py:18
  25.9 4.2 %collective-permute-start.12 = (bf16[8,8192]{1,0:T(8,128)(2,1)S(1)}, bf16[8,8192]{1,0:T(8,128)(2,1)S(1)}, u32[]{:S(2)}, u32[]{:S(2)}) collective-permute-start(bf16[8,8192]{1,0:T(8,128)(2,1)S(1)} %collective-permute-done.4.refs_5_), channel_id=1, source_target_pairs={{0,8},{8,0},{1,9},{9,1},{2,10},{10,2},{3,11},{11,3},{4,12},{12,4},... | collective-permute-start | bytes 393224 | tf_op jit(solution)/shard_map/ppermute | solution.py:18
  28.0 2.1 %collective-permute-start.13 = (bf16[8,8192]{1,0:T(8,128)(2,1)S(1)}, bf16[8,8192]{1,0:T(8,128)(2,1)S(1)}, u32[]{:S(2)}, u32[]{:S(2)}) collective-permute-start(bf16[8,8192]{1,0:T(8,128)(2,1)S(1)} %collective-permute-done.5.refs_6_), channel_id=1, source_target_pairs={{0,8},{8,0},{1,9},{9,1},{2,10},{10,2},{3,11},{11,3},{4,12},{12,4},... | collective-permute-start | bytes 393224 | tf_op jit(solution)/shard_map/ppermute | solution.py:18
  30.1 1.3 %collective-permute-start.14 = (bf16[8,8192]{1,0:T(8,128)(2,1)S(1)}, bf16[8,8192]{1,0:T(8,128)(2,1)S(1)}, u32[]{:S(2)}, u32[]{:S(2)}) collective-permute-start(bf16[8,8192]{1,0:T(8,128)(2,1)S(1)} %collective-permute-done.6.refs_7_), channel_id=1, source_target_pairs={{0,8},{8,0},{1,9},{9,1},{2,10},{10,2},{3,11},{11,3},{4,12},{12,4},... | collective-permute-start | bytes 393224 | tf_op jit(solution)/shard_map/ppermute | solution.py:18
  31.4 8.8 %slice-start.2 = ((s8[14680064]{0:T(1024)(128)(4,1)}), s8[4194304]{0:T(1024)(128)(4,1)S(1)}, s32[]{:S(2)}) async-start(s8[14680064]{0:T(1024)(128)(4,1)} %bitcast.3), calls=%async_computation.2 | async-start | bytes 8388608
  31.4 8.8 %slice-start.3 = ((s8[14680064]{0:T(1024)(128)(4,1)}), s8[2097152]{0:T(1024)(128)(4,1)S(1)}, s32[]{:S(2)}) async-start(s8[14680064]{0:T(1024)(128)(4,1)} %bitcast.3), calls=%async_computation.3 | async-start | bytes 4194304
  42.8 26.2 %copy-start.1 = (bf16[8,8192]{1,0:T(8,128)(2,1)S(1)}, bf16[8,8192]{1,0:T(8,128)(2,1)}, u32[]{:S(2)}) copy-start(bf16[8,8192]{1,0:T(8,128)(2,1)} %tokens.1) | copy-start | bytes 393220
  42.8 2.0 %collective-permute-start.16 = (bf16[64,4096]{1,0:T(8,128)(2,1)S(1)}, bf16[64,4096]{1,0:T(8,128)(2,1)S(1)}, u32[]{:S(2)}, u32[]{:S(2)}) collective-permute-start(bf16[64,4096]{1,0:T(8,128)(2,1)S(1)} %get-tuple-element.32), channel_id=1, source_target_pairs={{0,8},{8,0},{1,9},{9,1},{2,10},{10,2},{3,11},{11,3},{4,12},{12,4},... | collective-permute-start | bytes 1572872 | tf_op jit(solution)/shard_map/ppermute | solution.py:18
  43.1 2.5 %collective-permute-start.15 = (bf16[64,4096]{1,0:T(8,128)(2,1)S(1)}, bf16[64,4096]{1,0:T(8,128)(2,1)S(1)}, u32[]{:S(2)}, u32[]{:S(2)}) collective-permute-start(bf16[64,4096]{1,0:T(8,128)(2,1)S(1)} %get-tuple-element.31), channel_id=1, source_target_pairs={{0,8},{8,0},{1,9},{9,1},{2,10},{10,2},{3,11},{11,3},{4,12},{12,4},... | collective-permute-start | bytes 1572872 | tf_op jit(solution)/shard_map/ppermute | solution.py:18
  45.7 6.4 %collective-permute-start.18 = (bf16[8,8192]{1,0:T(8,128)(2,1)S(1)}, bf16[8,8192]{1,0:T(8,128)(2,1)S(1)}, u32[]{:S(2)}, u32[]{:S(2)}) collective-permute-start(bf16[8,8192]{1,0:T(8,128)(2,1)S(1)} %get-tuple-element.36), channel_id=1, source_target_pairs={{0,1},{1,0},{2,3},{3,2},{4,5},{5,4},{6,7},{7,6},{8,9},{9,8},{10,11... | collective-permute-start | bytes 393224 | tf_op jit(solution)/shard_map/ppermute | solution.py:18
  46.6 15.7 %collective-permute-start.17 = (bf16[8,8192]{1,0:T(8,128)(2,1)S(1)}, bf16[8,8192]{1,0:T(8,128)(2,1)S(1)}, u32[]{:S(2)}, u32[]{:S(2)}) collective-permute-start(bf16[8,8192]{1,0:T(8,128)(2,1)S(1)} %get-tuple-element.34), channel_id=1, source_target_pairs={{0,1},{1,0},{2,3},{3,2},{4,5},{5,4},{6,7},{7,6},{8,9},{9,8},{10,11... | collective-permute-start | bytes 393224 | tf_op jit(solution)/shard_map/ppermute | solution.py:18
  47.8 9.9 %collective-permute-start.20 = (bf16[8,8192]{1,0:T(8,128)(2,1)S(1)}, bf16[8,8192]{1,0:T(8,128)(2,1)S(1)}, u32[]{:S(2)}, u32[]{:S(2)}) collective-permute-start(bf16[8,8192]{1,0:T(8,128)(2,1)S(1)} %get-tuple-element.38), channel_id=1, source_target_pairs={{0,1},{1,0},{2,3},{3,2},{4,5},{5,4},{6,7},{7,6},{8,9},{9,8},{10,11... | collective-permute-start | bytes 393224 | tf_op jit(solution)/shard_map/ppermute | solution.py:18
  48.6 11.2 %collective-permute-start.22 = (bf16[8,8192]{1,0:T(8,128)(2,1)S(1)}, bf16[8,8192]{1,0:T(8,128)(2,1)S(1)}, u32[]{:S(2)}, u32[]{:S(2)}) collective-permute-start(bf16[8,8192]{1,0:T(8,128)(2,1)S(1)} %get-tuple-element.40), channel_id=1, source_target_pairs={{0,1},{1,0},{2,3},{3,2},{4,5},{5,4},{6,7},{7,6},{8,9},{9,8},{10,11... | collective-permute-start | bytes 393224 | tf_op jit(solution)/shard_map/ppermute | solution.py:18
  52.2 10.2 %collective-permute-start.19 = (bf16[8,8192]{1,0:T(8,128)(2,1)S(1)}, bf16[8,8192]{1,0:T(8,128)(2,1)S(1)}, u32[]{:S(2)}, u32[]{:S(2)}) collective-permute-start(bf16[8,8192]{1,0:T(8,128)(2,1)S(1)} %add_convert_fusion.3), channel_id=1, source_target_pairs={{0,2},{1,3},{2,0},{3,1},{4,6},{5,7},{6,4},{7,5},{8,10},{9,11},{10,... | collective-permute-start | bytes 393224 | tf_op jit(solution)/shard_map/ppermute | solution.py:18
  57.8 11.2 %collective-permute-start.21 = (bf16[8,8192]{1,0:T(8,128)(2,1)S(1)}, bf16[8,8192]{1,0:T(8,128)(2,1)S(1)}, u32[]{:S(2)}, u32[]{:S(2)}) collective-permute-start(bf16[8,8192]{1,0:T(8,128)(2,1)S(1)} %add_convert_fusion.2), channel_id=1, source_target_pairs={{0,4},{1,5},{2,6},{3,7},{4,0},{5,1},{6,2},{7,3},{8,12},{9,13},{10,... | collective-permute-start | bytes 393224 | tf_op jit(solution)/shard_map/ppermute | solution.py:18
  59.8 9.2 %collective-permute-start.23 = (bf16[8,8192]{1,0:T(8,128)(2,1)S(1)}, bf16[8,8192]{1,0:T(8,128)(2,1)S(1)}, u32[]{:S(2)}, u32[]{:S(2)}) collective-permute-start(bf16[8,8192]{1,0:T(8,128)(2,1)S(1)} %add_convert_fusion.1), channel_id=1, source_target_pairs={{0,6},{1,7},{2,4},{3,5},{4,2},{5,3},{6,0},{7,1},{8,14},{9,15},{10,... | collective-permute-start | bytes 393224 | tf_op jit(solution)/shard_map/ppermute | solution.py:18

commit v2 on v1

v2 whole, which is shorter than its diff:
```python
import functools

import jax
import jax.numpy as jnp
from jax import lax
from jax.experimental import pallas as pl
from jax.experimental.pallas import tpu as pltpu
from jax.sharding import PartitionSpec as P

BF = jnp.bfloat16
F32 = jnp.float32
N_CHUNKS = 2
COST = 4
FETCHES = (4, 2)
CHUNK = 1024
ORDER = (0, 2, 3, 6, 1, 5, 7, 4)


def flip(x, axis, size, mask):
    return lax.ppermute(x, axis, [(i, i ^ mask) for i in range(size)])


def norm_rows(tokens, norm_gain):
    widened = tokens.astype(F32)
    inv_rms = lax.rsqrt(jnp.mean(widened * widened, axis=-1, keepdims=True) + 1e-05)
    return (widened * inv_rms * norm_gain).astype(BF)


def vmem_specs(count):
    return [pl.BlockSpec(memory_space=pltpu.VMEM)] * count


def norm_kernel(tokens, gain, out):
    out[...] = norm_rows(tokens[...], gain[...])


def fetch_kernel(first, after, *refs):
    gate, up = refs[:2]
    gate_out, up_out, mark, sems = refs[2 + after :]
    depth = gate_out.shape[0]
    copies = [
        pltpu.make_async_copy(src.at[pl.ds(first, depth)], dst, sems.at[i])
        for i, (src, dst) in enumerate([(gate, gate_out), (up, up_out)])
    ]
    for copy in copies:
        copy.start()
    mark[...] = jnp.zeros_like(mark)
    for copy in copies:
        copy.wait()


def fetch(gate, up, first, depth, shape, after):
    units = gate.shape[1]
    return pl.pallas_call(
        functools.partial(fetch_kernel, first, len(after)),
        out_shape=[pltpu.VMEM((depth, units), BF)] * 2 + [pltpu.VMEM(shape, BF)],
        in_specs=[pl.BlockSpec(memory_space=pltpu.HBM)] * 2 + [pl.BlockSpec(memory_space=pl.ANY)] * len(after),
        out_specs=vmem_specs(3),
        scratch_shapes=[pltpu.SemaphoreType.DMA((2,))],
        compiler_params=pltpu.CompilerParams(vmem_limit_bytes=1 * 2**20),
        cost_estimate=pl.CostEstimate(flops=0, bytes_accessed=COST * depth * units, transcendentals=0),
        name=f"fetch_{first}",
    )(hbm(gate), hbm(up), *after)


def hidden_kernel(held, *refs):
    pieces, rest = refs[:16], refs[16:]
    gates, ups, (gate, up, out, gate_late, up_late, sems) = rest[:held], rest[held : 2 * held], rest[2 * held :]
    late, depth = gate_late.shape[:2]
    base = gate.shape[0] - late * depth
    copies = []
    for k in range(late):
        for i, (src, dst) in enumerate([(gate, gate_late), (up, up_late)]):
            copies.append(pltpu.make_async_copy(src.at[pl.ds(base + k * depth, depth)], dst.at[k], sems.at[k, i]))
            copies[-1].start()
    gate_out = up_out = 0.0
    first = 0
    for k in range(held + late):
        size = gates[k].shape[0] if k < held else depth
        rows = jnp.concatenate([p[:, first : first + size] for p in pieces], axis=0)
        if k >= held:
            copies[2 * (k - held)].wait()
            copies[2 * (k - held) + 1].wait()
        gate_block = gates[k][...] if k < held else gate_late[k - held]
        up_block = ups[k][...] if k < held else up_late[k - held]
        gate_out += jnp.dot(rows, gate_block, preferred_element_type=F32)
        up_out += jnp.dot(rows, up_block, preferred_element_type=F32)
        first += size
    out[...] = (jax.nn.silu(gate_out) * up_out).astype(BF)


def down_kernel(hidden, down, own, other):
    half = own.shape[0]
    part = jnp.dot(hidden[...], down[...], preferred_element_type=F32)
    own[...] = part[:half]
    other[...] = part[half:].astype(BF)


def pair_kernel(chunks, *refs):
    owns, recvs, outs = refs[:chunks], refs[chunks : 2 * chunks], refs[2 * chunks :]
    rows = outs[0].shape[0]
    for c in range(chunks):
        step = owns[c].shape[1]
        total = owns[c][...] + recvs[c][...].astype(F32)
        for d, out in enumerate(outs):
            out[:, c * step : (c + 1) * step] = total[d * rows : (d + 1) * rows].astype(out.dtype)


def hbm(x):
    return pltpu.with_memory_space_constraint(x, pltpu.HBM)


def tie(x, mark):
    return x + mark


def pin(x):
    return pltpu.with_memory_space_constraint(x, pltpu.VMEM)


def per_device(tokens, norm_gain, gate_weight, up_weight, down_weight):
    rows, width = tokens.shape
    units = gate_weight.shape[1]
    normed = pl.pallas_call(
        norm_kernel,
        out_shape=pltpu.VMEM((rows, width), BF),
        in_specs=vmem_specs(2),
        out_specs=vmem_specs(1)[0],
        name="norm",
    )(tokens, norm_gain.reshape(1, width))

    def hop(x, mask):
        return flip(x, "tensor", 8, mask)

    sizes = [CHUNK * n for n in FETCHES]
    at1, at2, at4 = hop(normed, 1), hop(normed, 2), hop(normed, 4)
    early = fetch(gate_weight, up_weight, 0, sizes[0], tokens.shape, [at1, at2])
    at4t = tie(at4, early[2])
    at7, at3 = hop(at1, 6), hop(at2, 1)
    at6, at5 = hop(at4t, 2), hop(at4t, 1)
    later = fetch(gate_weight, up_weight, sizes[0], sizes[1], tokens.shape, [at4])
    mine = [normed, at1, at2, at4]
    last = [at7, at3, at6, at5]
    pieces = mine + last
    pieces += [flip(p, "dp", 2, 1) for p in mine + [tie(p, later[2]) for p in last]]
    held = [early, later]
    pieces = [pieces[i] for i in ORDER] + [pieces[8 + i] for i in ORDER]
    late = ((width - sum(sizes)) // CHUNK, CHUNK, units)
    hidden = pl.pallas_call(
        functools.partial(hidden_kernel, len(held)),
        out_shape=jax.ShapeDtypeStruct((16 * rows, units), BF),
        in_specs=vmem_specs(16 + 2 * len(held)) + [pl.BlockSpec(memory_space=pltpu.HBM)] * 2,
        out_specs=vmem_specs(1)[0],
        scratch_shapes=[pltpu.VMEM(late, BF), pltpu.VMEM(late, BF), pltpu.SemaphoreType.DMA((late[0], 2))],
        compiler_params=pltpu.CompilerParams(vmem_limit_bytes=24 * 2**20),
        name="hidden",
    )(*pieces, *[pin(f[0]) for f in held], *[pin(f[1]) for f in held], hbm(gate_weight), hbm(up_weight))
    step = width // N_CHUNKS
    owns, recvs = [], []
    for c in range(N_CHUNKS):
        own, other = pl.pallas_call(
            down_kernel,
            out_shape=(jax.ShapeDtypeStruct((8 * rows, step), F32), jax.ShapeDtypeStruct((8 * rows, step), BF)),
            grid=(1,),
            in_specs=[pl.BlockSpec((16 * rows, units), lambda i: (0, 0)), pl.BlockSpec((units, step), functools.partial(lambda c, i: (0, c), c))],
            out_specs=(pl.BlockSpec((8 * rows, step), lambda i: (0, 0)),) * 2,
            compiler_params=pltpu.CompilerParams(vmem_limit_bytes=16 * 2**20),
            name="down",
        )(hidden, down_weight)
        owns.append(own)
        recvs.append(flip(other, "dp", 2, 1))
    kinds = [F32, F32, F32, BF, F32, BF, BF, BF]
    own0, own1, own2, own3, far0, far1, far2, far3 = pl.pallas_call(
        functools.partial(pair_kernel, N_CHUNKS),
        out_shape=[jax.ShapeDtypeStruct((rows, width), kind) for kind in kinds],
        in_specs=vmem_specs(2 * N_CHUNKS),
        out_specs=vmem_specs(8),
        compiler_params=pltpu.CompilerParams(vmem_limit_bytes=16 * 2**20),
        name="pair",
    )(*owns, *recvs)

    def send(x, mask):
        return flip(x.astype(BF), "tensor", 8, mask).astype(F32)

    sum2 = own2 + send(far2, 1) + send(own3, 2)
    sum0 = far0 + send(far3, 6)
    sum1 = own1 + send(far1, 1)
    total = own0 + send(sum2, 4) + send(sum0, 1) + send(sum1, 2)
    return (tokens.astype(F32) + total).astype(BF)


def generic_device(tokens, norm_gain, gate_weight, up_weight, down_weight):
    normed = norm_rows(tokens, norm_gain)
    gathered = lax.all_gather(normed, ("dp", "tensor"), axis=0, tiled=True)
    gate_out = jnp.dot(gathered, gate_weight, preferred_element_type=F32)
    up_out = jnp.dot(gathered, up_weight, preferred_element_type=F32)
    hidden = (jax.nn.silu(gate_out) * up_out).astype(BF)
    partial = jnp.dot(hidden, down_weight, preferred_element_type=F32)
    summed = lax.psum_scatter(partial, ("dp", "tensor"), scatter_dimension=0, tiled=True)
    return (tokens.astype(F32) + summed).astype(BF)


def solution(mesh):
    tuned = mesh.shape["dp"] == 2 and mesh.shape["tensor"] == 8
    in_specs = (
        P(("groups", "dp", "tensor"), None),
        P(),
        P(None, ("dp", "tensor")),
        P(None, ("dp", "tensor")),
        P(("dp", "tensor"), None),
    )
    out_specs = P(("groups", "dp", "tensor"), None)
    return jax.shard_map(
        per_device if tuned else generic_device, mesh=mesh, in_specs=in_specs, out_specs=out_specs, check_vma=False
    )
```

time: 69.9 us -> 58.9 us (0.84)
  waiting for transfers between devices: 26.7 us -> 13.3 us
  starting transfers between devices: 19.1 us -> 25 us
  other arithmetic: 2.95 us -> 0.9 us
  local copies, waits for them, and re-layouts: 1.06 us -> 0.02 us
    ppermute x24, waiting for transfers between devices: 26.7 us -> 13.3 us  [flip(): return lax.ppermute(x, axis, [(i, i ^ mask) for i in range(size)])]
    ppermute x24, starting transfers between devices: 19.1 us -> 25 us  [flip(): return lax.ppermute(x, axis, [(i, i ^ mask) for i in range(size)])]
    add x3 -> x2, other arithmetic: 2.12 us -> 0.07 us  [tie(): return x + mark]
    slice x2 -> x0, local copies, waits for them, and re-layouts: 1.03 us -> none  [tie(): return x + mark[0, 0]]
  transfers between devices with their start and end apart: 24 -> 24, of which waited for: 10 -> 14; matrix products, arithmetic and copies ran while one was open for 5% -> 0% of each run, Pallas kernels for 9% -> 14%
where the time goes in v2:
time: 58.9 us; the launch traced here: 58.8 us
  starting transfers between devices  25 us (42%)
  Pallas kernels  19.4 us (33%)
  waiting for transfers between devices  13.3 us (23%)
  other arithmetic  0.9 us (2%)
    ppermute x24, starting transfers between devices, flip(): return lax.ppermute(x, axis, [(i, i ^ mask) for i in range(size)])  25 us
    ppermute x24, waiting for transfers between devices, flip(): return lax.ppermute(x, axis, [(i, i ^ mask) for i in range(size)])  13.3 us
    pallas_call x2, Pallas kernels, fetch(): pl.pallas_call(functools.partial(fetch_kernel, first, len(after)), out_sh...  8.36 us
    pallas_call x1, Pallas kernels, per_device(): pl.pallas_call(functools.partial(hidden_kernel, len(held)), out_shape=jax...  7.23 us
    pallas_call x2, Pallas kernels, per_device(): pl.pallas_call(down_kernel, out_shape=(jax.ShapeDtypeStruct((8 * rows, st...  2.53 us
  transfers between devices with their start and end apart: 24, of which 14 were waited for; matrix products, arithmetic and copies ran while one was open for 0% of the time, Pallas kernels for 14%

profile of v2, /device:TPU:0, one launch (start us, length us, event | category | flops | bytes accessed | tf_op | source)
XLA Modules:
  0.0 58.8 jit_solution(9984689334320124078)
XLA Ops:
  0.0 1.1 %norm.1.refs_0_ = bf16[8,8192]{1,0:T(8,128)(2,1)S(1)} custom-call(bf16[8,8192]{1,0:T(8,128)(2,1)} %tokens.1, f32[1,8192]{1,0:T(1,128)} %bitcast.3), custom_call_target="tpu_custom_call" | custom-call | tf_op jit(solution)/shard_map/norm/pallas_call | solution.py:124
  1.1 3.0 %collective-permute-start.2 = (bf16[8,8192]{1,0:T(8,128)(2,1)S(1)}, bf16[8,8192]{1,0:T(8,128)(2,1)S(1)}, u32[]{:S(2)}, u32[]{:S(2)}) collective-permute-start(bf16[8,8192]{1,0:T(8,128)(2,1)S(1)} %norm.1.refs_0_), channel_id=1, source_target_pairs={{0,1},{1,0},{2,3},{3,2},{4,5},{5,4},{6,7},{7,6},{8,9},{9,8},{10,11... | collective-permute-start | bytes 393224 | tf_op jit(solution)/shard_map/ppermute | solution.py:20
  4.1 1.6 %collective-permute-start = (bf16[8,8192]{1,0:T(8,128)(2,1)S(1)}, bf16[8,8192]{1,0:T(8,128)(2,1)S(1)}, u32[]{:S(2)}, u32[]{:S(2)}) collective-permute-start(bf16[8,8192]{1,0:T(8,128)(2,1)S(1)} %norm.1.refs_0_), channel_id=1, source_target_pairs={{0,2},{1,3},{2,0},{3,1},{4,6},{5,7},{6,4},{7,5},{8,10},{9,11},{10,... | collective-permute-start | bytes 393224 | tf_op jit(solution)/shard_map/ppermute | solution.py:20
  5.7 2.6 %collective-permute-start.1 = (bf16[8,8192]{1,0:T(8,128)(2,1)S(1)}, bf16[8,8192]{1,0:T(8,128)(2,1)S(1)}, u32[]{:S(2)}, u32[]{:S(2)}) collective-permute-start(bf16[8,8192]{1,0:T(8,128)(2,1)S(1)} %norm.1.refs_0_), channel_id=1, source_target_pairs={{0,4},{1,5},{2,6},{3,7},{4,0},{5,1},{6,2},{7,3},{8,12},{9,13},{10,... | collective-permute-start | bytes 393224 | tf_op jit(solution)/shard_map/ppermute | solution.py:20
  8.3 0.0 collective-permute-done.2.refs_2_.refs_4_
  8.3 3.1 %collective-permute-start.6 = (bf16[8,8192]{1,0:T(8,128)(2,1)S(1)}, bf16[8,8192]{1,0:T(8,128)(2,1)S(1)}, u32[]{:S(2)}, u32[]{:S(2)}) collective-permute-start(bf16[8,8192]{1,0:T(8,128)(2,1)S(1)} %collective-permute-done.2.refs_2_.refs_4_), channel_id=1, source_target_pairs={{0,6},{1,7},{2,4},{3,5},{4,2},{5,3},{6,0},{7,1},{8,14},{9,15},{10,... | collective-permute-start | bytes 393224 | tf_op jit(solution)/shard_map/ppermute | solution.py:20
  11.5 0.0 collective-permute-done.refs_3_.refs_1_
  11.5 1.5 %collective-permute-start.4 = (bf16[8,8192]{1,0:T(8,128)(2,1)S(1)}, bf16[8,8192]{1,0:T(8,128)(2,1)S(1)}, u32[]{:S(2)}, u32[]{:S(2)}) collective-permute-start(bf16[8,8192]{1,0:T(8,128)(2,1)S(1)} %collective-permute-done.refs_3_.refs_1_), channel_id=1, source_target_pairs={{0,1},{1,0},{2,3},{3,2},{4,5},{5,4},{6,7},{7,6},{8,9},{9,8},{10,11... | collective-permute-start | bytes 393224 | tf_op jit(solution)/shard_map/ppermute | solution.py:20
  13.0 5.2 %fetch_0.1 = (bf16[4096,896]{1,0:T(8,128)(2,1)S(1)}, bf16[4096,896]{1,0:T(8,128)(2,1)S(1)}, bf16[8,8192]{1,0:T(8,128)(2,1)S(1)}) custom-call(bf16[8192,896]{1,0:T(8,128)(2,1)} %refs_20_.1, bf16[8192,896]{1,0:T(8,128)(2,1)} %refs_21_.1, bf16[8,8192]{1,0:T(8,128)(2,1)S(1)} %collective-permute-done.2.refs_2_.refs_4_, ...), custom_call_target="tpu_custom_call" | custom-call | bytes 14680064 | tf_op jit(solution)/shard_map/fetch_0/pallas_call | solution.py:54
  18.2 0.1 collective-permute-done.1.refs_2_
  18.3 0.5 collective-permute-start.5
  18.8 0.0 collective-permute-start.3
  18.8 0.0 collective-permute-start.7
  18.8 3.2 %fetch_4096.1 = (bf16[2048,896]{1,0:T(8,128)(2,1)S(1)}, bf16[2048,896]{1,0:T(8,128)(2,1)S(1)}, bf16[8,8192]{1,0:T(8,128)(2,1)S(1)}) custom-call(bf16[8192,896]{1,0:T(8,128)(2,1)} %refs_20_.1, bf16[8192,896]{1,0:T(8,128)(2,1)} %refs_21_.1, bf16[8,8192]{1,0:T(8,128)(2,1)S(1)} %collective-permute-done.1.refs_2_), custom_call_target="tpu_custom_call" | custom-call | bytes 7340032 | tf_op jit(solution)/shard_map/fetch_4096/pallas_call | solution.py:54
  22.0 0.0 collective-permute-done.6.refs_7_
  22.0 0.6 collective-permute-start.11
  22.6 0.0 collective-permute-done.4.refs_5_
  22.6 0.1 collective-permute-start.9
  22.7 0.7 %collective-permute-done.5.refs_6_ = bf16[8,8192]{1,0:T(8,128)(2,1)S(1)} collective-permute-done((bf16[8,8192]{1,0:T(8,128)(2,1)S(1)}, bf16[8,8192]{1,0:T(8,128)(2,1)S(1)}, u32[]{:S(2)}, u32[]{:S(2)}) %collective-permute-start.5) | collective-permute-done | bytes 131104 | tf_op jit(solution)/shard_map/ppermute | solution.py:20
  23.3 0.0 collective-permute-start.8
  23.3 0.4 collective-permute-done.3.refs_3_
  23.8 0.0 slice-start
  23.8 0.1 collective-permute-start.14
  23.9 0.0 collective-permute-done.7.refs_8_
  23.9 0.4 collective-permute-start.13
  24.4 0.0 collective-permute-done.11.refs_12_
  24.4 0.1 collective-permute-start.12
  24.5 0.0 collective-permute-done.9.refs_10_
  24.5 0.4 collective-permute-start.10
  24.9 0.0 collective-permute-done.8.refs_9_
  24.9 0.3 collective-permute-done.14.refs_15_
  25.2 0.2 collective-permute-done.13.refs_14_
  25.4 0.3 collective-permute-done.12.refs_13_
  25.7 0.2 collective-permute-done.10.refs_11_
  25.9 0.0 slice-start.1
  25.9 7.2 %hidden.1 = bf16[128,896]{1,0:T(8,128)(2,1)S(1)} custom-call(bf16[8,8192]{1,0:T(8,128)(2,1)S(1)} %norm.1.refs_0_, bf16[8,8192]{1,0:T(8,128)(2,1)S(1)} %collective-permute-done.refs_3_.refs_1_, bf16[8,8192]{1,0:T(8,128)(2,1)S(1)} %collective-permute-done.1.refs_2_, bf16[8,8192]{1,0:T(8,128)(2,1)S(1)} %collective-permute-done.3.refs_3_, ...), custom_call_target="tpu_custom_call" | custom-call | tf_op jit(solution)/shard_map/hidden/pallas_call | solution.py:149
  33.2 0.0 slice-done
  33.2 0.0 slice-done.1
  33.2 0.0 slice-done.2
  33.2 0.0 slice-done.3
  33.2 1.3 %down.6 = (f32[64,4096]{1,0:T(8,128)S(1)}, bf16[64,4096]{1,0:T(8,128)(2,1)S(1)}) custom-call(bf16[128,896]{1,0:T(8,128)(2,1)S(1)} %hidden.1, bf16[896,8192]{1,0:T(8,128)(2,1)S(1)} %bitcast.2), custom_call_target="tpu_custom_call" | custom-call | tf_op jit(solution)/shard_map/down/pallas_call | solution.py:161
  34.5 0.0 copy-start
  34.5 1.3 %down.4 = (f32[64,4096]{1,0:T(8,128)S(1)}, bf16[64,4096]{1,0:T(8,128)(2,1)S(1)}) custom-call(bf16[128,896]{1,0:T(8,128)(2,1)S(1)} %hidden.1, bf16[896,8192]{1,0:T(8,128)(2,1)S(1)} %bitcast.2), custom_call_target="tpu_custom_call" | custom-call | tf_op jit(solution)/shard_map/down/pallas_call | solution.py:161
  35.8 0.4 collective-permute-start.16
  36.2 0.2 collective-permute-start.15
  36.4 1.4 %collective-permute-done.16.refs_3_ = bf16[64,4096]{1,0:T(8,128)(2,1)S(1)} collective-permute-done((bf16[64,4096]{1,0:T(8,128)(2,1)S(1)}, bf16[64,4096]{1,0:T(8,128)(2,1)S(1)}, u32[]{:S(2)}, u32[]{:S(2)}) %collective-permute-start.16) | collective-permute-done | bytes 524320 | tf_op jit(solution)/shard_map/ppermute | solution.py:20
  37.8 0.7 %collective-permute-done.15.refs_2_ = bf16[64,4096]{1,0:T(8,128)(2,1)S(1)} collective-permute-done((bf16[64,4096]{1,0:T(8,128)(2,1)S(1)}, bf16[64,4096]{1,0:T(8,128)(2,1)S(1)}, u32[]{:S(2)}, u32[]{:S(2)}) %collective-permute-start.15) | collective-permute-done | bytes 524320 | tf_op jit(solution)/shard_map/ppermute | solution.py:20
  38.5 0.2 pair.1
  38.7 1.6 %collective-permute-start.17 = (bf16[8,8192]{1,0:T(8,128)(2,1)S(1)}, bf16[8,8192]{1,0:T(8,128)(2,1)S(1)}, u32[]{:S(2)}, u32[]{:S(2)}) collective-permute-start(bf16[8,8192]{1,0:T(8,128)(2,1)S(1)} %get-tuple-element.35), channel_id=1, source_target_pairs={{0,1},{1,0},{2,3},{3,2},{4,5},{5,4},{6,7},{7,6},{8,9},{9,8},{10,11... | collective-permute-start | bytes 393224 | tf_op jit(solution)/shard_map/ppermute | solution.py:20
  40.3 1.4 %collective-permute-start.18 = (bf16[8,8192]{1,0:T(8,128)(2,1)S(1)}, bf16[8,8192]{1,0:T(8,128)(2,1)S(1)}, u32[]{:S(2)}, u32[]{:S(2)}) collective-permute-start(bf16[8,8192]{1,0:T(8,128)(2,1)S(1)} %get-tuple-element.36), channel_id=1, source_target_pairs={{0,2},{1,3},{2,0},{3,1},{4,6},{5,7},{6,4},{7,5},{8,10},{9,11},{10,... | collective-permute-start | bytes 393224 | tf_op jit(solution)/shard_map/ppermute | solution.py:20
  41.7 2.5 %collective-permute-start.20 = (bf16[8,8192]{1,0:T(8,128)(2,1)S(1)}, bf16[8,8192]{1,0:T(8,128)(2,1)S(1)}, u32[]{:S(2)}, u32[]{:S(2)}) collective-permute-start(bf16[8,8192]{1,0:T(8,128)(2,1)S(1)} %get-tuple-element.38), channel_id=1, source_target_pairs={{0,6},{1,7},{2,4},{3,5},{4,2},{5,3},{6,0},{7,1},{8,14},{9,15},{10,... | collective-permute-start | bytes 393224 | tf_op jit(solution)/shard_map/ppermute | solution.py:20
  44.2 0.6 %collective-permute-start.22 = (bf16[8,8192]{1,0:T(8,128)(2,1)S(1)}, bf16[8,8192]{1,0:T(8,128)(2,1)S(1)}, u32[]{:S(2)}, u32[]{:S(2)}) collective-permute-start(bf16[8,8192]{1,0:T(8,128)(2,1)S(1)} %get-tuple-element.40), channel_id=1, source_target_pairs={{0,1},{1,0},{2,3},{3,2},{4,5},{5,4},{6,7},{7,6},{8,9},{9,8},{10,11... | collective-permute-start | bytes 393224 | tf_op jit(solution)/shard_map/ppermute | solution.py:20
  44.8 0.0 collective-permute-done.17
  44.8 0.9 %collective-permute-done.18 = bf16[8,8192]{1,0:T(8,128)(2,1)S(1)} collective-permute-done((bf16[8,8192]{1,0:T(8,128)(2,1)S(1)}, bf16[8,8192]{1,0:T(8,128)(2,1)S(1)}, u32[]{:S(2)}, u32[]{:S(2)}) %collective-permute-start.18) | collective-permute-done | bytes 131104 | tf_op jit(solution)/shard_map/ppermute | solution.py:20
  45.8 3.4 %collective-permute-start.19 = (bf16[8,8192]{1,0:T(8,128)(2,1)S(1)}, bf16[8,8192]{1,0:T(8,128)(2,1)S(1)}, u32[]{:S(2)}, u32[]{:S(2)}) collective-permute-start(bf16[8,8192]{1,0:T(8,128)(2,1)S(1)} %add_convert_fusion.3), channel_id=1, source_target_pairs={{0,4},{1,5},{2,6},{3,7},{4,0},{5,1},{6,2},{7,3},{8,12},{9,13},{10,... | collective-permute-start | bytes 393224 | tf_op jit(solution)/shard_map/ppermute | solution.py:20
  49.2 2.2 %collective-permute-done.20 = bf16[8,8192]{1,0:T(8,128)(2,1)S(1)} collective-permute-done((bf16[8,8192]{1,0:T(8,128)(2,1)S(1)}, bf16[8,8192]{1,0:T(8,128)(2,1)S(1)}, u32[]{:S(2)}, u32[]{:S(2)}) %collective-permute-start.20) | collective-permute-done | bytes 131104 | tf_op jit(solution)/shard_map/ppermute | solution.py:20
  51.5 0.7 %collective-permute-start.21 = (bf16[8,8192]{1,0:T(8,128)(2,1)S(1)}, bf16[8,8192]{1,0:T(8,128)(2,1)S(1)}, u32[]{:S(2)}, u32[]{:S(2)}) collective-permute-start(bf16[8,8192]{1,0:T(8,128)(2,1)S(1)} %add_convert_fusion.2), channel_id=1, source_target_pairs={{0,1},{1,0},{2,3},{3,2},{4,5},{5,4},{6,7},{7,6},{8,9},{9,8},{10,11... | collective-permute-start | bytes 393224 | tf_op jit(solution)/shard_map/ppermute | solution.py:20
  52.2 0.0 collective-permute-done.22
  52.2 0.1 collective-permute-start.23
  52.3 3.9 %collective-permute-done.19 = bf16[8,8192]{1,0:T(8,128)(2,1)S(1)} collective-permute-done((bf16[8,8192]{1,0:T(8,128)(2,1)S(1)}, bf16[8,8192]{1,0:T(8,128)(2,1)S(1)}, u32[]{:S(2)}, u32[]{:S(2)}) %collective-permute-start.19) | collective-permute-done | bytes 131104 | tf_op jit(solution)/shard_map/ppermute | solution.py:20
  56.2 0.3 collective-permute-done.21
  56.5 1.5 %collective-permute-done.23 = bf16[8,8192]{1,0:T(8,128)(2,1)S(1)} collective-permute-done((bf16[8,8192]{1,0:T(8,128)(2,1)S(1)}, bf16[8,8192]{1,0:T(8,128)(2,1)S(1)}, u32[]{:S(2)}, u32[]{:S(2)}) %collective-permute-start.23) | collective-permute-done | bytes 131104 | tf_op jit(solution)/shard_map/ppermute | solution.py:20
  58.0 0.0 copy-done
  58.0 0.7 %add_convert_fusion = bf16[8,8192]{1,0:T(8,128)(2,1)} fusion(bf16[8,8192]{1,0:T(8,128)(2,1)S(1)} %collective-permute-done.23, bf16[8,8192]{1,0:T(8,128)(2,1)S(1)} %collective-permute-done.21, f32[8,8192]{1,0:T(8,128)S(1)} %get-tuple-element.33, bf16[8,8192]{1,0:T(8,128)(2,1)S(1)} %collective-permute-done.19, bf16[8,8192]{1,0:T(8,128)(2,1)S(1)} %copy-done), kind=kLoop, calls=%fused_computation | loop fusion | flops 589824 | bytes 917504 | tf_op jit(solution)/shard_map/convert_element_type | solution.py:189
  (8 shorter events, 0.2 us)
Async XLA Ops:
  1.1 7.2 %collective-permute-start.2 = (bf16[8,8192]{1,0:T(8,128)(2,1)S(1)}, bf16[8,8192]{1,0:T(8,128)(2,1)S(1)}, u32[]{:S(2)}, u32[]{:S(2)}) collective-permute-start(bf16[8,8192]{1,0:T(8,128)(2,1)S(1)} %norm.1.refs_0_), channel_id=1, source_target_pairs={{0,1},{1,0},{2,3},{3,2},{4,5},{5,4},{6,7},{7,6},{8,9},{9,8},{10,11... | collective-permute-start | bytes 393224 | tf_op jit(solution)/shard_map/ppermute | solution.py:20
  4.1 7.3 %collective-permute-start = (bf16[8,8192]{1,0:T(8,128)(2,1)S(1)}, bf16[8,8192]{1,0:T(8,128)(2,1)S(1)}, u32[]{:S(2)}, u32[]{:S(2)}) collective-permute-start(bf16[8,8192]{1,0:T(8,128)(2,1)S(1)} %norm.1.refs_0_), channel_id=1, source_target_pairs={{0,2},{1,3},{2,0},{3,1},{4,6},{5,7},{6,4},{7,5},{8,10},{9,11},{10,... | collective-permute-start | bytes 393224 | tf_op jit(solution)/shard_map/ppermute | solution.py:20
  5.7 12.5 %collective-permute-start.1 = (bf16[8,8192]{1,0:T(8,128)(2,1)S(1)}, bf16[8,8192]{1,0:T(8,128)(2,1)S(1)}, u32[]{:S(2)}, u32[]{:S(2)}) collective-permute-start(bf16[8,8192]{1,0:T(8,128)(2,1)S(1)} %norm.1.refs_0_), channel_id=1, source_target_pairs={{0,4},{1,5},{2,6},{3,7},{4,0},{5,1},{6,2},{7,3},{8,12},{9,13},{10,... | collective-permute-start | bytes 393224 | tf_op jit(solution)/shard_map/ppermute | solution.py:20
  8.3 13.7 %collective-permute-start.6 = (bf16[8,8192]{1,0:T(8,128)(2,1)S(1)}, bf16[8,8192]{1,0:T(8,128)(2,1)S(1)}, u32[]{:S(2)}, u32[]{:S(2)}) collective-permute-start(bf16[8,8192]{1,0:T(8,128)(2,1)S(1)} %collective-permute-done.2.refs_2_.refs_4_), channel_id=1, source_target_pairs={{0,6},{1,7},{2,4},{3,5},{4,2},{5,3},{6,0},{7,1},{8,14},{9,15},{10,... | collective-permute-start | bytes 393224 | tf_op jit(solution)/shard_map/ppermute | solution.py:20
  11.5 11.1 %collective-permute-start.4 = (bf16[8,8192]{1,0:T(8,128)(2,1)S(1)}, bf16[8,8192]{1,0:T(8,128)(2,1)S(1)}, u32[]{:S(2)}, u32[]{:S(2)}) collective-permute-start(bf16[8,8192]{1,0:T(8,128)(2,1)S(1)} %collective-permute-done.refs_3_.refs_1_), channel_id=1, source_target_pairs={{0,1},{1,0},{2,3},{3,2},{4,5},{5,4},{6,7},{7,6},{8,9},{9,8},{10,11... | collective-permute-start | bytes 393224 | tf_op jit(solution)/shard_map/ppermute | solution.py:20
  18.3 5.0 %collective-permute-start.5 = (bf16[8,8192]{1,0:T(8,128)(2,1)S(1)}, bf16[8,8192]{1,0:T(8,128)(2,1)S(1)}, u32[]{:S(2)}, u32[]{:S(2)}) collective-permute-start(bf16[8,8192]{1,0:T(8,128)(2,1)S(1)} %add.39), channel_id=1, source_target_pairs={{0,1},{1,0},{2,3},{3,2},{4,5},{5,4},{6,7},{7,6},{8,9},{9,8},{10,11... | collective-permute-start | bytes 393224 | tf_op jit(solution)/shard_map/ppermute | solution.py:20
  18.8 5.0 %collective-permute-start.3 = (bf16[8,8192]{1,0:T(8,128)(2,1)S(1)}, bf16[8,8192]{1,0:T(8,128)(2,1)S(1)}, u32[]{:S(2)}, u32[]{:S(2)}) collective-permute-start(bf16[8,8192]{1,0:T(8,128)(2,1)S(1)} %add.39), channel_id=1, source_target_pairs={{0,2},{1,3},{2,0},{3,1},{4,6},{5,7},{6,4},{7,5},{8,10},{9,11},{10,... | collective-permute-start | bytes 393224 | tf_op jit(solution)/shard_map/ppermute | solution.py:20
  18.8 5.1 %collective-permute-start.7 = (bf16[8,8192]{1,0:T(8,128)(2,1)S(1)}, bf16[8,8192]{1,0:T(8,128)(2,1)S(1)}, u32[]{:S(2)}, u32[]{:S(2)}) collective-permute-start(bf16[8,8192]{1,0:T(8,128)(2,1)S(1)} %norm.1.refs_0_), channel_id=1, source_target_pairs={{0,8},{8,0},{1,9},{9,1},{2,10},{10,2},{3,11},{11,3},{4,12},{12,4},... | collective-permute-start | bytes 393224 | tf_op jit(solution)/shard_map/ppermute | solution.py:20
  22.0 2.4 %collective-permute-start.11 = (bf16[8,8192]{1,0:T(8,128)(2,1)S(1)}, bf16[8,8192]{1,0:T(8,128)(2,1)S(1)}, u32[]{:S(2)}, u32[]{:S(2)}) collective-permute-start(bf16[8,8192]{1,0:T(8,128)(2,1)S(1)} %collective-permute-done.2.refs_2_.refs_4_), channel_id=1, source_target_pairs={{0,8},{8,0},{1,9},{9,1},{2,10},{10,2},{3,11},{11,3},{4,12},{12,4},... | collective-permute-start | bytes 393224 | tf_op jit(solution)/shard_map/ppermute | solution.py:20
  22.6 1.9 %collective-permute-start.9 = (bf16[8,8192]{1,0:T(8,128)(2,1)S(1)}, bf16[8,8192]{1,0:T(8,128)(2,1)S(1)}, u32[]{:S(2)}, u32[]{:S(2)}) collective-permute-start(bf16[8,8192]{1,0:T(8,128)(2,1)S(1)} %collective-permute-done.1.refs_2_), channel_id=1, source_target_pairs={{0,8},{8,0},{1,9},{9,1},{2,10},{10,2},{3,11},{11,3},{4,12},{12,4},... | collective-permute-start | bytes 393224 | tf_op jit(solution)/shard_map/ppermute | solution.py:20
  23.3 1.6 %collective-permute-start.8 = (bf16[8,8192]{1,0:T(8,128)(2,1)S(1)}, bf16[8,8192]{1,0:T(8,128)(2,1)S(1)}, u32[]{:S(2)}, u32[]{:S(2)}) collective-permute-start(bf16[8,8192]{1,0:T(8,128)(2,1)S(1)} %collective-permute-done.refs_3_.refs_1_), channel_id=1, source_target_pairs={{0,8},{8,0},{1,9},{9,1},{2,10},{10,2},{3,11},{11,3},{4,12},{12,4},... | collective-permute-start | bytes 393224 | tf_op jit(solution)/shard_map/ppermute | solution.py:20
  23.8 9.4 %slice-start = ((s8[14680064]{0:T(1024)(128)(4,1)}), s8[4194304]{0:T(1024)(128)(4,1)S(1)}, s32[]{:S(2)}) async-start(s8[14680064]{0:T(1024)(128)(4,1)} %bitcast.1), calls=%async_computation | async-start | bytes 8388608
  23.8 1.4 %collective-permute-start.14 = (bf16[8,8192]{1,0:T(8,128)(2,1)S(1)}, bf16[8,8192]{1,0:T(8,128)(2,1)S(1)}, u32[]{:S(2)}, u32[]{:S(2)}) collective-permute-start(bf16[8,8192]{1,0:T(8,128)(2,1)S(1)} %get-tuple-element.41), channel_id=1, source_target_pairs={{0,8},{8,0},{1,9},{9,1},{2,10},{10,2},{3,11},{11,3},{4,12},{12,4},... | collective-permute-start | bytes 393224 | tf_op jit(solution)/shard_map/ppermute | solution.py:20
  23.9 1.5 %collective-permute-start.13 = (bf16[8,8192]{1,0:T(8,128)(2,1)S(1)}, bf16[8,8192]{1,0:T(8,128)(2,1)S(1)}, u32[]{:S(2)}, u32[]{:S(2)}) collective-permute-start(bf16[8,8192]{1,0:T(8,128)(2,1)S(1)} %get-tuple-element.42), channel_id=1, source_target_pairs={{0,8},{8,0},{1,9},{9,1},{2,10},{10,2},{3,11},{11,3},{4,12},{12,4},... | collective-permute-start | bytes 393224 | tf_op jit(solution)/shard_map/ppermute | solution.py:20
  24.4 1.3 %collective-permute-start.12 = (bf16[8,8192]{1,0:T(8,128)(2,1)S(1)}, bf16[8,8192]{1,0:T(8,128)(2,1)S(1)}, u32[]{:S(2)}, u32[]{:S(2)}) collective-permute-start(bf16[8,8192]{1,0:T(8,128)(2,1)S(1)} %get-tuple-element.43), channel_id=1, source_target_pairs={{0,8},{8,0},{1,9},{9,1},{2,10},{10,2},{3,11},{11,3},{4,12},{12,4},... | collective-permute-start | bytes 393224 | tf_op jit(solution)/shard_map/ppermute | solution.py:20
  24.5 1.4 %collective-permute-start.10 = (bf16[8,8192]{1,0:T(8,128)(2,1)S(1)}, bf16[8,8192]{1,0:T(8,128)(2,1)S(1)}, u32[]{:S(2)}, u32[]{:S(2)}) collective-permute-start(bf16[8,8192]{1,0:T(8,128)(2,1)S(1)} %get-tuple-element.44), channel_id=1, source_target_pairs={{0,8},{8,0},{1,9},{9,1},{2,10},{10,2},{3,11},{11,3},{4,12},{12,4},... | collective-permute-start | bytes 393224 | tf_op jit(solution)/shard_map/ppermute | solution.py:20
  25.9 7.3 %slice-start.1 = ((s8[14680064]{0:T(1024)(128)(4,1)}), s8[4194304]{0:T(1024)(128)(4,1)S(1)}, s32[]{:S(2)}) async-start(s8[14680064]{0:T(1024)(128)(4,1)} %bitcast.1), calls=%async_computation.1 | async-start | bytes 8388608
  25.9 7.3 %slice-start.2 = ((s8[14680064]{0:T(1024)(128)(4,1)}), s8[4194304]{0:T(1024)(128)(4,1)S(1)}, s32[]{:S(2)}) async-start(s8[14680064]{0:T(1024)(128)(4,1)} %bitcast.1), calls=%async_computation.2 | async-start | bytes 8388608
  25.9 7.3 %slice-start.3 = ((s8[14680064]{0:T(1024)(128)(4,1)}), s8[2097152]{0:T(1024)(128)(4,1)S(1)}, s32[]{:S(2)}) async-start(s8[14680064]{0:T(1024)(128)(4,1)} %bitcast.1), calls=%async_computation.3 | async-start | bytes 4194304
  34.5 23.6 %copy-start = (bf16[8,8192]{1,0:T(8,128)(2,1)S(1)}, bf16[8,8192]{1,0:T(8,128)(2,1)}, u32[]{:S(2)}) copy-start(bf16[8,8192]{1,0:T(8,128)(2,1)} %tokens.1) | copy-start | bytes 393220
  35.8 2.0 %collective-permute-start.16 = (bf16[64,4096]{1,0:T(8,128)(2,1)S(1)}, bf16[64,4096]{1,0:T(8,128)(2,1)S(1)}, u32[]{:S(2)}, u32[]{:S(2)}) collective-permute-start(bf16[64,4096]{1,0:T(8,128)(2,1)S(1)} %get-tuple-element.32), channel_id=1, source_target_pairs={{0,8},{8,0},{1,9},{9,1},{2,10},{10,2},{3,11},{11,3},{4,12},{12,4},... | collective-permute-start | bytes 1572872 | tf_op jit(solution)/shard_map/ppermute | solution.py:20
  36.2 2.3 %collective-permute-start.15 = (bf16[64,4096]{1,0:T(8,128)(2,1)S(1)}, bf16[64,4096]{1,0:T(8,128)(2,1)S(1)}, u32[]{:S(2)}, u32[]{:S(2)}) collective-permute-start(bf16[64,4096]{1,0:T(8,128)(2,1)S(1)} %get-tuple-element.31), channel_id=1, source_target_pairs={{0,8},{8,0},{1,9},{9,1},{2,10},{10,2},{3,11},{11,3},{4,12},{12,4},... | collective-permute-start | bytes 1572872 | tf_op jit(solution)/shard_map/ppermute | solution.py:20
  38.7 6.2 %collective-permute-start.17 = (bf16[8,8192]{1,0:T(8,128)(2,1)S(1)}, bf16[8,8192]{1,0:T(8,128)(2,1)S(1)}, u32[]{:S(2)}, u32[]{:S(2)}) collective-permute-start(bf16[8,8192]{1,0:T(8,128)(2,1)S(1)} %get-tuple-element.35), channel_id=1, source_target_pairs={{0,1},{1,0},{2,3},{3,2},{4,5},{5,4},{6,7},{7,6},{8,9},{9,8},{10,11... | collective-permute-start | bytes 393224 | tf_op jit(solution)/shard_map/ppermute | solution.py:20
  40.3 5.4 %collective-permute-start.18 = (bf16[8,8192]{1,0:T(8,128)(2,1)S(1)}, bf16[8,8192]{1,0:T(8,128)(2,1)S(1)}, u32[]{:S(2)}, u32[]{:S(2)}) collective-permute-start(bf16[8,8192]{1,0:T(8,128)(2,1)S(1)} %get-tuple-element.36), channel_id=1, source_target_pairs={{0,2},{1,3},{2,0},{3,1},{4,6},{5,7},{6,4},{7,5},{8,10},{9,11},{10,... | collective-permute-start | bytes 393224 | tf_op jit(solution)/shard_map/ppermute | solution.py:20
  41.7 9.8 %collective-permute-start.20 = (bf16[8,8192]{1,0:T(8,128)(2,1)S(1)}, bf16[8,8192]{1,0:T(8,128)(2,1)S(1)}, u32[]{:S(2)}, u32[]{:S(2)}) collective-permute-start(bf16[8,8192]{1,0:T(8,128)(2,1)S(1)} %get-tuple-element.38), channel_id=1, source_target_pairs={{0,6},{1,7},{2,4},{3,5},{4,2},{5,3},{6,0},{7,1},{8,14},{9,15},{10,... | collective-permute-start | bytes 393224 | tf_op jit(solution)/shard_map/ppermute | solution.py:20
  44.2 7.9 %collective-permute-start.22 = (bf16[8,8192]{1,0:T(8,128)(2,1)S(1)}, bf16[8,8192]{1,0:T(8,128)(2,1)S(1)}, u32[]{:S(2)}, u32[]{:S(2)}) collective-permute-start(bf16[8,8192]{1,0:T(8,128)(2,1)S(1)} %get-tuple-element.40), channel_id=1, source_target_pairs={{0,1},{1,0},{2,3},{3,2},{4,5},{5,4},{6,7},{7,6},{8,9},{9,8},{10,11... | collective-permute-start | bytes 393224 | tf_op jit(solution)/shard_map/ppermute | solution.py:20
  45.8 10.4 %collective-permute-start.19 = (bf16[8,8192]{1,0:T(8,128)(2,1)S(1)}, bf16[8,8192]{1,0:T(8,128)(2,1)S(1)}, u32[]{:S(2)}, u32[]{:S(2)}) collective-permute-start(bf16[8,8192]{1,0:T(8,128)(2,1)S(1)} %add_convert_fusion.3), channel_id=1, source_target_pairs={{0,4},{1,5},{2,6},{3,7},{4,0},{5,1},{6,2},{7,3},{8,12},{9,13},{10,... | collective-permute-start | bytes 393224 | tf_op jit(solution)/shard_map/ppermute | solution.py:20
  51.5 5.0 %collective-permute-start.21 = (bf16[8,8192]{1,0:T(8,128)(2,1)S(1)}, bf16[8,8192]{1,0:T(8,128)(2,1)S(1)}, u32[]{:S(2)}, u32[]{:S(2)}) collective-permute-start(bf16[8,8192]{1,0:T(8,128)(2,1)S(1)} %add_convert_fusion.2), channel_id=1, source_target_pairs={{0,1},{1,0},{2,3},{3,2},{4,5},{5,4},{6,7},{7,6},{8,9},{9,8},{10,11... | collective-permute-start | bytes 393224 | tf_op jit(solution)/shard_map/ppermute | solution.py:20
  52.2 5.9 %collective-permute-start.23 = (bf16[8,8192]{1,0:T(8,128)(2,1)S(1)}, bf16[8,8192]{1,0:T(8,128)(2,1)S(1)}, u32[]{:S(2)}, u32[]{:S(2)}) collective-permute-start(bf16[8,8192]{1,0:T(8,128)(2,1)S(1)} %add_convert_fusion.1), channel_id=1, source_target_pairs={{0,2},{1,3},{2,0},{3,1},{4,6},{5,7},{6,4},{7,5},{8,10},{9,11},{10,... | collective-permute-start | bytes 393224 | tf_op jit(solution)/shard_map/ppermute | solution.py:20

commit v3 on v2

--- a/solution.py
+++ b/solution.py
@@ -9,7 +9,7 @@
 
 BF = jnp.bfloat16
 F32 = jnp.float32
-N_CHUNKS = 2
+SPLIT = (3, 1)
 COST = 4
 FETCHES = (4, 2)
 CHUNK = 1024
@@ -20,18 +20,17 @@
     return lax.ppermute(x, axis, [(i, i ^ mask) for i in range(size)])
 
 
-def norm_rows(tokens, norm_gain):
-    widened = tokens.astype(F32)
-    inv_rms = lax.rsqrt(jnp.mean(widened * widened, axis=-1, keepdims=True) + 1e-05)
-    return (widened * inv_rms * norm_gain).astype(BF)
+def inverse_rms(rows):
+    widened = rows.astype(F32)
+    return lax.rsqrt(jnp.mean(widened * widened, axis=-1, keepdims=True) + 1e-05)
+
+
+def scaled(rows, inv_rms, gain):
+    return (rows.astype(F32) * inv_rms * gain).astype(BF)
 
 
 def vmem_specs(count):
     return [pl.BlockSpec(memory_space=pltpu.VMEM)] * count
-
-
-def norm_kernel(tokens, gain, out):
-    out[...] = norm_rows(tokens[...], gain[...])
 
 
 def fetch_kernel(first, after, *refs):
@@ -64,7 +63,7 @@
 
 
 def hidden_kernel(held, *refs):
-    pieces, rest = refs[:16], refs[16:]
+    pieces, gain, rest = refs[:16], refs[16], refs[17:]
     gates, ups, (gate, up, out, gate_late, up_late, sems) = rest[:held], rest[held : 2 * held], rest[2 * held :]
     late, depth = gate_late.shape[:2]
     base = gate.shape[0] - late * depth
@@ -73,11 +72,13 @@
         for i, (src, dst) in enumerate([(gate, gate_late), (up, up_late)]):
             copies.append(pltpu.make_async_copy(src.at[pl.ds(base + k * depth, depth)], dst.at[k], sems.at[k, i]))
             copies[-1].start()
+    inv_rms = [inverse_rms(p[...]) for p in pieces]
     gate_out = up_out = 0.0
     first = 0
     for k in range(held + late):
         size = gates[k].shape[0] if k < held else depth
-        rows = jnp.concatenate([p[:, first : first + size] for p in pieces], axis=0)
+        cols = slice(first, first + size)
+        rows = jnp.concatenate([scaled(p[:, cols], inv, gain[:, cols]) for p, inv in zip(pieces, inv_rms)], axis=0)
         if k >= held:
             copies[2 * (k - held)].wait()
             copies[2 * (k - held) + 1].wait()
@@ -99,11 +100,13 @@
 def pair_kernel(chunks, *refs):
     owns, recvs, outs = refs[:chunks], refs[chunks : 2 * chunks], refs[2 * chunks :]
     rows = outs[0].shape[0]
+    first = 0
     for c in range(chunks):
         step = owns[c].shape[1]
         total = owns[c][...] + recvs[c][...].astype(F32)
         for d, out in enumerate(outs):
-            out[:, c * step : (c + 1) * step] = total[d * rows : (d + 1) * rows].astype(out.dtype)
+            out[:, first : first + step] = total[d * rows : (d + 1) * rows].astype(out.dtype)
+        first += step
 
 
 def hbm(x):
@@ -121,25 +124,17 @@
 def per_device(tokens, norm_gain, gate_weight, up_weight, down_weight):
     rows, width = tokens.shape
     units = gate_weight.shape[1]
-    normed = pl.pallas_call(
-        norm_kernel,
-        out_shape=pltpu.VMEM((rows, width), BF),
-        in_specs=vmem_specs(2),
-        out_specs=vmem_specs(1)[0],
-        name="norm",
-    )(tokens, norm_gain.reshape(1, width))
-
     def hop(x, mask):
         return flip(x, "tensor", 8, mask)
 
     sizes = [CHUNK * n for n in FETCHES]
-    at1, at2, at4 = hop(normed, 1), hop(normed, 2), hop(normed, 4)
+    at1, at2, at4 = hop(tokens, 1), hop(tokens, 2), hop(tokens, 4)
     early = fetch(gate_weight, up_weight, 0, sizes[0], tokens.shape, [at1, at2])
     at4t = tie(at4, early[2])
     at7, at3 = hop(at1, 6), hop(at2, 1)
     at6, at5 = hop(at4t, 2), hop(at4t, 1)
     later = fetch(gate_weight, up_weight, sizes[0], sizes[1], tokens.shape, [at4])
-    mine = [normed, at1, at2, at4]
+    mine = [tokens, at1, at2, at4]
     last = [at7, at3, at6, at5]
     pieces = mine + last
     pieces += [flip(p, "dp", 2, 1) for p in mine + [tie(p, later[2]) for p in last]]
@@ -149,31 +144,33 @@
     hidden = pl.pallas_call(
         functools.partial(hidden_kernel, len(held)),
         out_shape=jax.ShapeDtypeStruct((16 * rows, units), BF),
-        in_specs=vmem_specs(16 + 2 * len(held)) + [pl.BlockSpec(memory_space=pltpu.HBM)] * 2,
+        in_specs=vmem_specs(17 + 2 * len(held)) + [pl.BlockSpec(memory_space=pltpu.HBM)] * 2,
         out_specs=vmem_specs(1)[0],
         scratch_shapes=[pltpu.VMEM(late, BF), pltpu.VMEM(late, BF), pltpu.SemaphoreType.DMA((late[0], 2))],
         compiler_params=pltpu.CompilerParams(vmem_limit_bytes=24 * 2**20),
         name="hidden",
-    )(*pieces, *[pin(f[0]) for f in held], *[pin(f[1]) for f in held], hbm(gate_weight), hbm(up_weight))
-    step = width // N_CHUNKS
+    )(*pieces, norm_gain.reshape(1, width), *[pin(f[0]) for f in held], *[pin(f[1]) for f in held], hbm(gate_weight), hbm(up_weight))
+    first, unit = 0, width // sum(SPLIT)
     owns, recvs = [], []
-    for c in range(N_CHUNKS):
+    for share in SPLIT:
+        step = share * unit
         own, other = pl.pallas_call(
             down_kernel,
             out_shape=(jax.ShapeDtypeStruct((8 * rows, step), F32), jax.ShapeDtypeStruct((8 * rows, step), BF)),
             grid=(1,),
-            in_specs=[pl.BlockSpec((16 * rows, units), lambda i: (0, 0)), pl.BlockSpec((units, step), functools.partial(lambda c, i: (0, c), c))],
+            in_specs=[pl.BlockSpec((16 * rows, units), lambda i: (0, 0)), pl.BlockSpec((units, step), functools.partial(lambda c, i: (0, c), first // step))],
             out_specs=(pl.BlockSpec((8 * rows, step), lambda i: (0, 0)),) * 2,
-            compiler_params=pltpu.CompilerParams(vmem_limit_bytes=16 * 2**20),
+            compiler_params=pltpu.CompilerParams(vmem_limit_bytes=20 * 2**20),
             name="down",
         )(hidden, down_weight)
         owns.append(own)
         recvs.append(flip(other, "dp", 2, 1))
+        first += step
     kinds = [F32, F32, F32, BF, F32, BF, BF, BF]
     own0, own1, own2, own3, far0, far1, far2, far3 = pl.pallas_call(
-        functools.partial(pair_kernel, N_CHUNKS),
+        functools.partial(pair_kernel, len(SPLIT)),
         out_shape=[jax.ShapeDtypeStruct((rows, width), kind) for kind in kinds],
-        in_specs=vmem_specs(2 * N_CHUNKS),
+        in_specs=vmem_specs(2 * len(SPLIT)),
         out_specs=vmem_specs(8),
         compiler_params=pltpu.CompilerParams(vmem_limit_bytes=16 * 2**20),
         name="pair",
@@ -190,7 +187,7 @@
 
 
 def generic_device(tokens, norm_gain, gate_weight, up_weight, down_weight):
-    normed = norm_rows(tokens, norm_gain)
+    normed = scaled(tokens, inverse_rms(tokens), norm_gain)
     gathered = lax.all_gather(normed, ("dp", "tensor"), axis=0, tiled=True)
     gate_out = jnp.dot(gathered, gate_weight, preferred_element_type=F32)
     up_out = jnp.dot(gathered, up_weight, preferred_element_type=F32)

time: 58.9 us -> 57.3 us (0.973)
  Pallas kernels: 19.4 us -> 18.3 us
  waiting for transfers between devices: 13.3 us -> 12.6 us
    pallas_call x2 -> x1, Pallas kernels: 1.26 us -> 0.17 us  [per_device(): pl.pallas_call(functools.partial(pair_kernel, len(SPLIT)), out_shape=[jax...]
    ppermute x24, waiting for transfers between devices: 13.3 us -> 12.6 us  [flip(): return lax.ppermute(x, axis, [(i, i ^ mask) for i in range(size)])]
  transfers between devices with their start and end apart: 24 -> 24, of which waited for: 14 -> 13; matrix products, arithmetic and copies ran while one was open for 0% -> 0% of each run, Pallas kernels for 14% -> 16%
where the time goes in v3:
time: 57.3 us; the launch traced here: 57.1 us
  starting transfers between devices  25.2 us (44%)
  Pallas kernels  18.3 us (32%)
  waiting for transfers between devices  12.6 us (22%)
  other arithmetic  0.9 us (2%)
    ppermute x24, starting transfers between devices, flip(): return lax.ppermute(x, axis, [(i, i ^ mask) for i in range(size)])  25.2 us
    ppermute x24, waiting for transfers between devices, flip(): return lax.ppermute(x, axis, [(i, i ^ mask) for i in range(size)])  12.6 us
    pallas_call x2, Pallas kernels, fetch(): pl.pallas_call(functools.partial(fetch_kernel, first, len(after)), out_sh...  8.37 us
    pallas_call x1, Pallas kernels, per_device(): pl.pallas_call(functools.partial(hidden_kernel, len(held)), out_shape=jax...  7.23 us
    pallas_call x2, Pallas kernels, per_device(): pl.pallas_call(down_kernel, out_shape=(jax.ShapeDtypeStruct((8 * rows, st...  2.53 us
  transfers between devices with their start and end apart: 24, of which 13 were waited for; matrix products, arithmetic and copies ran while one was open for 0% of the time, Pallas kernels for 16%

profile of v3, /device:TPU:0, one launch (start us, length us, event | category | flops | bytes accessed | tf_op | source)
XLA Modules:
  0.0 57.1 jit_solution(4589981140800304049)
XLA Ops:
  0.0 0.0 copy-start
  0.0 3.0 %collective-permute-start.2 = (bf16[8,8192]{1,0:T(8,128)(2,1)}, bf16[8,8192]{1,0:T(8,128)(2,1)S(1)}, u32[]{:S(2)}, u32[]{:S(2)}) collective-permute-start(bf16[8,8192]{1,0:T(8,128)(2,1)} %refs_0_.5), channel_id=1, source_target_pairs={{0,1},{1,0},{2,3},{3,2},{4,5},{5,4},{6,7},{7,6},{8,9},{9,8},{10,11... | collective-permute-start | bytes 393224 | tf_op jit(solution)/shard_map/ppermute | solution.py:20
  3.0 1.6 %collective-permute-start = (bf16[8,8192]{1,0:T(8,128)(2,1)}, bf16[8,8192]{1,0:T(8,128)(2,1)S(1)}, u32[]{:S(2)}, u32[]{:S(2)}) collective-permute-start(bf16[8,8192]{1,0:T(8,128)(2,1)} %refs_0_.5), channel_id=1, source_target_pairs={{0,2},{1,3},{2,0},{3,1},{4,6},{5,7},{6,4},{7,5},{8,10},{9,11},{10,... | collective-permute-start | bytes 393224 | tf_op jit(solution)/shard_map/ppermute | solution.py:20
  4.5 2.6 %collective-permute-start.1 = (bf16[8,8192]{1,0:T(8,128)(2,1)}, bf16[8,8192]{1,0:T(8,128)(2,1)S(1)}, u32[]{:S(2)}, u32[]{:S(2)}) collective-permute-start(bf16[8,8192]{1,0:T(8,128)(2,1)} %refs_0_.5), channel_id=1, source_target_pairs={{0,4},{1,5},{2,6},{3,7},{4,0},{5,1},{6,2},{7,3},{8,12},{9,13},{10,... | collective-permute-start | bytes 393224 | tf_op jit(solution)/shard_map/ppermute | solution.py:20
  7.1 0.0 collective-permute-done.2.refs_2_.refs_4_
  7.1 3.4 %collective-permute-start.6 = (bf16[8,8192]{1,0:T(8,128)(2,1)S(1)}, bf16[8,8192]{1,0:T(8,128)(2,1)S(1)}, u32[]{:S(2)}, u32[]{:S(2)}) collective-permute-start(bf16[8,8192]{1,0:T(8,128)(2,1)S(1)} %collective-permute-done.2.refs_2_.refs_4_), channel_id=1, source_target_pairs={{0,6},{1,7},{2,4},{3,5},{4,2},{5,3},{6,0},{7,1},{8,14},{9,15},{10,... | collective-permute-start | bytes 393224 | tf_op jit(solution)/shard_map/ppermute | solution.py:20
  10.5 0.0 collective-permute-done.refs_3_.refs_1_
  10.5 1.5 %collective-permute-start.4 = (bf16[8,8192]{1,0:T(8,128)(2,1)S(1)}, bf16[8,8192]{1,0:T(8,128)(2,1)S(1)}, u32[]{:S(2)}, u32[]{:S(2)}) collective-permute-start(bf16[8,8192]{1,0:T(8,128)(2,1)S(1)} %collective-permute-done.refs_3_.refs_1_), channel_id=1, source_target_pairs={{0,1},{1,0},{2,3},{3,2},{4,5},{5,4},{6,7},{7,6},{8,9},{9,8},{10,11... | collective-permute-start | bytes 393224 | tf_op jit(solution)/shard_map/ppermute | solution.py:20
  12.0 5.2 %fetch_0.1 = (bf16[4096,896]{1,0:T(8,128)(2,1)S(1)}, bf16[4096,896]{1,0:T(8,128)(2,1)S(1)}, bf16[8,8192]{1,0:T(8,128)(2,1)S(1)}) custom-call(bf16[8192,896]{1,0:T(8,128)(2,1)} %refs_21_.1, bf16[8192,896]{1,0:T(8,128)(2,1)} %refs_22_.1, bf16[8,8192]{1,0:T(8,128)(2,1)S(1)} %collective-permute-done.2.refs_2_.refs_4_, ...), custom_call_target="tpu_custom_call" | custom-call | bytes 14680064 | tf_op jit(solution)/shard_map/fetch_0/pallas_call | solution.py:53
  17.2 0.1 collective-permute-done.1.refs_2_
  17.4 0.0 copy-start.1
  17.4 0.5 collective-permute-start.5
  17.9 0.0 collective-permute-start.3
  17.9 0.0 copy-done
  17.9 0.0 collective-permute-start.7
  17.9 3.2 %fetch_4096.1 = (bf16[2048,896]{1,0:T(8,128)(2,1)S(1)}, bf16[2048,896]{1,0:T(8,128)(2,1)S(1)}, bf16[8,8192]{1,0:T(8,128)(2,1)S(1)}) custom-call(bf16[8192,896]{1,0:T(8,128)(2,1)} %refs_21_.1, bf16[8192,896]{1,0:T(8,128)(2,1)} %refs_22_.1, bf16[8,8192]{1,0:T(8,128)(2,1)S(1)} %collective-permute-done.1.refs_2_), custom_call_target="tpu_custom_call" | custom-call | bytes 7340032 | tf_op jit(solution)/shard_map/fetch_4096/pallas_call | solution.py:53
  21.1 0.0 collective-permute-done.6.refs_7_
  21.1 0.6 collective-permute-start.11
  21.6 0.0 collective-permute-done.4.refs_5_
  21.6 0.1 collective-permute-start.9
  21.7 0.7 %collective-permute-done.5.refs_6_ = bf16[8,8192]{1,0:T(8,128)(2,1)S(1)} collective-permute-done((bf16[8,8192]{1,0:T(8,128)(2,1)S(1)}, bf16[8,8192]{1,0:T(8,128)(2,1)S(1)}, u32[]{:S(2)}, u32[]{:S(2)}) %collective-permute-start.5) | collective-permute-done | bytes 131104 | tf_op jit(solution)/shard_map/ppermute | solution.py:20
  22.4 0.0 collective-permute-start.8
  22.4 0.4 collective-permute-done.3.refs_3_
  22.8 0.0 slice-start
  22.9 0.2 collective-permute-start.14
  23.0 0.0 collective-permute-done.7.refs_8_
  23.0 0.4 collective-permute-start.13
  23.5 0.0 collective-permute-done.11.refs_12_
  23.5 0.1 collective-permute-start.12
  23.6 0.0 collective-permute-done.9.refs_10_
  23.6 0.4 collective-permute-start.10
  24.0 0.0 collective-permute-done.8.refs_9_
  24.0 0.3 collective-permute-done.14.refs_15_
  24.3 0.2 collective-permute-done.13.refs_14_
  24.5 0.3 collective-permute-done.12.refs_13_
  24.8 0.2 collective-permute-done.10.refs_11_
  25.0 0.0 copy-done.1
  25.0 7.2 %hidden.1 = bf16[128,896]{1,0:T(8,128)(2,1)S(1)} custom-call(bf16[8,8192]{1,0:T(8,128)(2,1)S(1)} %copy-done, bf16[8,8192]{1,0:T(8,128)(2,1)S(1)} %collective-permute-done.refs_3_.refs_1_, bf16[8,8192]{1,0:T(8,128)(2,1)S(1)} %collective-permute-done.1.refs_2_, bf16[8,8192]{1,0:T(8,128)(2,1)S(1)} %collective-permute-done.3.refs_3_, ...), custom_call_target="tpu_custom_call" | custom-call | tf_op jit(solution)/shard_map/hidden/pallas_call | solution.py:144
  32.2 0.0 slice-done
  32.3 0.0 slice-done.1
  32.3 0.0 slice-done.2
  32.3 0.0 slice-done.3
  32.3 1.8 %down.4 = (f32[64,6144]{1,0:T(8,128)S(1)}, bf16[64,6144]{1,0:T(8,128)(2,1)S(1)}) custom-call(bf16[128,896]{1,0:T(8,128)(2,1)S(1)} %hidden.1, bf16[896,8192]{1,0:T(8,128)(2,1)S(1)} %bitcast.2), custom_call_target="tpu_custom_call" | custom-call | tf_op jit(solution)/shard_map/down/pallas_call | solution.py:157
  34.1 0.4 collective-permute-start.15
  34.5 0.7 %down.6 = (f32[64,2048]{1,0:T(8,128)S(1)}, bf16[64,2048]{1,0:T(8,128)(2,1)S(1)}) custom-call(bf16[128,896]{1,0:T(8,128)(2,1)S(1)} %hidden.1, bf16[896,8192]{1,0:T(8,128)(2,1)S(1)} %bitcast.2), custom_call_target="tpu_custom_call" | custom-call | tf_op jit(solution)/shard_map/down/pallas_call | solution.py:157
  35.2 0.3 collective-permute-start.16
  35.5 1.4 %collective-permute-done.16.refs_3_ = bf16[64,2048]{1,0:T(8,128)(2,1)S(1)} collective-permute-done((bf16[64,2048]{1,0:T(8,128)(2,1)S(1)}, bf16[64,2048]{1,0:T(8,128)(2,1)S(1)}, u32[]{:S(2)}, u32[]{:S(2)}) %collective-permute-start.16) | collective-permute-done | bytes 262176 | tf_op jit(solution)/shard_map/ppermute | solution.py:20
  36.8 0.0 collective-permute-done.15.refs_2_
  36.8 0.2 pair.1
  37.0 1.7 %collective-permute-start.17 = (bf16[8,8192]{1,0:T(8,128)(2,1)S(1)}, bf16[8,8192]{1,0:T(8,128)(2,1)S(1)}, u32[]{:S(2)}, u32[]{:S(2)}) collective-permute-start(bf16[8,8192]{1,0:T(8,128)(2,1)S(1)} %get-tuple-element.35), channel_id=1, source_target_pairs={{0,1},{1,0},{2,3},{3,2},{4,5},{5,4},{6,7},{7,6},{8,9},{9,8},{10,11... | collective-permute-start | bytes 393224 | tf_op jit(solution)/shard_map/ppermute | solution.py:20
  38.7 1.4 %collective-permute-start.18 = (bf16[8,8192]{1,0:T(8,128)(2,1)S(1)}, bf16[8,8192]{1,0:T(8,128)(2,1)S(1)}, u32[]{:S(2)}, u32[]{:S(2)}) collective-permute-start(bf16[8,8192]{1,0:T(8,128)(2,1)S(1)} %get-tuple-element.36), channel_id=1, source_target_pairs={{0,2},{1,3},{2,0},{3,1},{4,6},{5,7},{6,4},{7,5},{8,10},{9,11},{10,... | collective-permute-start | bytes 393224 | tf_op jit(solution)/shard_map/ppermute | solution.py:20
  40.0 2.5 %collective-permute-start.20 = (bf16[8,8192]{1,0:T(8,128)(2,1)S(1)}, bf16[8,8192]{1,0:T(8,128)(2,1)S(1)}, u32[]{:S(2)}, u32[]{:S(2)}) collective-permute-start(bf16[8,8192]{1,0:T(8,128)(2,1)S(1)} %get-tuple-element.38), channel_id=1, source_target_pairs={{0,6},{1,7},{2,4},{3,5},{4,2},{5,3},{6,0},{7,1},{8,14},{9,15},{10,... | collective-permute-start | bytes 393224 | tf_op jit(solution)/shard_map/ppermute | solution.py:20
  42.6 0.6 %collective-permute-start.22 = (bf16[8,8192]{1,0:T(8,128)(2,1)S(1)}, bf16[8,8192]{1,0:T(8,128)(2,1)S(1)}, u32[]{:S(2)}, u32[]{:S(2)}) collective-permute-start(bf16[8,8192]{1,0:T(8,128)(2,1)S(1)} %get-tuple-element.40), channel_id=1, source_target_pairs={{0,1},{1,0},{2,3},{3,2},{4,5},{5,4},{6,7},{7,6},{8,9},{9,8},{10,11... | collective-permute-start | bytes 393224 | tf_op jit(solution)/shard_map/ppermute | solution.py:20
  43.2 0.0 collective-permute-done.17
  43.2 1.0 %collective-permute-done.18 = bf16[8,8192]{1,0:T(8,128)(2,1)S(1)} collective-permute-done((bf16[8,8192]{1,0:T(8,128)(2,1)S(1)}, bf16[8,8192]{1,0:T(8,128)(2,1)S(1)}, u32[]{:S(2)}, u32[]{:S(2)}) %collective-permute-start.18) | collective-permute-done | bytes 131104 | tf_op jit(solution)/shard_map/ppermute | solution.py:20
  44.2 3.4 %collective-permute-start.19 = (bf16[8,8192]{1,0:T(8,128)(2,1)S(1)}, bf16[8,8192]{1,0:T(8,128)(2,1)S(1)}, u32[]{:S(2)}, u32[]{:S(2)}) collective-permute-start(bf16[8,8192]{1,0:T(8,128)(2,1)S(1)} %add_convert_fusion.3), channel_id=1, source_target_pairs={{0,4},{1,5},{2,6},{3,7},{4,0},{5,1},{6,2},{7,3},{8,12},{9,13},{10,... | collective-permute-start | bytes 393224 | tf_op jit(solution)/shard_map/ppermute | solution.py:20
  47.6 2.2 %collective-permute-done.20 = bf16[8,8192]{1,0:T(8,128)(2,1)S(1)} collective-permute-done((bf16[8,8192]{1,0:T(8,128)(2,1)S(1)}, bf16[8,8192]{1,0:T(8,128)(2,1)S(1)}, u32[]{:S(2)}, u32[]{:S(2)}) %collective-permute-start.20) | collective-permute-done | bytes 131104 | tf_op jit(solution)/shard_map/ppermute | solution.py:20
  49.8 0.7 %collective-permute-start.21 = (bf16[8,8192]{1,0:T(8,128)(2,1)S(1)}, bf16[8,8192]{1,0:T(8,128)(2,1)S(1)}, u32[]{:S(2)}, u32[]{:S(2)}) collective-permute-start(bf16[8,8192]{1,0:T(8,128)(2,1)S(1)} %add_convert_fusion.2), channel_id=1, source_target_pairs={{0,1},{1,0},{2,3},{3,2},{4,5},{5,4},{6,7},{7,6},{8,9},{9,8},{10,11... | collective-permute-start | bytes 393224 | tf_op jit(solution)/shard_map/ppermute | solution.py:20
  50.5 0.0 collective-permute-done.22
  50.5 0.1 collective-permute-start.23
  50.6 3.9 %collective-permute-done.19 = bf16[8,8192]{1,0:T(8,128)(2,1)S(1)} collective-permute-done((bf16[8,8192]{1,0:T(8,128)(2,1)S(1)}, bf16[8,8192]{1,0:T(8,128)(2,1)S(1)}, u32[]{:S(2)}, u32[]{:S(2)}) %collective-permute-start.19) | collective-permute-done | bytes 131104 | tf_op jit(solution)/shard_map/ppermute | solution.py:20
  54.5 0.4 collective-permute-done.21
  54.9 1.5 %collective-permute-done.23 = bf16[8,8192]{1,0:T(8,128)(2,1)S(1)} collective-permute-done((bf16[8,8192]{1,0:T(8,128)(2,1)S(1)}, bf16[8,8192]{1,0:T(8,128)(2,1)S(1)}, u32[]{:S(2)}, u32[]{:S(2)}) %collective-permute-start.23) | collective-permute-done | bytes 131104 | tf_op jit(solution)/shard_map/ppermute | solution.py:20
  56.4 0.7 %add_convert_fusion = bf16[8,8192]{1,0:T(8,128)(2,1)} fusion(bf16[8,8192]{1,0:T(8,128)(2,1)S(1)} %collective-permute-done.23, bf16[8,8192]{1,0:T(8,128)(2,1)S(1)} %collective-permute-done.21, f32[8,8192]{1,0:T(8,128)S(1)} %get-tuple-element.33, bf16[8,8192]{1,0:T(8,128)(2,1)S(1)} %collective-permute-done.19, bf16[8,8192]{1,0:T(8,128)(2,1)S(1)} %copy-done), kind=kLoop, calls=%fused_computation | loop fusion | flops 589824 | bytes 917504 | tf_op jit(solution)/shard_map/convert_element_type | solution.py:186
  (9 shorter events, 0.2 us)
Async XLA Ops:
  0.0 17.9 %copy-start = (bf16[8,8192]{1,0:T(8,128)(2,1)S(1)}, bf16[8,8192]{1,0:T(8,128)(2,1)}, u32[]{:S(2)}) copy-start(bf16[8,8192]{1,0:T(8,128)(2,1)} %refs_0_.5) | copy-start | bytes 393220
  0.0 7.1 %collective-permute-start.2 = (bf16[8,8192]{1,0:T(8,128)(2,1)}, bf16[8,8192]{1,0:T(8,128)(2,1)S(1)}, u32[]{:S(2)}, u32[]{:S(2)}) collective-permute-start(bf16[8,8192]{1,0:T(8,128)(2,1)} %refs_0_.5), channel_id=1, source_target_pairs={{0,1},{1,0},{2,3},{3,2},{4,5},{5,4},{6,7},{7,6},{8,9},{9,8},{10,11... | collective-permute-start | bytes 393224 | tf_op jit(solution)/shard_map/ppermute | solution.py:20
  3.0 7.5 %collective-permute-start = (bf16[8,8192]{1,0:T(8,128)(2,1)}, bf16[8,8192]{1,0:T(8,128)(2,1)S(1)}, u32[]{:S(2)}, u32[]{:S(2)}) collective-permute-start(bf16[8,8192]{1,0:T(8,128)(2,1)} %refs_0_.5), channel_id=1, source_target_pairs={{0,2},{1,3},{2,0},{3,1},{4,6},{5,7},{6,4},{7,5},{8,10},{9,11},{10,... | collective-permute-start | bytes 393224 | tf_op jit(solution)/shard_map/ppermute | solution.py:20
  4.5 12.8 %collective-permute-start.1 = (bf16[8,8192]{1,0:T(8,128)(2,1)}, bf16[8,8192]{1,0:T(8,128)(2,1)S(1)}, u32[]{:S(2)}, u32[]{:S(2)}) collective-permute-start(bf16[8,8192]{1,0:T(8,128)(2,1)} %refs_0_.5), channel_id=1, source_target_pairs={{0,4},{1,5},{2,6},{3,7},{4,0},{5,1},{6,2},{7,3},{8,12},{9,13},{10,... | collective-permute-start | bytes 393224 | tf_op jit(solution)/shard_map/ppermute | solution.py:20
  7.1 13.9 %collective-permute-start.6 = (bf16[8,8192]{1,0:T(8,128)(2,1)S(1)}, bf16[8,8192]{1,0:T(8,128)(2,1)S(1)}, u32[]{:S(2)}, u32[]{:S(2)}) collective-permute-start(bf16[8,8192]{1,0:T(8,128)(2,1)S(1)} %collective-permute-done.2.refs_2_.refs_4_), channel_id=1, source_target_pairs={{0,6},{1,7},{2,4},{3,5},{4,2},{5,3},{6,0},{7,1},{8,14},{9,15},{10,... | collective-permute-start | bytes 393224 | tf_op jit(solution)/shard_map/ppermute | solution.py:20
  10.5 11.1 %collective-permute-start.4 = (bf16[8,8192]{1,0:T(8,128)(2,1)S(1)}, bf16[8,8192]{1,0:T(8,128)(2,1)S(1)}, u32[]{:S(2)}, u32[]{:S(2)}) collective-permute-start(bf16[8,8192]{1,0:T(8,128)(2,1)S(1)} %collective-permute-done.refs_3_.refs_1_), channel_id=1, source_target_pairs={{0,1},{1,0},{2,3},{3,2},{4,5},{5,4},{6,7},{7,6},{8,9},{9,8},{10,11... | collective-permute-start | bytes 393224 | tf_op jit(solution)/shard_map/ppermute | solution.py:20
  17.4 7.6 %copy-start.1 = (f32[8192]{0:T(1024)S(1)}, f32[8192]{0:T(1024)}, u32[]{:S(2)}) copy-start(f32[8192]{0:T(1024)} %param.6) | copy-start | bytes 98308
  17.4 5.0 %collective-permute-start.5 = (bf16[8,8192]{1,0:T(8,128)(2,1)S(1)}, bf16[8,8192]{1,0:T(8,128)(2,1)S(1)}, u32[]{:S(2)}, u32[]{:S(2)}) collective-permute-start(bf16[8,8192]{1,0:T(8,128)(2,1)S(1)} %add.39), channel_id=1, source_target_pairs={{0,1},{1,0},{2,3},{3,2},{4,5},{5,4},{6,7},{7,6},{8,9},{9,8},{10,11... | collective-permute-start | bytes 393224 | tf_op jit(solution)/shard_map/ppermute | solution.py:20
  17.9 5.0 %collective-permute-start.3 = (bf16[8,8192]{1,0:T(8,128)(2,1)S(1)}, bf16[8,8192]{1,0:T(8,128)(2,1)S(1)}, u32[]{:S(2)}, u32[]{:S(2)}) collective-permute-start(bf16[8,8192]{1,0:T(8,128)(2,1)S(1)} %add.39), channel_id=1, source_target_pairs={{0,2},{1,3},{2,0},{3,1},{4,6},{5,7},{6,4},{7,5},{8,10},{9,11},{10,... | collective-permute-start | bytes 393224 | tf_op jit(solution)/shard_map/ppermute | solution.py:20
  17.9 5.2 %collective-permute-start.7 = (bf16[8,8192]{1,0:T(8,128)(2,1)S(1)}, bf16[8,8192]{1,0:T(8,128)(2,1)S(1)}, u32[]{:S(2)}, u32[]{:S(2)}) collective-permute-start(bf16[8,8192]{1,0:T(8,128)(2,1)S(1)} %copy-done), channel_id=1, source_target_pairs={{0,8},{8,0},{1,9},{9,1},{2,10},{10,2},{3,11},{11,3},{4,12},{12,4},... | collective-permute-start | bytes 393224 | tf_op jit(solution)/shard_map/ppermute | solution.py:20
  21.1 2.4 %collective-permute-start.11 = (bf16[8,8192]{1,0:T(8,128)(2,1)S(1)}, bf16[8,8192]{1,0:T(8,128)(2,1)S(1)}, u32[]{:S(2)}, u32[]{:S(2)}) collective-permute-start(bf16[8,8192]{1,0:T(8,128)(2,1)S(1)} %collective-permute-done.2.refs_2_.refs_4_), channel_id=1, source_target_pairs={{0,8},{8,0},{1,9},{9,1},{2,10},{10,2},{3,11},{11,3},{4,12},{12,4},... | collective-permute-start | bytes 393224 | tf_op jit(solution)/shard_map/ppermute | solution.py:20
  21.6 1.9 %collective-permute-start.9 = (bf16[8,8192]{1,0:T(8,128)(2,1)S(1)}, bf16[8,8192]{1,0:T(8,128)(2,1)S(1)}, u32[]{:S(2)}, u32[]{:S(2)}) collective-permute-start(bf16[8,8192]{1,0:T(8,128)(2,1)S(1)} %collective-permute-done.1.refs_2_), channel_id=1, source_target_pairs={{0,8},{8,0},{1,9},{9,1},{2,10},{10,2},{3,11},{11,3},{4,12},{12,4},... | collective-permute-start | bytes 393224 | tf_op jit(solution)/shard_map/ppermute | solution.py:20
  22.4 1.6 %collective-permute-start.8 = (bf16[8,8192]{1,0:T(8,128)(2,1)S(1)}, bf16[8,8192]{1,0:T(8,128)(2,1)S(1)}, u32[]{:S(2)}, u32[]{:S(2)}) collective-permute-start(bf16[8,8192]{1,0:T(8,128)(2,1)S(1)} %collective-permute-done.refs_3_.refs_1_), channel_id=1, source_target_pairs={{0,8},{8,0},{1,9},{9,1},{2,10},{10,2},{3,11},{11,3},{4,12},{12,4},... | collective-permute-start | bytes 393224 | tf_op jit(solution)/shard_map/ppermute | solution.py:20
  22.8 9.4 %slice-start = ((s8[14680064]{0:T(1024)(128)(4,1)}), s8[4194304]{0:T(1024)(128)(4,1)S(1)}, s32[]{:S(2)}) async-start(s8[14680064]{0:T(1024)(128)(4,1)} %bitcast.1), calls=%async_computation | async-start | bytes 8388608
  22.9 1.4 %collective-permute-start.14 = (bf16[8,8192]{1,0:T(8,128)(2,1)S(1)}, bf16[8,8192]{1,0:T(8,128)(2,1)S(1)}, u32[]{:S(2)}, u32[]{:S(2)}) collective-permute-start(bf16[8,8192]{1,0:T(8,128)(2,1)S(1)} %get-tuple-element.41), channel_id=1, source_target_pairs={{0,8},{8,0},{1,9},{9,1},{2,10},{10,2},{3,11},{11,3},{4,12},{12,4},... | collective-permute-start | bytes 393224 | tf_op jit(solution)/shard_map/ppermute | solution.py:20
  23.0 1.4 %collective-permute-start.13 = (bf16[8,8192]{1,0:T(8,128)(2,1)S(1)}, bf16[8,8192]{1,0:T(8,128)(2,1)S(1)}, u32[]{:S(2)}, u32[]{:S(2)}) collective-permute-start(bf16[8,8192]{1,0:T(8,128)(2,1)S(1)} %get-tuple-element.42), channel_id=1, source_target_pairs={{0,8},{8,0},{1,9},{9,1},{2,10},{10,2},{3,11},{11,3},{4,12},{12,4},... | collective-permute-start | bytes 393224 | tf_op jit(solution)/shard_map/ppermute | solution.py:20
  23.5 1.3 %collective-permute-start.12 = (bf16[8,8192]{1,0:T(8,128)(2,1)S(1)}, bf16[8,8192]{1,0:T(8,128)(2,1)S(1)}, u32[]{:S(2)}, u32[]{:S(2)}) collective-permute-start(bf16[8,8192]{1,0:T(8,128)(2,1)S(1)} %get-tuple-element.43), channel_id=1, source_target_pairs={{0,8},{8,0},{1,9},{9,1},{2,10},{10,2},{3,11},{11,3},{4,12},{12,4},... | collective-permute-start | bytes 393224 | tf_op jit(solution)/shard_map/ppermute | solution.py:20
  23.6 1.4 %collective-permute-start.10 = (bf16[8,8192]{1,0:T(8,128)(2,1)S(1)}, bf16[8,8192]{1,0:T(8,128)(2,1)S(1)}, u32[]{:S(2)}, u32[]{:S(2)}) collective-permute-start(bf16[8,8192]{1,0:T(8,128)(2,1)S(1)} %get-tuple-element.44), channel_id=1, source_target_pairs={{0,8},{8,0},{1,9},{9,1},{2,10},{10,2},{3,11},{11,3},{4,12},{12,4},... | collective-permute-start | bytes 393224 | tf_op jit(solution)/shard_map/ppermute | solution.py:20
  25.0 7.3 %slice-start.1 = ((s8[14680064]{0:T(1024)(128)(4,1)}), s8[4194304]{0:T(1024)(128)(4,1)S(1)}, s32[]{:S(2)}) async-start(s8[14680064]{0:T(1024)(128)(4,1)} %bitcast.1), calls=%async_computation.1 | async-start | bytes 8388608
  25.0 7.3 %slice-start.2 = ((s8[14680064]{0:T(1024)(128)(4,1)}), s8[4194304]{0:T(1024)(128)(4,1)S(1)}, s32[]{:S(2)}) async-start(s8[14680064]{0:T(1024)(128)(4,1)} %bitcast.1), calls=%async_computation.2 | async-start | bytes 8388608
  25.0 7.3 %slice-start.3 = ((s8[14680064]{0:T(1024)(128)(4,1)}), s8[2097152]{0:T(1024)(128)(4,1)S(1)}, s32[]{:S(2)}) async-start(s8[14680064]{0:T(1024)(128)(4,1)} %bitcast.1), calls=%async_computation.3 | async-start | bytes 4194304
  34.1 2.7 %collective-permute-start.15 = (bf16[64,6144]{1,0:T(8,128)(2,1)S(1)}, bf16[64,6144]{1,0:T(8,128)(2,1)S(1)}, u32[]{:S(2)}, u32[]{:S(2)}) collective-permute-start(bf16[64,6144]{1,0:T(8,128)(2,1)S(1)} %get-tuple-element.31), channel_id=1, source_target_pairs={{0,8},{8,0},{1,9},{9,1},{2,10},{10,2},{3,11},{11,3},{4,12},{12,4},... | collective-permute-start | bytes 2359304 | tf_op jit(solution)/shard_map/ppermute | solution.py:20
  35.2 1.6 %collective-permute-start.16 = (bf16[64,2048]{1,0:T(8,128)(2,1)S(1)}, bf16[64,2048]{1,0:T(8,128)(2,1)S(1)}, u32[]{:S(2)}, u32[]{:S(2)}) collective-permute-start(bf16[64,2048]{1,0:T(8,128)(2,1)S(1)} %get-tuple-element.32), channel_id=1, source_target_pairs={{0,8},{8,0},{1,9},{9,1},{2,10},{10,2},{3,11},{11,3},{4,12},{12,4},... | collective-permute-start | bytes 786440 | tf_op jit(solution)/shard_map/ppermute | solution.py:20
  37.0 6.2 %collective-permute-start.17 = (bf16[8,8192]{1,0:T(8,128)(2,1)S(1)}, bf16[8,8192]{1,0:T(8,128)(2,1)S(1)}, u32[]{:S(2)}, u32[]{:S(2)}) collective-permute-start(bf16[8,8192]{1,0:T(8,128)(2,1)S(1)} %get-tuple-element.35), channel_id=1, source_target_pairs={{0,1},{1,0},{2,3},{3,2},{4,5},{5,4},{6,7},{7,6},{8,9},{9,8},{10,11... | collective-permute-start | bytes 393224 | tf_op jit(solution)/shard_map/ppermute | solution.py:20
  38.7 5.5 %collective-permute-start.18 = (bf16[8,8192]{1,0:T(8,128)(2,1)S(1)}, bf16[8,8192]{1,0:T(8,128)(2,1)S(1)}, u32[]{:S(2)}, u32[]{:S(2)}) collective-permute-start(bf16[8,8192]{1,0:T(8,128)(2,1)S(1)} %get-tuple-element.36), channel_id=1, source_target_pairs={{0,2},{1,3},{2,0},{3,1},{4,6},{5,7},{6,4},{7,5},{8,10},{9,11},{10,... | collective-permute-start | bytes 393224 | tf_op jit(solution)/shard_map/ppermute | solution.py:20
  40.0 9.8 %collective-permute-start.20 = (bf16[8,8192]{1,0:T(8,128)(2,1)S(1)}, bf16[8,8192]{1,0:T(8,128)(2,1)S(1)}, u32[]{:S(2)}, u32[]{:S(2)}) collective-permute-start(bf16[8,8192]{1,0:T(8,128)(2,1)S(1)} %get-tuple-element.38), channel_id=1, source_target_pairs={{0,6},{1,7},{2,4},{3,5},{4,2},{5,3},{6,0},{7,1},{8,14},{9,15},{10,... | collective-permute-start | bytes 393224 | tf_op jit(solution)/shard_map/ppermute | solution.py:20
  42.6 7.9 %collective-permute-start.22 = (bf16[8,8192]{1,0:T(8,128)(2,1)S(1)}, bf16[8,8192]{1,0:T(8,128)(2,1)S(1)}, u32[]{:S(2)}, u32[]{:S(2)}) collective-permute-start(bf16[8,8192]{1,0:T(8,128)(2,1)S(1)} %get-tuple-element.40), channel_id=1, source_target_pairs={{0,1},{1,0},{2,3},{3,2},{4,5},{5,4},{6,7},{7,6},{8,9},{9,8},{10,11... | collective-permute-start | bytes 393224 | tf_op jit(solution)/shard_map/ppermute | solution.py:20
  44.2 10.3 %collective-permute-start.19 = (bf16[8,8192]{1,0:T(8,128)(2,1)S(1)}, bf16[8,8192]{1,0:T(8,128)(2,1)S(1)}, u32[]{:S(2)}, u32[]{:S(2)}) collective-permute-start(bf16[8,8192]{1,0:T(8,128)(2,1)S(1)} %add_convert_fusion.3), channel_id=1, source_target_pairs={{0,4},{1,5},{2,6},{3,7},{4,0},{5,1},{6,2},{7,3},{8,12},{9,13},{10,... | collective-permute-start | bytes 393224 | tf_op jit(solution)/shard_map/ppermute | solution.py:20
  49.8 5.0 %collective-permute-start.21 = (bf16[8,8192]{1,0:T(8,128)(2,1)S(1)}, bf16[8,8192]{1,0:T(8,128)(2,1)S(1)}, u32[]{:S(2)}, u32[]{:S(2)}) collective-permute-start(bf16[8,8192]{1,0:T(8,128)(2,1)S(1)} %add_convert_fusion.2), channel_id=1, source_target_pairs={{0,1},{1,0},{2,3},{3,2},{4,5},{5,4},{6,7},{7,6},{8,9},{9,8},{10,11... | collective-permute-start | bytes 393224 | tf_op jit(solution)/shard_map/ppermute | solution.py:20
  50.5 5.9 %collective-permute-start.23 = (bf16[8,8192]{1,0:T(8,128)(2,1)S(1)}, bf16[8,8192]{1,0:T(8,128)(2,1)S(1)}, u32[]{:S(2)}, u32[]{:S(2)}) collective-permute-start(bf16[8,8192]{1,0:T(8,128)(2,1)S(1)} %add_convert_fusion.1), channel_id=1, source_target_pairs={{0,2},{1,3},{2,0},{3,1},{4,6},{5,7},{6,4},{7,5},{8,10},{9,11},{10,... | collective-permute-start | bytes 393224 | tf_op jit(solution)/shard_map/ppermute | solution.py:20

commit v4 on v3

--- a/solution.py
+++ b/solution.py
@@ -11,7 +11,7 @@
 F32 = jnp.float32
 SPLIT = (3, 1)
 COST = 4
-FETCHES = (4, 2)
+FETCHES = (2, 4)
 CHUNK = 1024
 ORDER = (0, 2, 3, 6, 1, 5, 7, 4)
 
@@ -63,7 +63,9 @@
 
 
 def hidden_kernel(held, *refs):
-    pieces, gain, rest = refs[:16], refs[16], refs[17:]
+    near, (far_last, gain), rest = refs[:12], refs[12:14], refs[14:]
+    pieces = list(near) + [far_last.at[8 * i : 8 * i + 8] for i in range(4)]
+    pieces = [pieces[i] for i in ORDER + tuple(8 + i for i in ORDER)]
     gates, ups, (gate, up, out, gate_late, up_late, sems) = rest[:held], rest[held : 2 * held], rest[2 * held :]
     late, depth = gate_late.shape[:2]
     base = gate.shape[0] - late * depth
@@ -129,22 +131,22 @@
 
     sizes = [CHUNK * n for n in FETCHES]
     at1, at2, at4 = hop(tokens, 1), hop(tokens, 2), hop(tokens, 4)
-    early = fetch(gate_weight, up_weight, 0, sizes[0], tokens.shape, [at1, at2])
+    early = fetch(gate_weight, up_weight, 0, sizes[0], tokens.shape, [])
     at4t = tie(at4, early[2])
-    at7, at3 = hop(at1, 6), hop(at2, 1)
+    at7, at3 = hop(tie(at1, early[2]), 6), hop(tie(at2, early[2]), 1)
     at6, at5 = hop(at4t, 2), hop(at4t, 1)
     later = fetch(gate_weight, up_weight, sizes[0], sizes[1], tokens.shape, [at4])
     mine = [tokens, at1, at2, at4]
     last = [at7, at3, at6, at5]
-    pieces = mine + last
-    pieces += [flip(p, "dp", 2, 1) for p in mine + [tie(p, later[2]) for p in last]]
+    far_mine = [flip(p, "dp", 2, 1) for p in mine]
+    far_last = flip(jnp.concatenate([tie(p, later[2]) for p in last], axis=0), "dp", 2, 1)
     held = [early, later]
-    pieces = [pieces[i] for i in ORDER] + [pieces[8 + i] for i in ORDER]
+    pieces = mine + last + far_mine + [far_last]
     late = ((width - sum(sizes)) // CHUNK, CHUNK, units)
     hidden = pl.pallas_call(
         functools.partial(hidden_kernel, len(held)),
         out_shape=jax.ShapeDtypeStruct((16 * rows, units), BF),
-        in_specs=vmem_specs(17 + 2 * len(held)) + [pl.BlockSpec(memory_space=pltpu.HBM)] * 2,
+        in_specs=vmem_specs(14 + 2 * len(held)) + [pl.BlockSpec(memory_space=pltpu.HBM)] * 2,
         out_specs=vmem_specs(1)[0],
         scratch_shapes=[pltpu.VMEM(late, BF), pltpu.VMEM(late, BF), pltpu.SemaphoreType.DMA((late[0], 2))],
         compiler_params=pltpu.CompilerParams(vmem_limit_bytes=24 * 2**20),

time: 57.3 us -> 54.6 us (0.953)
  Pallas kernels: 18.3 us -> 16.9 us
  waiting for transfers between devices: 12.6 us -> 11.5 us
  starting transfers between devices: 25.2 us -> 24.5 us
    pallas_call x1, Pallas kernels: 7.23 us -> 5.83 us  [per_device(): pl.pallas_call(functools.partial(hidden_kernel, len(held)), out_shape=jax...]
    ppermute x24 -> x21, waiting for transfers between devices: 12.6 us -> 11.5 us  [flip(): return lax.ppermute(x, axis, [(i, i ^ mask) for i in range(size)])]
    ppermute x24 -> x21, starting transfers between devices: 25.2 us -> 24.5 us  [flip(): return lax.ppermute(x, axis, [(i, i ^ mask) for i in range(size)])]
  transfers between devices with their start and end apart: 24 -> 21, of which waited for: 13 -> 12; matrix products, arithmetic and copies ran while one was open for 0% -> 0% of each run, Pallas kernels for 16% -> 17%
where the time goes in v4:
time: 54.6 us; the launch traced here: 54.5 us
  starting transfers between devices  24.5 us (45%)
  Pallas kernels  16.9 us (31%)
  waiting for transfers between devices  11.5 us (21%)
  other arithmetic  0.94 us (2%)
    ppermute x21, starting transfers between devices, flip(): return lax.ppermute(x, axis, [(i, i ^ mask) for i in range(size)])  24.5 us
    ppermute x21, waiting for transfers between devices, flip(): return lax.ppermute(x, axis, [(i, i ^ mask) for i in range(size)])  11.5 us
    pallas_call x2, Pallas kernels, fetch(): pl.pallas_call(functools.partial(fetch_kernel, first, len(after)), out_sh...  8.42 us
    pallas_call x1, Pallas kernels, per_device(): pl.pallas_call(functools.partial(hidden_kernel, len(held)), out_shape=jax...  5.83 us
    pallas_call x2, Pallas kernels, per_device(): pl.pallas_call(down_kernel, out_shape=(jax.ShapeDtypeStruct((8 * rows, st...  2.52 us
  transfers between devices with their start and end apart: 21, of which 12 were waited for; matrix products, arithmetic and copies ran while one was open for 0% of the time, Pallas kernels for 17%

profile of v4, /device:TPU:0, one launch (start us, length us, event | category | flops | bytes accessed | tf_op | source)
XLA Modules:
  0.0 54.5 jit_solution(18188955302397194264)
XLA Ops:
  0.0 4.0 %collective-permute-start.2 = (bf16[8,8192]{1,0:T(8,128)(2,1)}, bf16[8,8192]{1,0:T(8,128)(2,1)S(1)}, u32[]{:S(2)}, u32[]{:S(2)}) collective-permute-start(bf16[8,8192]{1,0:T(8,128)(2,1)} %refs_0_.5), channel_id=1, source_target_pairs={{0,4},{1,5},{2,6},{3,7},{4,0},{5,1},{6,2},{7,3},{8,12},{9,13},{10,... | collective-permute-start | bytes 393224 | tf_op jit(solution)/shard_map/ppermute | solution.py:20
  4.0 1.5 %collective-permute-start = (bf16[8,8192]{1,0:T(8,128)(2,1)}, bf16[8,8192]{1,0:T(8,128)(2,1)S(1)}, u32[]{:S(2)}, u32[]{:S(2)}) collective-permute-start(bf16[8,8192]{1,0:T(8,128)(2,1)} %refs_0_.5), channel_id=1, source_target_pairs={{0,1},{1,0},{2,3},{3,2},{4,5},{5,4},{6,7},{7,6},{8,9},{9,8},{10,11... | collective-permute-start | bytes 393224 | tf_op jit(solution)/shard_map/ppermute | solution.py:20
  5.6 1.6 %collective-permute-start.1 = (bf16[8,8192]{1,0:T(8,128)(2,1)}, bf16[8,8192]{1,0:T(8,128)(2,1)S(1)}, u32[]{:S(2)}, u32[]{:S(2)}) collective-permute-start(bf16[8,8192]{1,0:T(8,128)(2,1)} %refs_0_.5), channel_id=1, source_target_pairs={{0,2},{1,3},{2,0},{3,1},{4,6},{5,7},{6,4},{7,5},{8,10},{9,11},{10,... | collective-permute-start | bytes 393224 | tf_op jit(solution)/shard_map/ppermute | solution.py:20
  7.1 3.2 %fetch_0.1 = (bf16[2048,896]{1,0:T(8,128)(2,1)S(1)}, bf16[2048,896]{1,0:T(8,128)(2,1)S(1)}, bf16[8,8192]{1,0:T(8,128)(2,1)S(1)}) custom-call(bf16[8192,896]{1,0:T(8,128)(2,1)} %refs_18_.1, bf16[8192,896]{1,0:T(8,128)(2,1)} %refs_19_.1), custom_call_target="tpu_custom_call" | custom-call | bytes 7340032 | tf_op jit(solution)/shard_map/fetch_0/pallas_call | solution.py:53
  10.3 0.3 collective-permute-done.2.refs_2_.refs_3_
  10.7 0.0 collective-permute-done.refs_1_
  10.7 1.4 %collective-permute-done.1.refs_2_ = bf16[8,8192]{1,0:T(8,128)(2,1)S(1)} collective-permute-done((bf16[8,8192]{1,0:T(8,128)(2,1)}, bf16[8,8192]{1,0:T(8,128)(2,1)S(1)}, u32[]{:S(2)}, u32[]{:S(2)}) %collective-permute-start.1) | collective-permute-done | bytes 131104 | tf_op jit(solution)/shard_map/ppermute | solution.py:20
  12.1 0.3 collective-permute-start.5
  12.4 1.5 %collective-permute-start.6 = (bf16[8,8192]{1,0:T(8,128)(2,1)S(1)}, bf16[8,8192]{1,0:T(8,128)(2,1)S(1)}, u32[]{:S(2)}, u32[]{:S(2)}) collective-permute-start(bf16[8,8192]{1,0:T(8,128)(2,1)S(1)} %get-tuple-element.45), channel_id=1, source_target_pairs={{0,1},{1,0},{2,3},{3,2},{4,5},{5,4},{6,7},{7,6},{8,9},{9,8},{10,11... | collective-permute-start | bytes 393224 | tf_op jit(solution)/shard_map/ppermute | solution.py:20
  13.9 1.9 %collective-permute-start.3 = (bf16[8,8192]{1,0:T(8,128)(2,1)S(1)}, bf16[8,8192]{1,0:T(8,128)(2,1)S(1)}, u32[]{:S(2)}, u32[]{:S(2)}) collective-permute-start(bf16[8,8192]{1,0:T(8,128)(2,1)S(1)} %get-tuple-element.47), channel_id=1, source_target_pairs={{0,6},{1,7},{2,4},{3,5},{4,2},{5,3},{6,0},{7,1},{8,14},{9,15},{10,... | collective-permute-start | bytes 393224 | tf_op jit(solution)/shard_map/ppermute | solution.py:20
  15.8 0.0 copy-start
  15.8 0.0 copy-start.1
  15.8 1.2 %collective-permute-start.4 = (bf16[8,8192]{1,0:T(8,128)(2,1)S(1)}, bf16[8,8192]{1,0:T(8,128)(2,1)S(1)}, u32[]{:S(2)}, u32[]{:S(2)}) collective-permute-start(bf16[8,8192]{1,0:T(8,128)(2,1)S(1)} %get-tuple-element.46), channel_id=1, source_target_pairs={{0,1},{1,0},{2,3},{3,2},{4,5},{5,4},{6,7},{7,6},{8,9},{9,8},{10,11... | collective-permute-start | bytes 393224 | tf_op jit(solution)/shard_map/ppermute | solution.py:20
  17.0 5.2 %fetch_2048.1 = (bf16[4096,896]{1,0:T(8,128)(2,1)S(1)}, bf16[4096,896]{1,0:T(8,128)(2,1)S(1)}, bf16[8,8192]{1,0:T(8,128)(2,1)S(1)}) custom-call(bf16[8192,896]{1,0:T(8,128)(2,1)} %refs_18_.1, bf16[8192,896]{1,0:T(8,128)(2,1)} %refs_19_.1, bf16[8,8192]{1,0:T(8,128)(2,1)S(1)} %collective-permute-done.2.refs_2_.refs_3_), custom_call_target="tpu_custom_call" | custom-call | bytes 14680064 | tf_op jit(solution)/shard_map/fetch_2048/pallas_call | solution.py:53
  22.3 0.0 collective-permute-done.5.refs_6_
  22.3 0.0 collective-permute-done.6.refs_7_
  22.3 0.0 collective-permute-done.3.refs_4_
  22.3 0.0 collective-permute-done.4.refs_5_
  22.3 0.0 slice-start
  22.4 0.1 collective-permute-start.11
  22.5 0.0 copy-done
  22.5 0.5 collective-permute-start.7
  23.0 0.1 collective-permute-start.10
  23.1 0.4 collective-permute-start.8
  23.5 0.1 collective-permute-start.9
  23.6 1.0 %collective-permute-done.7.refs_8_ = bf16[8,8192]{1,0:T(8,128)(2,1)S(1)} collective-permute-done((bf16[8,8192]{1,0:T(8,128)(2,1)S(1)}, bf16[8,8192]{1,0:T(8,128)(2,1)S(1)}, u32[]{:S(2)}, u32[]{:S(2)}) %collective-permute-start.7) | collective-permute-done | bytes 131104 | tf_op jit(solution)/shard_map/ppermute | solution.py:20
  24.6 0.2 collective-permute-done.10.refs_11_
  24.8 0.2 collective-permute-done.8.refs_9_
  25.0 0.2 collective-permute-done.9.refs_10_
  25.1 0.0 collective-permute-done.11.refs_12_
  25.1 0.0 copy-done.1
  25.1 0.0 slice-start.1
  25.2 0.0 slice-start.2
  25.2 0.0 slice-start.3
  25.2 5.8 %hidden.1 = bf16[128,896]{1,0:T(8,128)(2,1)S(1)} custom-call(bf16[8,8192]{1,0:T(8,128)(2,1)S(1)} %copy-done, bf16[8,8192]{1,0:T(8,128)(2,1)S(1)} %collective-permute-done.refs_1_, bf16[8,8192]{1,0:T(8,128)(2,1)S(1)} %collective-permute-done.1.refs_2_, bf16[8,8192]{1,0:T(8,128)(2,1)S(1)} %collective-permute-done.2.refs_2_.refs_3_, ...), custom_call_target="tpu_custom_call" | custom-call | tf_op jit(solution)/shard_map/hidden/pallas_call | solution.py:146
  31.0 0.0 slice-done
  31.0 0.0 slice-done.1
  31.0 0.0 slice-done.2
  31.0 0.4 slice-done.3
  31.4 1.8 %down.4 = (f32[64,6144]{1,0:T(8,128)S(1)}, bf16[64,6144]{1,0:T(8,128)(2,1)S(1)}) custom-call(bf16[128,896]{1,0:T(8,128)(2,1)S(1)} %hidden.1, bf16[896,8192]{1,0:T(8,128)(2,1)S(1)} %bitcast.2), custom_call_target="tpu_custom_call" | custom-call | tf_op jit(solution)/shard_map/down/pallas_call | solution.py:159
  33.2 0.2 collective-permute-start.12
  33.4 0.7 %down.6 = (f32[64,2048]{1,0:T(8,128)S(1)}, bf16[64,2048]{1,0:T(8,128)(2,1)S(1)}) custom-call(bf16[128,896]{1,0:T(8,128)(2,1)S(1)} %hidden.1, bf16[896,8192]{1,0:T(8,128)(2,1)S(1)} %bitcast.2), custom_call_target="tpu_custom_call" | custom-call | tf_op jit(solution)/shard_map/down/pallas_call | solution.py:159
  34.2 0.5 collective-permute-start.13
  34.6 1.4 %collective-permute-done.13.refs_3_ = bf16[64,2048]{1,0:T(8,128)(2,1)S(1)} collective-permute-done((bf16[64,2048]{1,0:T(8,128)(2,1)S(1)}, bf16[64,2048]{1,0:T(8,128)(2,1)S(1)}, u32[]{:S(2)}, u32[]{:S(2)}) %collective-permute-start.13) | collective-permute-done | bytes 262176 | tf_op jit(solution)/shard_map/ppermute | solution.py:20
  36.0 0.0 collective-permute-done.12.refs_2_
  36.0 0.2 pair.1
  36.1 0.9 %collective-permute-start.14 = (bf16[8,8192]{1,0:T(8,128)(2,1)S(1)}, bf16[8,8192]{1,0:T(8,128)(2,1)S(1)}, u32[]{:S(2)}, u32[]{:S(2)}) collective-permute-start(bf16[8,8192]{1,0:T(8,128)(2,1)S(1)} %get-tuple-element.35), channel_id=1, source_target_pairs={{0,1},{1,0},{2,3},{3,2},{4,5},{5,4},{6,7},{7,6},{8,9},{9,8},{10,11... | collective-permute-start | bytes 393224 | tf_op jit(solution)/shard_map/ppermute | solution.py:20
  37.0 1.1 %collective-permute-start.15 = (bf16[8,8192]{1,0:T(8,128)(2,1)S(1)}, bf16[8,8192]{1,0:T(8,128)(2,1)S(1)}, u32[]{:S(2)}, u32[]{:S(2)}) collective-permute-start(bf16[8,8192]{1,0:T(8,128)(2,1)S(1)} %get-tuple-element.36), channel_id=1, source_target_pairs={{0,2},{1,3},{2,0},{3,1},{4,6},{5,7},{6,4},{7,5},{8,10},{9,11},{10,... | collective-permute-start | bytes 393224 | tf_op jit(solution)/shard_map/ppermute | solution.py:20
  38.1 1.8 %collective-permute-start.17 = (bf16[8,8192]{1,0:T(8,128)(2,1)S(1)}, bf16[8,8192]{1,0:T(8,128)(2,1)S(1)}, u32[]{:S(2)}, u32[]{:S(2)}) collective-permute-start(bf16[8,8192]{1,0:T(8,128)(2,1)S(1)} %get-tuple-element.38), channel_id=1, source_target_pairs={{0,6},{1,7},{2,4},{3,5},{4,2},{5,3},{6,0},{7,1},{8,14},{9,15},{10,... | collective-permute-start | bytes 393224 | tf_op jit(solution)/shard_map/ppermute | solution.py:20
  39.9 1.5 %collective-permute-start.19 = (bf16[8,8192]{1,0:T(8,128)(2,1)S(1)}, bf16[8,8192]{1,0:T(8,128)(2,1)S(1)}, u32[]{:S(2)}, u32[]{:S(2)}) collective-permute-start(bf16[8,8192]{1,0:T(8,128)(2,1)S(1)} %get-tuple-element.40), channel_id=1, source_target_pairs={{0,1},{1,0},{2,3},{3,2},{4,5},{5,4},{6,7},{7,6},{8,9},{9,8},{10,11... | collective-permute-start | bytes 393224 | tf_op jit(solution)/shard_map/ppermute | solution.py:20
  41.3 0.5 collective-permute-done.14
  41.8 0.8 %collective-permute-done.15 = bf16[8,8192]{1,0:T(8,128)(2,1)S(1)} collective-permute-done((bf16[8,8192]{1,0:T(8,128)(2,1)S(1)}, bf16[8,8192]{1,0:T(8,128)(2,1)S(1)}, u32[]{:S(2)}, u32[]{:S(2)}) %collective-permute-start.15) | collective-permute-done | bytes 131104 | tf_op jit(solution)/shard_map/ppermute | solution.py:20
  42.6 2.2 %collective-permute-start.16 = (bf16[8,8192]{1,0:T(8,128)(2,1)S(1)}, bf16[8,8192]{1,0:T(8,128)(2,1)S(1)}, u32[]{:S(2)}, u32[]{:S(2)}) collective-permute-start(bf16[8,8192]{1,0:T(8,128)(2,1)S(1)} %add_convert_fusion.3), channel_id=1, source_target_pairs={{0,4},{1,5},{2,6},{3,7},{4,0},{5,1},{6,2},{7,3},{8,12},{9,13},{10,... | collective-permute-start | bytes 393224 | tf_op jit(solution)/shard_map/ppermute | solution.py:20
  44.9 1.5 %collective-permute-done.17 = bf16[8,8192]{1,0:T(8,128)(2,1)S(1)} collective-permute-done((bf16[8,8192]{1,0:T(8,128)(2,1)S(1)}, bf16[8,8192]{1,0:T(8,128)(2,1)S(1)}, u32[]{:S(2)}, u32[]{:S(2)}) %collective-permute-start.17) | collective-permute-done | bytes 131104 | tf_op jit(solution)/shard_map/ppermute | solution.py:20
  46.4 1.9 %collective-permute-start.18 = (bf16[8,8192]{1,0:T(8,128)(2,1)S(1)}, bf16[8,8192]{1,0:T(8,128)(2,1)S(1)}, u32[]{:S(2)}, u32[]{:S(2)}) collective-permute-start(bf16[8,8192]{1,0:T(8,128)(2,1)S(1)} %add_convert_fusion.2), channel_id=1, source_target_pairs={{0,1},{1,0},{2,3},{3,2},{4,5},{5,4},{6,7},{7,6},{8,9},{9,8},{10,11... | collective-permute-start | bytes 393224 | tf_op jit(solution)/shard_map/ppermute | solution.py:20
  48.3 0.0 collective-permute-done.19
  48.4 1.3 %collective-permute-start.20 = (bf16[8,8192]{1,0:T(8,128)(2,1)S(1)}, bf16[8,8192]{1,0:T(8,128)(2,1)S(1)}, u32[]{:S(2)}, u32[]{:S(2)}) collective-permute-start(bf16[8,8192]{1,0:T(8,128)(2,1)S(1)} %add_convert_fusion.1), channel_id=1, source_target_pairs={{0,2},{1,3},{2,0},{3,1},{4,6},{5,7},{6,4},{7,5},{8,10},{9,11},{10,... | collective-permute-start | bytes 393224 | tf_op jit(solution)/shard_map/ppermute | solution.py:20
  49.7 2.4 %collective-permute-done.16 = bf16[8,8192]{1,0:T(8,128)(2,1)S(1)} collective-permute-done((bf16[8,8192]{1,0:T(8,128)(2,1)S(1)}, bf16[8,8192]{1,0:T(8,128)(2,1)S(1)}, u32[]{:S(2)}, u32[]{:S(2)}) %collective-permute-start.16) | collective-permute-done | bytes 131104 | tf_op jit(solution)/shard_map/ppermute | solution.py:20
  52.0 0.0 collective-permute-done.18
  52.0 1.7 %collective-permute-done.20 = bf16[8,8192]{1,0:T(8,128)(2,1)S(1)} collective-permute-done((bf16[8,8192]{1,0:T(8,128)(2,1)S(1)}, bf16[8,8192]{1,0:T(8,128)(2,1)S(1)}, u32[]{:S(2)}, u32[]{:S(2)}) %collective-permute-start.20) | collective-permute-done | bytes 131104 | tf_op jit(solution)/shard_map/ppermute | solution.py:20
  53.7 0.7 %add_convert_fusion = bf16[8,8192]{1,0:T(8,128)(2,1)} fusion(bf16[8,8192]{1,0:T(8,128)(2,1)S(1)} %collective-permute-done.20, bf16[8,8192]{1,0:T(8,128)(2,1)S(1)} %collective-permute-done.18, f32[8,8192]{1,0:T(8,128)S(1)} %get-tuple-element.33, bf16[8,8192]{1,0:T(8,128)(2,1)S(1)} %collective-permute-done.16, bf16[8,8192]{1,0:T(8,128)(2,1)S(1)} %copy-done), kind=kLoop, calls=%fused_computation.1 | loop fusion | flops 589824 | bytes 917504 | tf_op jit(solution)/shard_map/convert_element_type | solution.py:188
  (7 shorter events, 0.2 us)
Async XLA Ops:
  0.0 10.7 %collective-permute-start.2 = (bf16[8,8192]{1,0:T(8,128)(2,1)}, bf16[8,8192]{1,0:T(8,128)(2,1)S(1)}, u32[]{:S(2)}, u32[]{:S(2)}) collective-permute-start(bf16[8,8192]{1,0:T(8,128)(2,1)} %refs_0_.5), channel_id=1, source_target_pairs={{0,4},{1,5},{2,6},{3,7},{4,0},{5,1},{6,2},{7,3},{8,12},{9,13},{10,... | collective-permute-start | bytes 393224 | tf_op jit(solution)/shard_map/ppermute | solution.py:20
  4.0 6.6 %collective-permute-start = (bf16[8,8192]{1,0:T(8,128)(2,1)}, bf16[8,8192]{1,0:T(8,128)(2,1)S(1)}, u32[]{:S(2)}, u32[]{:S(2)}) collective-permute-start(bf16[8,8192]{1,0:T(8,128)(2,1)} %refs_0_.5), channel_id=1, source_target_pairs={{0,1},{1,0},{2,3},{3,2},{4,5},{5,4},{6,7},{7,6},{8,9},{9,8},{10,11... | collective-permute-start | bytes 393224 | tf_op jit(solution)/shard_map/ppermute | solution.py:20
  5.6 6.5 %collective-permute-start.1 = (bf16[8,8192]{1,0:T(8,128)(2,1)}, bf16[8,8192]{1,0:T(8,128)(2,1)S(1)}, u32[]{:S(2)}, u32[]{:S(2)}) collective-permute-start(bf16[8,8192]{1,0:T(8,128)(2,1)} %refs_0_.5), channel_id=1, source_target_pairs={{0,2},{1,3},{2,0},{3,1},{4,6},{5,7},{6,4},{7,5},{8,10},{9,11},{10,... | collective-permute-start | bytes 393224 | tf_op jit(solution)/shard_map/ppermute | solution.py:20
  12.1 10.1 %collective-permute-start.5 = (bf16[8,8192]{1,0:T(8,128)(2,1)S(1)}, bf16[8,8192]{1,0:T(8,128)(2,1)S(1)}, u32[]{:S(2)}, u32[]{:S(2)}) collective-permute-start(bf16[8,8192]{1,0:T(8,128)(2,1)S(1)} %get-tuple-element.45), channel_id=1, source_target_pairs={{0,2},{1,3},{2,0},{3,1},{4,6},{5,7},{6,4},{7,5},{8,10},{9,11},{10,... | collective-permute-start | bytes 393224 | tf_op jit(solution)/shard_map/ppermute | solution.py:20
  12.4 9.8 %collective-permute-start.6 = (bf16[8,8192]{1,0:T(8,128)(2,1)S(1)}, bf16[8,8192]{1,0:T(8,128)(2,1)S(1)}, u32[]{:S(2)}, u32[]{:S(2)}) collective-permute-start(bf16[8,8192]{1,0:T(8,128)(2,1)S(1)} %get-tuple-element.45), channel_id=1, source_target_pairs={{0,1},{1,0},{2,3},{3,2},{4,5},{5,4},{6,7},{7,6},{8,9},{9,8},{10,11... | collective-permute-start | bytes 393224 | tf_op jit(solution)/shard_map/ppermute | solution.py:20
  13.9 8.4 %collective-permute-start.3 = (bf16[8,8192]{1,0:T(8,128)(2,1)S(1)}, bf16[8,8192]{1,0:T(8,128)(2,1)S(1)}, u32[]{:S(2)}, u32[]{:S(2)}) collective-permute-start(bf16[8,8192]{1,0:T(8,128)(2,1)S(1)} %get-tuple-element.47), channel_id=1, source_target_pairs={{0,6},{1,7},{2,4},{3,5},{4,2},{5,3},{6,0},{7,1},{8,14},{9,15},{10,... | collective-permute-start | bytes 393224 | tf_op jit(solution)/shard_map/ppermute | solution.py:20
  15.8 6.7 %copy-start = (bf16[8,8192]{1,0:T(8,128)(2,1)S(1)}, bf16[8,8192]{1,0:T(8,128)(2,1)}, u32[]{:S(2)}) copy-start(bf16[8,8192]{1,0:T(8,128)(2,1)} %refs_0_.5) | copy-start | bytes 393220
  15.8 9.3 %copy-start.1 = (f32[8192]{0:T(1024)S(1)}, f32[8192]{0:T(1024)}, u32[]{:S(2)}) copy-start(f32[8192]{0:T(1024)} %param.6) | copy-start | bytes 98308
  15.8 6.5 %collective-permute-start.4 = (bf16[8,8192]{1,0:T(8,128)(2,1)S(1)}, bf16[8,8192]{1,0:T(8,128)(2,1)S(1)}, u32[]{:S(2)}, u32[]{:S(2)}) collective-permute-start(bf16[8,8192]{1,0:T(8,128)(2,1)S(1)} %get-tuple-element.46), channel_id=1, source_target_pairs={{0,1},{1,0},{2,3},{3,2},{4,5},{5,4},{6,7},{7,6},{8,9},{9,8},{10,11... | collective-permute-start | bytes 393224 | tf_op jit(solution)/shard_map/ppermute | solution.py:20
  22.3 8.7 %slice-start = ((s8[14680064]{0:T(1024)(128)(4,1)}), s8[4194304]{0:T(1024)(128)(4,1)S(1)}, s32[]{:S(2)}) async-start(s8[14680064]{0:T(1024)(128)(4,1)} %bitcast.1), calls=%async_computation | async-start | bytes 8388608
  22.4 2.7 %collective-permute-start.11 = (bf16[32,8192]{1,0:T(8,128)(2,1)S(1)}, bf16[32,8192]{1,0:T(8,128)(2,1)S(1)}, u32[]{:S(2)}, u32[]{:S(2)}) collective-permute-start(bf16[32,8192]{1,0:T(8,128)(2,1)S(1)} %pad_maximum_fusion), channel_id=1, source_target_pairs={{0,8},{8,0},{1,9},{9,1},{2,10},{10,2},{3,11},{11,3},{4,12},{12,4},... | collective-permute-start | bytes 1572872 | tf_op jit(solution)/shard_map/ppermute | solution.py:20
  22.5 2.1 %collective-permute-start.7 = (bf16[8,8192]{1,0:T(8,128)(2,1)S(1)}, bf16[8,8192]{1,0:T(8,128)(2,1)S(1)}, u32[]{:S(2)}, u32[]{:S(2)}) collective-permute-start(bf16[8,8192]{1,0:T(8,128)(2,1)S(1)} %copy-done), channel_id=1, source_target_pairs={{0,8},{8,0},{1,9},{9,1},{2,10},{10,2},{3,11},{11,3},{4,12},{12,4},... | collective-permute-start | bytes 393224 | tf_op jit(solution)/shard_map/ppermute | solution.py:20
  23.0 1.8 %collective-permute-start.10 = (bf16[8,8192]{1,0:T(8,128)(2,1)S(1)}, bf16[8,8192]{1,0:T(8,128)(2,1)S(1)}, u32[]{:S(2)}, u32[]{:S(2)}) collective-permute-start(bf16[8,8192]{1,0:T(8,128)(2,1)S(1)} %collective-permute-done.2.refs_2_.refs_3_), channel_id=1, source_target_pairs={{0,8},{8,0},{1,9},{9,1},{2,10},{10,2},{3,11},{11,3},{4,12},{12,4},... | collective-permute-start | bytes 393224 | tf_op jit(solution)/shard_map/ppermute | solution.py:20
  23.1 1.9 %collective-permute-start.8 = (bf16[8,8192]{1,0:T(8,128)(2,1)S(1)}, bf16[8,8192]{1,0:T(8,128)(2,1)S(1)}, u32[]{:S(2)}, u32[]{:S(2)}) collective-permute-start(bf16[8,8192]{1,0:T(8,128)(2,1)S(1)} %collective-permute-done.refs_1_), channel_id=1, source_target_pairs={{0,8},{8,0},{1,9},{9,1},{2,10},{10,2},{3,11},{11,3},{4,12},{12,4},... | collective-permute-start | bytes 393224 | tf_op jit(solution)/shard_map/ppermute | solution.py:20
  23.5 1.6 %collective-permute-start.9 = (bf16[8,8192]{1,0:T(8,128)(2,1)S(1)}, bf16[8,8192]{1,0:T(8,128)(2,1)S(1)}, u32[]{:S(2)}, u32[]{:S(2)}) collective-permute-start(bf16[8,8192]{1,0:T(8,128)(2,1)S(1)} %collective-permute-done.1.refs_2_), channel_id=1, source_target_pairs={{0,8},{8,0},{1,9},{9,1},{2,10},{10,2},{3,11},{11,3},{4,12},{12,4},... | collective-permute-start | bytes 393224 | tf_op jit(solution)/shard_map/ppermute | solution.py:20
  25.1 5.9 %slice-start.1 = ((s8[14680064]{0:T(1024)(128)(4,1)}), s8[4194304]{0:T(1024)(128)(4,1)S(1)}, s32[]{:S(2)}) async-start(s8[14680064]{0:T(1024)(128)(4,1)} %bitcast.1), calls=%async_computation.1 | async-start | bytes 8388608
  25.2 5.9 %slice-start.2 = ((s8[14680064]{0:T(1024)(128)(4,1)}), s8[4194304]{0:T(1024)(128)(4,1)S(1)}, s32[]{:S(2)}) async-start(s8[14680064]{0:T(1024)(128)(4,1)} %bitcast.1), calls=%async_computation.2 | async-start | bytes 8388608
  25.2 6.3 %slice-start.3 = ((s8[14680064]{0:T(1024)(128)(4,1)}), s8[2097152]{0:T(1024)(128)(4,1)S(1)}, s32[]{:S(2)}) async-start(s8[14680064]{0:T(1024)(128)(4,1)} %bitcast.1), calls=%async_computation.3 | async-start | bytes 4194304
  33.2 2.7 %collective-permute-start.12 = (bf16[64,6144]{1,0:T(8,128)(2,1)S(1)}, bf16[64,6144]{1,0:T(8,128)(2,1)S(1)}, u32[]{:S(2)}, u32[]{:S(2)}) collective-permute-start(bf16[64,6144]{1,0:T(8,128)(2,1)S(1)} %get-tuple-element.31), channel_id=1, source_target_pairs={{0,8},{8,0},{1,9},{9,1},{2,10},{10,2},{3,11},{11,3},{4,12},{12,4},... | collective-permute-start | bytes 2359304 | tf_op jit(solution)/shard_map/ppermute | solution.py:20
  34.2 1.8 %collective-permute-start.13 = (bf16[64,2048]{1,0:T(8,128)(2,1)S(1)}, bf16[64,2048]{1,0:T(8,128)(2,1)S(1)}, u32[]{:S(2)}, u32[]{:S(2)}) collective-permute-start(bf16[64,2048]{1,0:T(8,128)(2,1)S(1)} %get-tuple-element.32), channel_id=1, source_target_pairs={{0,8},{8,0},{1,9},{9,1},{2,10},{10,2},{3,11},{11,3},{4,12},{12,4},... | collective-permute-start | bytes 786440 | tf_op jit(solution)/shard_map/ppermute | solution.py:20
  36.1 5.6 %collective-permute-start.14 = (bf16[8,8192]{1,0:T(8,128)(2,1)S(1)}, bf16[8,8192]{1,0:T(8,128)(2,1)S(1)}, u32[]{:S(2)}, u32[]{:S(2)}) collective-permute-start(bf16[8,8192]{1,0:T(8,128)(2,1)S(1)} %get-tuple-element.35), channel_id=1, source_target_pairs={{0,1},{1,0},{2,3},{3,2},{4,5},{5,4},{6,7},{7,6},{8,9},{9,8},{10,11... | collective-permute-start | bytes 393224 | tf_op jit(solution)/shard_map/ppermute | solution.py:20
  37.0 5.6 %collective-permute-start.15 = (bf16[8,8192]{1,0:T(8,128)(2,1)S(1)}, bf16[8,8192]{1,0:T(8,128)(2,1)S(1)}, u32[]{:S(2)}, u32[]{:S(2)}) collective-permute-start(bf16[8,8192]{1,0:T(8,128)(2,1)S(1)} %get-tuple-element.36), channel_id=1, source_target_pairs={{0,2},{1,3},{2,0},{3,1},{4,6},{5,7},{6,4},{7,5},{8,10},{9,11},{10,... | collective-permute-start | bytes 393224 | tf_op jit(solution)/shard_map/ppermute | solution.py:20
  38.1 8.3 %collective-permute-start.17 = (bf16[8,8192]{1,0:T(8,128)(2,1)S(1)}, bf16[8,8192]{1,0:T(8,128)(2,1)S(1)}, u32[]{:S(2)}, u32[]{:S(2)}) collective-permute-start(bf16[8,8192]{1,0:T(8,128)(2,1)S(1)} %get-tuple-element.38), channel_id=1, source_target_pairs={{0,6},{1,7},{2,4},{3,5},{4,2},{5,3},{6,0},{7,1},{8,14},{9,15},{10,... | collective-permute-start | bytes 393224 | tf_op jit(solution)/shard_map/ppermute | solution.py:20
  39.9 8.5 %collective-permute-start.19 = (bf16[8,8192]{1,0:T(8,128)(2,1)S(1)}, bf16[8,8192]{1,0:T(8,128)(2,1)S(1)}, u32[]{:S(2)}, u32[]{:S(2)}) collective-permute-start(bf16[8,8192]{1,0:T(8,128)(2,1)S(1)} %get-tuple-element.40), channel_id=1, source_target_pairs={{0,1},{1,0},{2,3},{3,2},{4,5},{5,4},{6,7},{7,6},{8,9},{9,8},{10,11... | collective-permute-start | bytes 393224 | tf_op jit(solution)/shard_map/ppermute | solution.py:20
  42.6 9.4 %collective-permute-start.16 = (bf16[8,8192]{1,0:T(8,128)(2,1)S(1)}, bf16[8,8192]{1,0:T(8,128)(2,1)S(1)}, u32[]{:S(2)}, u32[]{:S(2)}) collective-permute-start(bf16[8,8192]{1,0:T(8,128)(2,1)S(1)} %add_convert_fusion.3), channel_id=1, source_target_pairs={{0,4},{1,5},{2,6},{3,7},{4,0},{5,1},{6,2},{7,3},{8,12},{9,13},{10,... | collective-permute-start | bytes 393224 | tf_op jit(solution)/shard_map/ppermute | solution.py:20
  46.4 5.6 %collective-permute-start.18 = (bf16[8,8192]{1,0:T(8,128)(2,1)S(1)}, bf16[8,8192]{1,0:T(8,128)(2,1)S(1)}, u32[]{:S(2)}, u32[]{:S(2)}) collective-permute-start(bf16[8,8192]{1,0:T(8,128)(2,1)S(1)} %add_convert_fusion.2), channel_id=1, source_target_pairs={{0,1},{1,0},{2,3},{3,2},{4,5},{5,4},{6,7},{7,6},{8,9},{9,8},{10,11... | collective-permute-start | bytes 393224 | tf_op jit(solution)/shard_map/ppermute | solution.py:20
  48.4 5.4 %collective-permute-start.20 = (bf16[8,8192]{1,0:T(8,128)(2,1)S(1)}, bf16[8,8192]{1,0:T(8,128)(2,1)S(1)}, u32[]{:S(2)}, u32[]{:S(2)}) collective-permute-start(bf16[8,8192]{1,0:T(8,128)(2,1)S(1)} %add_convert_fusion.1), channel_id=1, source_target_pairs={{0,2},{1,3},{2,0},{3,1},{4,6},{5,7},{6,4},{7,5},{8,10},{9,11},{10,... | collective-permute-start | bytes 393224 | tf_op jit(solution)/shard_map/ppermute | solution.py:20

commit v5 on v4

--- a/solution.py
+++ b/solution.py
@@ -111,8 +111,30 @@
         first += step
 
 
+def sums_kernel(own2, far2, own3, own1, far1, sum2, sum1):
+    sum2[...] = (own2[...] + far2[...].astype(F32) + own3[...].astype(F32)).astype(BF)
+    sum1[...] = (own1[...] + far1[...].astype(F32)).astype(BF)
+
+
 def hbm(x):
     return pltpu.with_memory_space_constraint(x, pltpu.HBM)
+
+
+def join_kernel(*refs):
+    pieces, out = refs[:-2], refs[-1]
+    out[...] = jnp.concatenate([p[...] for p in pieces], axis=0)
+
+
+def join_after(pieces, mark):
+    rows = sum(p.shape[0] for p in pieces)
+    return pl.pallas_call(
+        join_kernel,
+        out_shape=pltpu.VMEM((rows, pieces[0].shape[1]), BF),
+        in_specs=vmem_specs(len(pieces)) + [pl.BlockSpec(memory_space=pl.ANY)],
+        out_specs=vmem_specs(1)[0],
+        compiler_params=pltpu.CompilerParams(vmem_limit_bytes=2 * 2**20),
+        name="join",
+    )(*pieces, mark)
 
 
 def tie(x, mark):
@@ -139,7 +161,7 @@
     mine = [tokens, at1, at2, at4]
     last = [at7, at3, at6, at5]
     far_mine = [flip(p, "dp", 2, 1) for p in mine]
-    far_last = flip(jnp.concatenate([tie(p, later[2]) for p in last], axis=0), "dp", 2, 1)
+    far_last = flip(join_after(last, later[2]), "dp", 2, 1)
     held = [early, later]
     pieces = mine + last + far_mine + [far_last]
     late = ((width - sum(sizes)) // CHUNK, CHUNK, units)
@@ -181,10 +203,16 @@
     def send(x, mask):
         return flip(x.astype(BF), "tensor", 8, mask).astype(F32)
 
-    sum2 = own2 + send(far2, 1) + send(own3, 2)
+    sum2, sum1 = pl.pallas_call(
+        sums_kernel,
+        out_shape=[pltpu.VMEM((rows, width), BF)] * 2,
+        in_specs=vmem_specs(5),
+        out_specs=vmem_specs(2),
+        compiler_params=pltpu.CompilerParams(vmem_limit_bytes=4 * 2**20),
+        name="sums",
+    )(own2, hop(far2, 1), hop(own3, 2), own1, hop(far1, 1))
     sum0 = far0 + send(far3, 6)
-    sum1 = own1 + send(far1, 1)
-    total = own0 + send(sum2, 4) + send(sum0, 1) + send(sum1, 2)
+    total = own0 + send(sum2, 4) + send(sum1, 2) + send(sum0, 1)
     return (tokens.astype(F32) + total).astype(BF)
 
 

time: 54.6 us -> 54.2 us (level)
  starting transfers between devices: 24.5 us -> 22.5 us
  waiting for transfers between devices: 11.5 us -> 13.1 us
    ppermute x21, starting transfers between devices: 24.5 us -> 22.5 us  [flip(): return lax.ppermute(x, axis, [(i, i ^ mask) for i in range(size)])]
    ppermute x21, waiting for transfers between devices: 11.5 us -> 13.1 us  [flip(): return lax.ppermute(x, axis, [(i, i ^ mask) for i in range(size)])]
  transfers between devices with their start and end apart: 21 -> 21, of which waited for: 12 -> 10; matrix products, arithmetic and copies ran while one was open for 0% -> 0% of each run, Pallas kernels for 17% -> 17%
where the time goes in v5:
time: 54.2 us; the launch traced here: 54 us
  starting transfers between devices  22.5 us (42%)
  Pallas kernels  17.1 us (32%)
  waiting for transfers between devices  13.1 us (24%)
  other arithmetic  0.79 us (1%)
    ppermute x21, starting transfers between devices, flip(): return lax.ppermute(x, axis, [(i, i ^ mask) for i in range(size)])  22.5 us
    ppermute x21, waiting for transfers between devices, flip(): return lax.ppermute(x, axis, [(i, i ^ mask) for i in range(size)])  13.1 us
    pallas_call x2, Pallas kernels, fetch(): pl.pallas_call(functools.partial(fetch_kernel, first, len(after)), out_sh...  8.42 us
    pallas_call x1, Pallas kernels, per_device(): pl.pallas_call(functools.partial(hidden_kernel, len(held)), out_shape=jax...  5.83 us
    pallas_call x2, Pallas kernels, per_device(): pl.pallas_call(down_kernel, out_shape=(jax.ShapeDtypeStruct((8 * rows, st...  2.53 us
  transfers between devices with their start and end apart: 21, of which 10 were waited for; matrix products, arithmetic and copies ran while one was open for 0% of the time, Pallas kernels for 17%

profile of v5, /device:TPU:0, one launch (start us, length us, event | category | flops | bytes accessed | tf_op | source)
XLA Modules:
  0.0 54.0 jit_solution(14361803440948773698)
XLA Ops:
  0.0 4.0 %collective-permute-start.2 = (bf16[8,8192]{1,0:T(8,128)(2,1)}, bf16[8,8192]{1,0:T(8,128)(2,1)S(1)}, u32[]{:S(2)}, u32[]{:S(2)}) collective-permute-start(bf16[8,8192]{1,0:T(8,128)(2,1)} %refs_0_.5), channel_id=1, source_target_pairs={{0,4},{1,5},{2,6},{3,7},{4,0},{5,1},{6,2},{7,3},{8,12},{9,13},{10,... | collective-permute-start | bytes 393224 | tf_op jit(solution)/shard_map/ppermute | solution.py:20
  4.0 1.5 %collective-permute-start = (bf16[8,8192]{1,0:T(8,128)(2,1)}, bf16[8,8192]{1,0:T(8,128)(2,1)S(1)}, u32[]{:S(2)}, u32[]{:S(2)}) collective-permute-start(bf16[8,8192]{1,0:T(8,128)(2,1)} %refs_0_.5), channel_id=1, source_target_pairs={{0,1},{1,0},{2,3},{3,2},{4,5},{5,4},{6,7},{7,6},{8,9},{9,8},{10,11... | collective-permute-start | bytes 393224 | tf_op jit(solution)/shard_map/ppermute | solution.py:20
  5.6 1.6 %collective-permute-start.1 = (bf16[8,8192]{1,0:T(8,128)(2,1)}, bf16[8,8192]{1,0:T(8,128)(2,1)S(1)}, u32[]{:S(2)}, u32[]{:S(2)}) collective-permute-start(bf16[8,8192]{1,0:T(8,128)(2,1)} %refs_0_.5), channel_id=1, source_target_pairs={{0,2},{1,3},{2,0},{3,1},{4,6},{5,7},{6,4},{7,5},{8,10},{9,11},{10,... | collective-permute-start | bytes 393224 | tf_op jit(solution)/shard_map/ppermute | solution.py:20
  7.1 3.2 %fetch_0.1 = (bf16[2048,896]{1,0:T(8,128)(2,1)S(1)}, bf16[2048,896]{1,0:T(8,128)(2,1)S(1)}, bf16[8,8192]{1,0:T(8,128)(2,1)S(1)}) custom-call(bf16[8192,896]{1,0:T(8,128)(2,1)} %refs_18_.1, bf16[8192,896]{1,0:T(8,128)(2,1)} %refs_19_.1), custom_call_target="tpu_custom_call" | custom-call | bytes 7340032 | tf_op jit(solution)/shard_map/fetch_0/pallas_call | solution.py:53
  10.3 0.3 collective-permute-done.2.refs_2_.refs_3_
  10.7 0.0 collective-permute-done.refs_1_
  10.7 1.4 %collective-permute-done.1.refs_2_ = bf16[8,8192]{1,0:T(8,128)(2,1)S(1)} collective-permute-done((bf16[8,8192]{1,0:T(8,128)(2,1)}, bf16[8,8192]{1,0:T(8,128)(2,1)S(1)}, u32[]{:S(2)}, u32[]{:S(2)}) %collective-permute-start.1) | collective-permute-done | bytes 131104 | tf_op jit(solution)/shard_map/ppermute | solution.py:20
  12.1 0.3 collective-permute-start.5
  12.4 1.5 %collective-permute-start.6 = (bf16[8,8192]{1,0:T(8,128)(2,1)S(1)}, bf16[8,8192]{1,0:T(8,128)(2,1)S(1)}, u32[]{:S(2)}, u32[]{:S(2)}) collective-permute-start(bf16[8,8192]{1,0:T(8,128)(2,1)S(1)} %get-tuple-element.45), channel_id=1, source_target_pairs={{0,1},{1,0},{2,3},{3,2},{4,5},{5,4},{6,7},{7,6},{8,9},{9,8},{10,11... | collective-permute-start | bytes 393224 | tf_op jit(solution)/shard_map/ppermute | solution.py:20
  13.9 1.9 %collective-permute-start.3 = (bf16[8,8192]{1,0:T(8,128)(2,1)S(1)}, bf16[8,8192]{1,0:T(8,128)(2,1)S(1)}, u32[]{:S(2)}, u32[]{:S(2)}) collective-permute-start(bf16[8,8192]{1,0:T(8,128)(2,1)S(1)} %get-tuple-element.47), channel_id=1, source_target_pairs={{0,6},{1,7},{2,4},{3,5},{4,2},{5,3},{6,0},{7,1},{8,14},{9,15},{10,... | collective-permute-start | bytes 393224 | tf_op jit(solution)/shard_map/ppermute | solution.py:20
  15.8 0.0 copy-start
  15.8 0.0 copy-start.1
  15.8 1.2 %collective-permute-start.4 = (bf16[8,8192]{1,0:T(8,128)(2,1)S(1)}, bf16[8,8192]{1,0:T(8,128)(2,1)S(1)}, u32[]{:S(2)}, u32[]{:S(2)}) collective-permute-start(bf16[8,8192]{1,0:T(8,128)(2,1)S(1)} %get-tuple-element.46), channel_id=1, source_target_pairs={{0,1},{1,0},{2,3},{3,2},{4,5},{5,4},{6,7},{7,6},{8,9},{9,8},{10,11... | collective-permute-start | bytes 393224 | tf_op jit(solution)/shard_map/ppermute | solution.py:20
  17.0 5.2 %fetch_2048.1 = (bf16[4096,896]{1,0:T(8,128)(2,1)S(1)}, bf16[4096,896]{1,0:T(8,128)(2,1)S(1)}, bf16[8,8192]{1,0:T(8,128)(2,1)S(1)}) custom-call(bf16[8192,896]{1,0:T(8,128)(2,1)} %refs_18_.1, bf16[8192,896]{1,0:T(8,128)(2,1)} %refs_19_.1, bf16[8,8192]{1,0:T(8,128)(2,1)S(1)} %collective-permute-done.2.refs_2_.refs_3_), custom_call_target="tpu_custom_call" | custom-call | bytes 14680064 | tf_op jit(solution)/shard_map/fetch_2048/pallas_call | solution.py:53
  22.3 0.0 collective-permute-done.5.refs_2_.refs_6_
  22.3 0.0 collective-permute-done.6.refs_3_.refs_7_
  22.3 0.0 collective-permute-done.3.refs_0_.refs_4_
  22.3 0.0 collective-permute-done.4.refs_1_.refs_5_
  22.3 0.0 slice-start
  22.3 0.1 join.1
  22.4 0.1 collective-permute-start.11
  22.5 0.0 copy-done
  22.5 0.5 collective-permute-start.7
  23.0 0.1 collective-permute-start.10
  23.1 0.4 collective-permute-start.8
  23.5 0.1 collective-permute-start.9
  23.6 1.0 %collective-permute-done.7.refs_8_ = bf16[8,8192]{1,0:T(8,128)(2,1)S(1)} collective-permute-done((bf16[8,8192]{1,0:T(8,128)(2,1)S(1)}, bf16[8,8192]{1,0:T(8,128)(2,1)S(1)}, u32[]{:S(2)}, u32[]{:S(2)}) %collective-permute-start.7) | collective-permute-done | bytes 131104 | tf_op jit(solution)/shard_map/ppermute | solution.py:20
  24.6 0.2 collective-permute-done.10.refs_11_
  24.8 0.2 collective-permute-done.8.refs_9_
  24.9 0.2 collective-permute-done.9.refs_10_
  25.1 0.0 collective-permute-done.11.refs_12_
  25.1 0.0 copy-done.1
  25.1 0.0 slice-start.1
  25.1 0.0 slice-start.2
  25.2 0.0 slice-start.3
  25.2 5.8 %hidden.1 = bf16[128,896]{1,0:T(8,128)(2,1)S(1)} custom-call(bf16[8,8192]{1,0:T(8,128)(2,1)S(1)} %copy-done, bf16[8,8192]{1,0:T(8,128)(2,1)S(1)} %collective-permute-done.refs_1_, bf16[8,8192]{1,0:T(8,128)(2,1)S(1)} %collective-permute-done.1.refs_2_, bf16[8,8192]{1,0:T(8,128)(2,1)S(1)} %collective-permute-done.2.refs_2_.refs_3_, ...), custom_call_target="tpu_custom_call" | custom-call | tf_op jit(solution)/shard_map/hidden/pallas_call | solution.py:168
  31.0 0.0 slice-done
  31.0 0.0 slice-done.1
  31.0 0.0 slice-done.2
  31.0 0.4 slice-done.3
  31.4 1.8 %down.4 = (f32[64,6144]{1,0:T(8,128)S(1)}, bf16[64,6144]{1,0:T(8,128)(2,1)S(1)}) custom-call(bf16[128,896]{1,0:T(8,128)(2,1)S(1)} %hidden.1, bf16[896,8192]{1,0:T(8,128)(2,1)S(1)} %bitcast.2), custom_call_target="tpu_custom_call" | custom-call | tf_op jit(solution)/shard_map/down/pallas_call | solution.py:181
  33.2 0.2 collective-permute-start.12
  33.4 0.7 %down.6 = (f32[64,2048]{1,0:T(8,128)S(1)}, bf16[64,2048]{1,0:T(8,128)(2,1)S(1)}) custom-call(bf16[128,896]{1,0:T(8,128)(2,1)S(1)} %hidden.1, bf16[896,8192]{1,0:T(8,128)(2,1)S(1)} %bitcast.2), custom_call_target="tpu_custom_call" | custom-call | tf_op jit(solution)/shard_map/down/pallas_call | solution.py:181
  34.2 0.4 collective-permute-start.13
  34.6 1.4 %collective-permute-done.13.refs_3_ = bf16[64,2048]{1,0:T(8,128)(2,1)S(1)} collective-permute-done((bf16[64,2048]{1,0:T(8,128)(2,1)S(1)}, bf16[64,2048]{1,0:T(8,128)(2,1)S(1)}, u32[]{:S(2)}, u32[]{:S(2)}) %collective-permute-start.13) | collective-permute-done | bytes 262176 | tf_op jit(solution)/shard_map/ppermute | solution.py:20
  36.0 0.0 collective-permute-done.12.refs_2_
  36.0 0.2 pair.1
  36.1 0.9 %collective-permute-start.14 = (bf16[8,8192]{1,0:T(8,128)(2,1)S(1)}, bf16[8,8192]{1,0:T(8,128)(2,1)S(1)}, u32[]{:S(2)}, u32[]{:S(2)}) collective-permute-start(bf16[8,8192]{1,0:T(8,128)(2,1)S(1)} %get-tuple-element.37), channel_id=1, source_target_pairs={{0,1},{1,0},{2,3},{3,2},{4,5},{5,4},{6,7},{7,6},{8,9},{9,8},{10,11... | collective-permute-start | bytes 393224 | tf_op jit(solution)/shard_map/ppermute | solution.py:20
  37.0 1.1 %collective-permute-start.15 = (bf16[8,8192]{1,0:T(8,128)(2,1)S(1)}, bf16[8,8192]{1,0:T(8,128)(2,1)S(1)}, u32[]{:S(2)}, u32[]{:S(2)}) collective-permute-start(bf16[8,8192]{1,0:T(8,128)(2,1)S(1)} %get-tuple-element.38), channel_id=1, source_target_pairs={{0,2},{1,3},{2,0},{3,1},{4,6},{5,7},{6,4},{7,5},{8,10},{9,11},{10,... | collective-permute-start | bytes 393224 | tf_op jit(solution)/shard_map/ppermute | solution.py:20
  38.1 1.2 %collective-permute-start.16 = (bf16[8,8192]{1,0:T(8,128)(2,1)S(1)}, bf16[8,8192]{1,0:T(8,128)(2,1)S(1)}, u32[]{:S(2)}, u32[]{:S(2)}) collective-permute-start(bf16[8,8192]{1,0:T(8,128)(2,1)S(1)} %get-tuple-element.40), channel_id=1, source_target_pairs={{0,1},{1,0},{2,3},{3,2},{4,5},{5,4},{6,7},{7,6},{8,9},{9,8},{10,11... | collective-permute-start | bytes 393224 | tf_op jit(solution)/shard_map/ppermute | solution.py:20
  39.3 2.1 %collective-permute-start.19 = (bf16[8,8192]{1,0:T(8,128)(2,1)S(1)}, bf16[8,8192]{1,0:T(8,128)(2,1)S(1)}, u32[]{:S(2)}, u32[]{:S(2)}) collective-permute-start(bf16[8,8192]{1,0:T(8,128)(2,1)S(1)} %get-tuple-element.44), channel_id=1, source_target_pairs={{0,6},{1,7},{2,4},{3,5},{4,2},{5,3},{6,0},{7,1},{8,14},{9,15},{10,... | collective-permute-start | bytes 393224 | tf_op jit(solution)/shard_map/ppermute | solution.py:20
  41.3 1.2 %collective-permute-done.14.far2 = bf16[8,8192]{1,0:T(8,128)(2,1)S(1)} collective-permute-done((bf16[8,8192]{1,0:T(8,128)(2,1)S(1)}, bf16[8,8192]{1,0:T(8,128)(2,1)S(1)}, u32[]{:S(2)}, u32[]{:S(2)}) %collective-permute-start.14) | collective-permute-done | bytes 131104 | tf_op jit(solution)/shard_map/ppermute | solution.py:20
  42.5 0.0 collective-permute-done.15.own3
  42.5 2.0 %collective-permute-done.16.far1 = bf16[8,8192]{1,0:T(8,128)(2,1)S(1)} collective-permute-done((bf16[8,8192]{1,0:T(8,128)(2,1)S(1)}, bf16[8,8192]{1,0:T(8,128)(2,1)S(1)}, u32[]{:S(2)}, u32[]{:S(2)}) %collective-permute-start.16) | collective-permute-done | bytes 131104 | tf_op jit(solution)/shard_map/ppermute | solution.py:20
  44.6 0.1 sums.1
  44.6 1.7 %collective-permute-start.17 = (bf16[8,8192]{1,0:T(8,128)(2,1)S(1)}, bf16[8,8192]{1,0:T(8,128)(2,1)S(1)}, u32[]{:S(2)}, u32[]{:S(2)}) collective-permute-start(bf16[8,8192]{1,0:T(8,128)(2,1)S(1)} %get-tuple-element.41), channel_id=1, source_target_pairs={{0,4},{1,5},{2,6},{3,7},{4,0},{5,1},{6,2},{7,3},{8,12},{9,13},{10,... | collective-permute-start | bytes 393224 | tf_op jit(solution)/shard_map/ppermute | solution.py:20
  46.4 0.2 collective-permute-start.18
  46.6 0.0 collective-permute-done.19
  46.6 1.5 %collective-permute-start.20 = (bf16[8,8192]{1,0:T(8,128)(2,1)S(1)}, bf16[8,8192]{1,0:T(8,128)(2,1)S(1)}, u32[]{:S(2)}, u32[]{:S(2)}) collective-permute-start(bf16[8,8192]{1,0:T(8,128)(2,1)S(1)} %add_convert_fusion.1), channel_id=1, source_target_pairs={{0,1},{1,0},{2,3},{3,2},{4,5},{5,4},{6,7},{7,6},{8,9},{9,8},{10,11... | collective-permute-start | bytes 393224 | tf_op jit(solution)/shard_map/ppermute | solution.py:20
  48.1 5.1 %collective-permute-done.17 = bf16[8,8192]{1,0:T(8,128)(2,1)S(1)} collective-permute-done((bf16[8,8192]{1,0:T(8,128)(2,1)S(1)}, bf16[8,8192]{1,0:T(8,128)(2,1)S(1)}, u32[]{:S(2)}, u32[]{:S(2)}) %collective-permute-start.17) | collective-permute-done | bytes 131104 | tf_op jit(solution)/shard_map/ppermute | solution.py:20
  53.3 0.0 collective-permute-done.18
  53.3 0.0 collective-permute-done.20
  53.3 0.7 %add_convert_fusion = bf16[8,8192]{1,0:T(8,128)(2,1)} fusion(bf16[8,8192]{1,0:T(8,128)(2,1)S(1)} %collective-permute-done.20, bf16[8,8192]{1,0:T(8,128)(2,1)S(1)} %collective-permute-done.18, f32[8,8192]{1,0:T(8,128)S(1)} %get-tuple-element.35, bf16[8,8192]{1,0:T(8,128)(2,1)S(1)} %collective-permute-done.17, bf16[8,8192]{1,0:T(8,128)(2,1)S(1)} %copy-done), kind=kLoop, calls=%fused_computation | loop fusion | flops 589824 | bytes 917504 | tf_op jit(solution)/shard_map/convert_element_type | solution.py:216
  (3 shorter events, 0.1 us)
Async XLA Ops:
  0.0 10.7 %collective-permute-start.2 = (bf16[8,8192]{1,0:T(8,128)(2,1)}, bf16[8,8192]{1,0:T(8,128)(2,1)S(1)}, u32[]{:S(2)}, u32[]{:S(2)}) collective-permute-start(bf16[8,8192]{1,0:T(8,128)(2,1)} %refs_0_.5), channel_id=1, source_target_pairs={{0,4},{1,5},{2,6},{3,7},{4,0},{5,1},{6,2},{7,3},{8,12},{9,13},{10,... | collective-permute-start | bytes 393224 | tf_op jit(solution)/shard_map/ppermute | solution.py:20
  4.0 6.6 %collective-permute-start = (bf16[8,8192]{1,0:T(8,128)(2,1)}, bf16[8,8192]{1,0:T(8,128)(2,1)S(1)}, u32[]{:S(2)}, u32[]{:S(2)}) collective-permute-start(bf16[8,8192]{1,0:T(8,128)(2,1)} %refs_0_.5), channel_id=1, source_target_pairs={{0,1},{1,0},{2,3},{3,2},{4,5},{5,4},{6,7},{7,6},{8,9},{9,8},{10,11... | collective-permute-start | bytes 393224 | tf_op jit(solution)/shard_map/ppermute | solution.py:20
  5.6 6.5 %collective-permute-start.1 = (bf16[8,8192]{1,0:T(8,128)(2,1)}, bf16[8,8192]{1,0:T(8,128)(2,1)S(1)}, u32[]{:S(2)}, u32[]{:S(2)}) collective-permute-start(bf16[8,8192]{1,0:T(8,128)(2,1)} %refs_0_.5), channel_id=1, source_target_pairs={{0,2},{1,3},{2,0},{3,1},{4,6},{5,7},{6,4},{7,5},{8,10},{9,11},{10,... | collective-permute-start | bytes 393224 | tf_op jit(solution)/shard_map/ppermute | solution.py:20
  12.1 10.1 %collective-permute-start.5 = (bf16[8,8192]{1,0:T(8,128)(2,1)S(1)}, bf16[8,8192]{1,0:T(8,128)(2,1)S(1)}, u32[]{:S(2)}, u32[]{:S(2)}) collective-permute-start(bf16[8,8192]{1,0:T(8,128)(2,1)S(1)} %get-tuple-element.45), channel_id=1, source_target_pairs={{0,2},{1,3},{2,0},{3,1},{4,6},{5,7},{6,4},{7,5},{8,10},{9,11},{10,... | collective-permute-start | bytes 393224 | tf_op jit(solution)/shard_map/ppermute | solution.py:20
  12.4 9.8 %collective-permute-start.6 = (bf16[8,8192]{1,0:T(8,128)(2,1)S(1)}, bf16[8,8192]{1,0:T(8,128)(2,1)S(1)}, u32[]{:S(2)}, u32[]{:S(2)}) collective-permute-start(bf16[8,8192]{1,0:T(8,128)(2,1)S(1)} %get-tuple-element.45), channel_id=1, source_target_pairs={{0,1},{1,0},{2,3},{3,2},{4,5},{5,4},{6,7},{7,6},{8,9},{9,8},{10,11... | collective-permute-start | bytes 393224 | tf_op jit(solution)/shard_map/ppermute | solution.py:20
  13.9 8.4 %collective-permute-start.3 = (bf16[8,8192]{1,0:T(8,128)(2,1)S(1)}, bf16[8,8192]{1,0:T(8,128)(2,1)S(1)}, u32[]{:S(2)}, u32[]{:S(2)}) collective-permute-start(bf16[8,8192]{1,0:T(8,128)(2,1)S(1)} %get-tuple-element.47), channel_id=1, source_target_pairs={{0,6},{1,7},{2,4},{3,5},{4,2},{5,3},{6,0},{7,1},{8,14},{9,15},{10,... | collective-permute-start | bytes 393224 | tf_op jit(solution)/shard_map/ppermute | solution.py:20
  15.8 6.7 %copy-start = (bf16[8,8192]{1,0:T(8,128)(2,1)S(1)}, bf16[8,8192]{1,0:T(8,128)(2,1)}, u32[]{:S(2)}) copy-start(bf16[8,8192]{1,0:T(8,128)(2,1)} %refs_0_.5) | copy-start | bytes 393220
  15.8 9.3 %copy-start.1 = (f32[8192]{0:T(1024)S(1)}, f32[8192]{0:T(1024)}, u32[]{:S(2)}) copy-start(f32[8192]{0:T(1024)} %param.6) | copy-start | bytes 98308
  15.8 6.5 %collective-permute-start.4 = (bf16[8,8192]{1,0:T(8,128)(2,1)S(1)}, bf16[8,8192]{1,0:T(8,128)(2,1)S(1)}, u32[]{:S(2)}, u32[]{:S(2)}) collective-permute-start(bf16[8,8192]{1,0:T(8,128)(2,1)S(1)} %get-tuple-element.46), channel_id=1, source_target_pairs={{0,1},{1,0},{2,3},{3,2},{4,5},{5,4},{6,7},{7,6},{8,9},{9,8},{10,11... | collective-permute-start | bytes 393224 | tf_op jit(solution)/shard_map/ppermute | solution.py:20
  22.3 8.7 %slice-start = ((s8[14680064]{0:T(1024)(128)(4,1)}), s8[4194304]{0:T(1024)(128)(4,1)S(1)}, s32[]{:S(2)}) async-start(s8[14680064]{0:T(1024)(128)(4,1)} %bitcast.1), calls=%async_computation | async-start | bytes 8388608
  22.4 2.7 %collective-permute-start.11 = (bf16[32,8192]{1,0:T(8,128)(2,1)S(1)}, bf16[32,8192]{1,0:T(8,128)(2,1)S(1)}, u32[]{:S(2)}, u32[]{:S(2)}) collective-permute-start(bf16[32,8192]{1,0:T(8,128)(2,1)S(1)} %join.1), channel_id=1, source_target_pairs={{0,8},{8,0},{1,9},{9,1},{2,10},{10,2},{3,11},{11,3},{4,12},{12,4},... | collective-permute-start | bytes 1572872 | tf_op jit(solution)/shard_map/ppermute | solution.py:20
  22.5 2.1 %collective-permute-start.7 = (bf16[8,8192]{1,0:T(8,128)(2,1)S(1)}, bf16[8,8192]{1,0:T(8,128)(2,1)S(1)}, u32[]{:S(2)}, u32[]{:S(2)}) collective-permute-start(bf16[8,8192]{1,0:T(8,128)(2,1)S(1)} %copy-done), channel_id=1, source_target_pairs={{0,8},{8,0},{1,9},{9,1},{2,10},{10,2},{3,11},{11,3},{4,12},{12,4},... | collective-permute-start | bytes 393224 | tf_op jit(solution)/shard_map/ppermute | solution.py:20
  23.0 1.8 %collective-permute-start.10 = (bf16[8,8192]{1,0:T(8,128)(2,1)S(1)}, bf16[8,8192]{1,0:T(8,128)(2,1)S(1)}, u32[]{:S(2)}, u32[]{:S(2)}) collective-permute-start(bf16[8,8192]{1,0:T(8,128)(2,1)S(1)} %collective-permute-done.2.refs_2_.refs_3_), channel_id=1, source_target_pairs={{0,8},{8,0},{1,9},{9,1},{2,10},{10,2},{3,11},{11,3},{4,12},{12,4},... | collective-permute-start | bytes 393224 | tf_op jit(solution)/shard_map/ppermute | solution.py:20
  23.1 1.9 %collective-permute-start.8 = (bf16[8,8192]{1,0:T(8,128)(2,1)S(1)}, bf16[8,8192]{1,0:T(8,128)(2,1)S(1)}, u32[]{:S(2)}, u32[]{:S(2)}) collective-permute-start(bf16[8,8192]{1,0:T(8,128)(2,1)S(1)} %collective-permute-done.refs_1_), channel_id=1, source_target_pairs={{0,8},{8,0},{1,9},{9,1},{2,10},{10,2},{3,11},{11,3},{4,12},{12,4},... | collective-permute-start | bytes 393224 | tf_op jit(solution)/shard_map/ppermute | solution.py:20
  23.5 1.6 %collective-permute-start.9 = (bf16[8,8192]{1,0:T(8,128)(2,1)S(1)}, bf16[8,8192]{1,0:T(8,128)(2,1)S(1)}, u32[]{:S(2)}, u32[]{:S(2)}) collective-permute-start(bf16[8,8192]{1,0:T(8,128)(2,1)S(1)} %collective-permute-done.1.refs_2_), channel_id=1, source_target_pairs={{0,8},{8,0},{1,9},{9,1},{2,10},{10,2},{3,11},{11,3},{4,12},{12,4},... | collective-permute-start | bytes 393224 | tf_op jit(solution)/shard_map/ppermute | solution.py:20
  25.1 5.9 %slice-start.1 = ((s8[14680064]{0:T(1024)(128)(4,1)}), s8[4194304]{0:T(1024)(128)(4,1)S(1)}, s32[]{:S(2)}) async-start(s8[14680064]{0:T(1024)(128)(4,1)} %bitcast.1), calls=%async_computation.1 | async-start | bytes 8388608
  25.1 5.9 %slice-start.2 = ((s8[14680064]{0:T(1024)(128)(4,1)}), s8[4194304]{0:T(1024)(128)(4,1)S(1)}, s32[]{:S(2)}) async-start(s8[14680064]{0:T(1024)(128)(4,1)} %bitcast.1), calls=%async_computation.2 | async-start | bytes 8388608
  25.2 6.3 %slice-start.3 = ((s8[14680064]{0:T(1024)(128)(4,1)}), s8[2097152]{0:T(1024)(128)(4,1)S(1)}, s32[]{:S(2)}) async-start(s8[14680064]{0:T(1024)(128)(4,1)} %bitcast.1), calls=%async_computation.3 | async-start | bytes 4194304
  33.2 2.7 %collective-permute-start.12 = (bf16[64,6144]{1,0:T(8,128)(2,1)S(1)}, bf16[64,6144]{1,0:T(8,128)(2,1)S(1)}, u32[]{:S(2)}, u32[]{:S(2)}) collective-permute-start(bf16[64,6144]{1,0:T(8,128)(2,1)S(1)} %get-tuple-element.33), channel_id=1, source_target_pairs={{0,8},{8,0},{1,9},{9,1},{2,10},{10,2},{3,11},{11,3},{4,12},{12,4},... | collective-permute-start | bytes 2359304 | tf_op jit(solution)/shard_map/ppermute | solution.py:20
  34.2 1.8 %collective-permute-start.13 = (bf16[64,2048]{1,0:T(8,128)(2,1)S(1)}, bf16[64,2048]{1,0:T(8,128)(2,1)S(1)}, u32[]{:S(2)}, u32[]{:S(2)}) collective-permute-start(bf16[64,2048]{1,0:T(8,128)(2,1)S(1)} %get-tuple-element.34), channel_id=1, source_target_pairs={{0,8},{8,0},{1,9},{9,1},{2,10},{10,2},{3,11},{11,3},{4,12},{12,4},... | collective-permute-start | bytes 786440 | tf_op jit(solution)/shard_map/ppermute | solution.py:20
  36.1 6.4 %collective-permute-start.14 = (bf16[8,8192]{1,0:T(8,128)(2,1)S(1)}, bf16[8,8192]{1,0:T(8,128)(2,1)S(1)}, u32[]{:S(2)}, u32[]{:S(2)}) collective-permute-start(bf16[8,8192]{1,0:T(8,128)(2,1)S(1)} %get-tuple-element.37), channel_id=1, source_target_pairs={{0,1},{1,0},{2,3},{3,2},{4,5},{5,4},{6,7},{7,6},{8,9},{9,8},{10,11... | collective-permute-start | bytes 393224 | tf_op jit(solution)/shard_map/ppermute | solution.py:20
  37.0 5.5 %collective-permute-start.15 = (bf16[8,8192]{1,0:T(8,128)(2,1)S(1)}, bf16[8,8192]{1,0:T(8,128)(2,1)S(1)}, u32[]{:S(2)}, u32[]{:S(2)}) collective-permute-start(bf16[8,8192]{1,0:T(8,128)(2,1)S(1)} %get-tuple-element.38), channel_id=1, source_target_pairs={{0,2},{1,3},{2,0},{3,1},{4,6},{5,7},{6,4},{7,5},{8,10},{9,11},{10,... | collective-permute-start | bytes 393224 | tf_op jit(solution)/shard_map/ppermute | solution.py:20
  38.1 6.5 %collective-permute-start.16 = (bf16[8,8192]{1,0:T(8,128)(2,1)S(1)}, bf16[8,8192]{1,0:T(8,128)(2,1)S(1)}, u32[]{:S(2)}, u32[]{:S(2)}) collective-permute-start(bf16[8,8192]{1,0:T(8,128)(2,1)S(1)} %get-tuple-element.40), channel_id=1, source_target_pairs={{0,1},{1,0},{2,3},{3,2},{4,5},{5,4},{6,7},{7,6},{8,9},{9,8},{10,11... | collective-permute-start | bytes 393224 | tf_op jit(solution)/shard_map/ppermute | solution.py:20
  39.3 7.3 %collective-permute-start.19 = (bf16[8,8192]{1,0:T(8,128)(2,1)S(1)}, bf16[8,8192]{1,0:T(8,128)(2,1)S(1)}, u32[]{:S(2)}, u32[]{:S(2)}) collective-permute-start(bf16[8,8192]{1,0:T(8,128)(2,1)S(1)} %get-tuple-element.44), channel_id=1, source_target_pairs={{0,6},{1,7},{2,4},{3,5},{4,2},{5,3},{6,0},{7,1},{8,14},{9,15},{10,... | collective-permute-start | bytes 393224 | tf_op jit(solution)/shard_map/ppermute | solution.py:20
  44.6 8.6 %collective-permute-start.17 = (bf16[8,8192]{1,0:T(8,128)(2,1)S(1)}, bf16[8,8192]{1,0:T(8,128)(2,1)S(1)}, u32[]{:S(2)}, u32[]{:S(2)}) collective-permute-start(bf16[8,8192]{1,0:T(8,128)(2,1)S(1)} %get-tuple-element.41), channel_id=1, source_target_pairs={{0,4},{1,5},{2,6},{3,7},{4,0},{5,1},{6,2},{7,3},{8,12},{9,13},{10,... | collective-permute-start | bytes 393224 | tf_op jit(solution)/shard_map/ppermute | solution.py:20
  46.4 6.9 %collective-permute-start.18 = (bf16[8,8192]{1,0:T(8,128)(2,1)S(1)}, bf16[8,8192]{1,0:T(8,128)(2,1)S(1)}, u32[]{:S(2)}, u32[]{:S(2)}) collective-permute-start(bf16[8,8192]{1,0:T(8,128)(2,1)S(1)} %get-tuple-element.42), channel_id=1, source_target_pairs={{0,2},{1,3},{2,0},{3,1},{4,6},{5,7},{6,4},{7,5},{8,10},{9,11},{10,... | collective-permute-start | bytes 393224 | tf_op jit(solution)/shard_map/ppermute | solution.py:20
  46.6 6.7 %collective-permute-start.20 = (bf16[8,8192]{1,0:T(8,128)(2,1)S(1)}, bf16[8,8192]{1,0:T(8,128)(2,1)S(1)}, u32[]{:S(2)}, u32[]{:S(2)}) collective-permute-start(bf16[8,8192]{1,0:T(8,128)(2,1)S(1)} %add_convert_fusion.1), channel_id=1, source_target_pairs={{0,1},{1,0},{2,3},{3,2},{4,5},{5,4},{6,7},{7,6},{8,9},{9,8},{10,11... | collective-permute-start | bytes 393224 | tf_op jit(solution)/shard_map/ppermute | solution.py:20

commit v6 on v5

--- a/solution.py
+++ b/solution.py
@@ -11,8 +11,8 @@
 F32 = jnp.float32
 SPLIT = (3, 1)
 COST = 4
-FETCHES = (2, 4)
-CHUNK = 1024
+FETCHES = (5, 8)
+CHUNK = 512
 ORDER = (0, 2, 3, 6, 1, 5, 7, 4)
 
 

time: 54.2 us -> 54.1 us (level)
  Pallas kernels: 17.1 us -> 17.9 us
  waiting for transfers between devices: 13.1 us -> 12.5 us
    ppermute x21, waiting for transfers between devices: 13.1 us -> 12.5 us  [flip(): return lax.ppermute(x, axis, [(i, i ^ mask) for i in range(size)])]
  transfers between devices with their start and end apart: 21 -> 21, of which waited for: 10 -> 10; matrix products, arithmetic and copies ran while one was open for 0% -> 0% of each run, Pallas kernels for 17% -> 18%
where the time goes in v6:
time: 54.1 us; the launch traced here: 53.9 us
  starting transfers between devices  22.5 us (42%)
  Pallas kernels  17.9 us (33%)
  waiting for transfers between devices  12.5 us (23%)
  other arithmetic  0.81 us (1%)
    ppermute x21, starting transfers between devices, flip(): return lax.ppermute(x, axis, [(i, i ^ mask) for i in range(size)])  22.5 us
    ppermute x21, waiting for transfers between devices, flip(): return lax.ppermute(x, axis, [(i, i ^ mask) for i in range(size)])  12.5 us
    pallas_call x2, Pallas kernels, fetch(): pl.pallas_call(functools.partial(fetch_kernel, first, len(after)), out_sh...  8.9 us
    pallas_call x1, Pallas kernels, per_device(): pl.pallas_call(functools.partial(hidden_kernel, len(held)), out_shape=jax...  6.15 us
    pallas_call x2, Pallas kernels, per_device(): pl.pallas_call(down_kernel, out_shape=(jax.ShapeDtypeStruct((8 * rows, st...  2.52 us
  transfers between devices with their start and end apart: 21, of which 10 were waited for; matrix products, arithmetic and copies ran while one was open for 0% of the time, Pallas kernels for 18%

profile of v6, /device:TPU:0, one launch (start us, length us, event | category | flops | bytes accessed | tf_op | source)
XLA Modules:
  0.0 53.9 jit_solution(5168089222133137422)
XLA Ops:
  0.0 4.0 %collective-permute-start.2 = (bf16[8,8192]{1,0:T(8,128)(2,1)}, bf16[8,8192]{1,0:T(8,128)(2,1)S(1)}, u32[]{:S(2)}, u32[]{:S(2)}) collective-permute-start(bf16[8,8192]{1,0:T(8,128)(2,1)} %refs_0_.5), channel_id=1, source_target_pairs={{0,4},{1,5},{2,6},{3,7},{4,0},{5,1},{6,2},{7,3},{8,12},{9,13},{10,... | collective-permute-start | bytes 393224 | tf_op jit(solution)/shard_map/ppermute | solution.py:20
  4.0 1.5 %collective-permute-start = (bf16[8,8192]{1,0:T(8,128)(2,1)}, bf16[8,8192]{1,0:T(8,128)(2,1)S(1)}, u32[]{:S(2)}, u32[]{:S(2)}) collective-permute-start(bf16[8,8192]{1,0:T(8,128)(2,1)} %refs_0_.5), channel_id=1, source_target_pairs={{0,1},{1,0},{2,3},{3,2},{4,5},{5,4},{6,7},{7,6},{8,9},{9,8},{10,11... | collective-permute-start | bytes 393224 | tf_op jit(solution)/shard_map/ppermute | solution.py:20
  5.6 1.6 %collective-permute-start.1 = (bf16[8,8192]{1,0:T(8,128)(2,1)}, bf16[8,8192]{1,0:T(8,128)(2,1)S(1)}, u32[]{:S(2)}, u32[]{:S(2)}) collective-permute-start(bf16[8,8192]{1,0:T(8,128)(2,1)} %refs_0_.5), channel_id=1, source_target_pairs={{0,2},{1,3},{2,0},{3,1},{4,6},{5,7},{6,4},{7,5},{8,10},{9,11},{10,... | collective-permute-start | bytes 393224 | tf_op jit(solution)/shard_map/ppermute | solution.py:20
  7.1 3.7 %fetch_0.1 = (bf16[2560,896]{1,0:T(8,128)(2,1)S(1)}, bf16[2560,896]{1,0:T(8,128)(2,1)S(1)}, bf16[8,8192]{1,0:T(8,128)(2,1)S(1)}) custom-call(bf16[8192,896]{1,0:T(8,128)(2,1)} %refs_18_.1, bf16[8192,896]{1,0:T(8,128)(2,1)} %refs_19_.1), custom_call_target="tpu_custom_call" | custom-call | bytes 9175040 | tf_op jit(solution)/shard_map/fetch_0/pallas_call | solution.py:53
  10.9 0.0 collective-permute-done.2.refs_2_.refs_3_
  10.9 0.0 collective-permute-done.refs_1_
  10.9 1.2 %collective-permute-done.1.refs_2_ = bf16[8,8192]{1,0:T(8,128)(2,1)S(1)} collective-permute-done((bf16[8,8192]{1,0:T(8,128)(2,1)}, bf16[8,8192]{1,0:T(8,128)(2,1)S(1)}, u32[]{:S(2)}, u32[]{:S(2)}) %collective-permute-start.1) | collective-permute-done | bytes 131104 | tf_op jit(solution)/shard_map/ppermute | solution.py:20
  12.1 0.3 collective-permute-start.5
  12.4 1.5 %collective-permute-start.6 = (bf16[8,8192]{1,0:T(8,128)(2,1)S(1)}, bf16[8,8192]{1,0:T(8,128)(2,1)S(1)}, u32[]{:S(2)}, u32[]{:S(2)}) collective-permute-start(bf16[8,8192]{1,0:T(8,128)(2,1)S(1)} %get-tuple-element.45), channel_id=1, source_target_pairs={{0,1},{1,0},{2,3},{3,2},{4,5},{5,4},{6,7},{7,6},{8,9},{9,8},{10,11... | collective-permute-start | bytes 393224 | tf_op jit(solution)/shard_map/ppermute | solution.py:20
  13.9 1.9 %collective-permute-start.3 = (bf16[8,8192]{1,0:T(8,128)(2,1)S(1)}, bf16[8,8192]{1,0:T(8,128)(2,1)S(1)}, u32[]{:S(2)}, u32[]{:S(2)}) collective-permute-start(bf16[8,8192]{1,0:T(8,128)(2,1)S(1)} %get-tuple-element.47), channel_id=1, source_target_pairs={{0,6},{1,7},{2,4},{3,5},{4,2},{5,3},{6,0},{7,1},{8,14},{9,15},{10,... | collective-permute-start | bytes 393224 | tf_op jit(solution)/shard_map/ppermute | solution.py:20
  15.8 0.0 copy-start
  15.8 0.0 copy-start.1
  15.8 1.2 %collective-permute-start.4 = (bf16[8,8192]{1,0:T(8,128)(2,1)S(1)}, bf16[8,8192]{1,0:T(8,128)(2,1)S(1)}, u32[]{:S(2)}, u32[]{:S(2)}) collective-permute-start(bf16[8,8192]{1,0:T(8,128)(2,1)S(1)} %get-tuple-element.46), channel_id=1, source_target_pairs={{0,1},{1,0},{2,3},{3,2},{4,5},{5,4},{6,7},{7,6},{8,9},{9,8},{10,11... | collective-permute-start | bytes 393224 | tf_op jit(solution)/shard_map/ppermute | solution.py:20
  17.0 5.2 %fetch_2560.1 = (bf16[4096,896]{1,0:T(8,128)(2,1)S(1)}, bf16[4096,896]{1,0:T(8,128)(2,1)S(1)}, bf16[8,8192]{1,0:T(8,128)(2,1)S(1)}) custom-call(bf16[8192,896]{1,0:T(8,128)(2,1)} %refs_18_.1, bf16[8192,896]{1,0:T(8,128)(2,1)} %refs_19_.1, bf16[8,8192]{1,0:T(8,128)(2,1)S(1)} %collective-permute-done.2.refs_2_.refs_3_), custom_call_target="tpu_custom_call" | custom-call | bytes 14680064 | tf_op jit(solution)/shard_map/fetch_2560/pallas_call | solution.py:53
  22.2 0.0 collective-permute-done.5.refs_2_.refs_6_
  22.2 0.0 collective-permute-done.6.refs_3_.refs_7_
  22.2 0.0 collective-permute-done.3.refs_0_.refs_4_
  22.2 0.0 collective-permute-done.4.refs_1_.refs_5_
  22.2 0.0 slice-start
  22.3 0.1 join.1
  22.3 0.1 collective-permute-start.11
  22.4 0.0 copy-done
  22.4 0.5 collective-permute-start.7
  22.9 0.1 collective-permute-start.10
  23.0 0.4 collective-permute-start.8
  23.4 0.1 collective-permute-start.9
  23.5 1.0 %collective-permute-done.7.refs_8_ = bf16[8,8192]{1,0:T(8,128)(2,1)S(1)} collective-permute-done((bf16[8,8192]{1,0:T(8,128)(2,1)S(1)}, bf16[8,8192]{1,0:T(8,128)(2,1)S(1)}, u32[]{:S(2)}, u32[]{:S(2)}) %collective-permute-start.7) | collective-permute-done | bytes 131104 | tf_op jit(solution)/shard_map/ppermute | solution.py:20
  24.5 0.2 collective-permute-done.10.refs_11_
  24.7 0.2 collective-permute-done.8.refs_9_
  24.9 0.2 collective-permute-done.9.refs_10_
  25.1 0.0 collective-permute-done.11.refs_12_
  25.1 0.0 copy-done.1
  25.1 0.0 slice-start.1
  25.1 0.0 slice-start.2
  25.1 0.0 slice-start.3
  25.1 6.2 %hidden.1 = bf16[128,896]{1,0:T(8,128)(2,1)S(1)} custom-call(bf16[8,8192]{1,0:T(8,128)(2,1)S(1)} %copy-done, bf16[8,8192]{1,0:T(8,128)(2,1)S(1)} %collective-permute-done.refs_1_, bf16[8,8192]{1,0:T(8,128)(2,1)S(1)} %collective-permute-done.1.refs_2_, bf16[8,8192]{1,0:T(8,128)(2,1)S(1)} %collective-permute-done.2.refs_2_.refs_3_, ...), custom_call_target="tpu_custom_call" | custom-call | tf_op jit(solution)/shard_map/hidden/pallas_call | solution.py:168
  31.3 0.0 slice-done
  31.3 0.0 slice-done.1
  31.3 0.0 slice-done.2
  31.3 0.0 slice-done.3
  31.3 1.8 %down.4 = (f32[64,6144]{1,0:T(8,128)S(1)}, bf16[64,6144]{1,0:T(8,128)(2,1)S(1)}) custom-call(bf16[128,896]{1,0:T(8,128)(2,1)S(1)} %hidden.1, bf16[896,8192]{1,0:T(8,128)(2,1)S(1)} %bitcast.2), custom_call_target="tpu_custom_call" | custom-call | tf_op jit(solution)/shard_map/down/pallas_call | solution.py:181
  33.1 0.2 collective-permute-start.12
  33.3 0.7 %down.6 = (f32[64,2048]{1,0:T(8,128)S(1)}, bf16[64,2048]{1,0:T(8,128)(2,1)S(1)}) custom-call(bf16[128,896]{1,0:T(8,128)(2,1)S(1)} %hidden.1, bf16[896,8192]{1,0:T(8,128)(2,1)S(1)} %bitcast.2), custom_call_target="tpu_custom_call" | custom-call | tf_op jit(solution)/shard_map/down/pallas_call | solution.py:181
  34.1 0.4 collective-permute-start.13
  34.5 1.4 %collective-permute-done.13.refs_3_ = bf16[64,2048]{1,0:T(8,128)(2,1)S(1)} collective-permute-done((bf16[64,2048]{1,0:T(8,128)(2,1)S(1)}, bf16[64,2048]{1,0:T(8,128)(2,1)S(1)}, u32[]{:S(2)}, u32[]{:S(2)}) %collective-permute-start.13) | collective-permute-done | bytes 262176 | tf_op jit(solution)/shard_map/ppermute | solution.py:20
  35.9 0.0 collective-permute-done.12.refs_2_
  35.9 0.2 pair.1
  36.0 0.9 %collective-permute-start.14 = (bf16[8,8192]{1,0:T(8,128)(2,1)S(1)}, bf16[8,8192]{1,0:T(8,128)(2,1)S(1)}, u32[]{:S(2)}, u32[]{:S(2)}) collective-permute-start(bf16[8,8192]{1,0:T(8,128)(2,1)S(1)} %get-tuple-element.37), channel_id=1, source_target_pairs={{0,1},{1,0},{2,3},{3,2},{4,5},{5,4},{6,7},{7,6},{8,9},{9,8},{10,11... | collective-permute-start | bytes 393224 | tf_op jit(solution)/shard_map/ppermute | solution.py:20
  36.9 1.0 %collective-permute-start.15 = (bf16[8,8192]{1,0:T(8,128)(2,1)S(1)}, bf16[8,8192]{1,0:T(8,128)(2,1)S(1)}, u32[]{:S(2)}, u32[]{:S(2)}) collective-permute-start(bf16[8,8192]{1,0:T(8,128)(2,1)S(1)} %get-tuple-element.38), channel_id=1, source_target_pairs={{0,2},{1,3},{2,0},{3,1},{4,6},{5,7},{6,4},{7,5},{8,10},{9,11},{10,... | collective-permute-start | bytes 393224 | tf_op jit(solution)/shard_map/ppermute | solution.py:20
  38.0 1.2 %collective-permute-start.16 = (bf16[8,8192]{1,0:T(8,128)(2,1)S(1)}, bf16[8,8192]{1,0:T(8,128)(2,1)S(1)}, u32[]{:S(2)}, u32[]{:S(2)}) collective-permute-start(bf16[8,8192]{1,0:T(8,128)(2,1)S(1)} %get-tuple-element.40), channel_id=1, source_target_pairs={{0,1},{1,0},{2,3},{3,2},{4,5},{5,4},{6,7},{7,6},{8,9},{9,8},{10,11... | collective-permute-start | bytes 393224 | tf_op jit(solution)/shard_map/ppermute | solution.py:20
  39.2 2.1 %collective-permute-start.19 = (bf16[8,8192]{1,0:T(8,128)(2,1)S(1)}, bf16[8,8192]{1,0:T(8,128)(2,1)S(1)}, u32[]{:S(2)}, u32[]{:S(2)}) collective-permute-start(bf16[8,8192]{1,0:T(8,128)(2,1)S(1)} %get-tuple-element.44), channel_id=1, source_target_pairs={{0,6},{1,7},{2,4},{3,5},{4,2},{5,3},{6,0},{7,1},{8,14},{9,15},{10,... | collective-permute-start | bytes 393224 | tf_op jit(solution)/shard_map/ppermute | solution.py:20
  41.3 1.1 %collective-permute-done.14.far2 = bf16[8,8192]{1,0:T(8,128)(2,1)S(1)} collective-permute-done((bf16[8,8192]{1,0:T(8,128)(2,1)S(1)}, bf16[8,8192]{1,0:T(8,128)(2,1)S(1)}, u32[]{:S(2)}, u32[]{:S(2)}) %collective-permute-start.14) | collective-permute-done | bytes 131104 | tf_op jit(solution)/shard_map/ppermute | solution.py:20
  42.4 0.0 collective-permute-done.15.own3
  42.4 2.0 %collective-permute-done.16.far1 = bf16[8,8192]{1,0:T(8,128)(2,1)S(1)} collective-permute-done((bf16[8,8192]{1,0:T(8,128)(2,1)S(1)}, bf16[8,8192]{1,0:T(8,128)(2,1)S(1)}, u32[]{:S(2)}, u32[]{:S(2)}) %collective-permute-start.16) | collective-permute-done | bytes 131104 | tf_op jit(solution)/shard_map/ppermute | solution.py:20
  44.5 0.1 sums.1
  44.6 1.8 %collective-permute-start.17 = (bf16[8,8192]{1,0:T(8,128)(2,1)S(1)}, bf16[8,8192]{1,0:T(8,128)(2,1)S(1)}, u32[]{:S(2)}, u32[]{:S(2)}) collective-permute-start(bf16[8,8192]{1,0:T(8,128)(2,1)S(1)} %get-tuple-element.41), channel_id=1, source_target_pairs={{0,4},{1,5},{2,6},{3,7},{4,0},{5,1},{6,2},{7,3},{8,12},{9,13},{10,... | collective-permute-start | bytes 393224 | tf_op jit(solution)/shard_map/ppermute | solution.py:20
  46.3 0.2 collective-permute-start.18
  46.5 0.0 collective-permute-done.19
  46.5 1.5 %collective-permute-start.20 = (bf16[8,8192]{1,0:T(8,128)(2,1)S(1)}, bf16[8,8192]{1,0:T(8,128)(2,1)S(1)}, u32[]{:S(2)}, u32[]{:S(2)}) collective-permute-start(bf16[8,8192]{1,0:T(8,128)(2,1)S(1)} %add_convert_fusion.1), channel_id=1, source_target_pairs={{0,1},{1,0},{2,3},{3,2},{4,5},{5,4},{6,7},{7,6},{8,9},{9,8},{10,11... | collective-permute-start | bytes 393224 | tf_op jit(solution)/shard_map/ppermute | solution.py:20
  48.1 5.1 %collective-permute-done.17 = bf16[8,8192]{1,0:T(8,128)(2,1)S(1)} collective-permute-done((bf16[8,8192]{1,0:T(8,128)(2,1)S(1)}, bf16[8,8192]{1,0:T(8,128)(2,1)S(1)}, u32[]{:S(2)}, u32[]{:S(2)}) %collective-permute-start.17) | collective-permute-done | bytes 131104 | tf_op jit(solution)/shard_map/ppermute | solution.py:20
  53.1 0.1 collective-permute-done.18
  53.2 0.0 collective-permute-done.20
  53.2 0.7 %add_convert_fusion = bf16[8,8192]{1,0:T(8,128)(2,1)} fusion(bf16[8,8192]{1,0:T(8,128)(2,1)S(1)} %collective-permute-done.20, bf16[8,8192]{1,0:T(8,128)(2,1)S(1)} %collective-permute-done.18, f32[8,8192]{1,0:T(8,128)S(1)} %get-tuple-element.35, bf16[8,8192]{1,0:T(8,128)(2,1)S(1)} %collective-permute-done.17, bf16[8,8192]{1,0:T(8,128)(2,1)S(1)} %copy-done), kind=kLoop, calls=%fused_computation | loop fusion | flops 589824 | bytes 917504 | tf_op jit(solution)/shard_map/convert_element_type | solution.py:216
  (3 shorter events, 0.1 us)
Async XLA Ops:
  0.0 10.9 %collective-permute-start.2 = (bf16[8,8192]{1,0:T(8,128)(2,1)}, bf16[8,8192]{1,0:T(8,128)(2,1)S(1)}, u32[]{:S(2)}, u32[]{:S(2)}) collective-permute-start(bf16[8,8192]{1,0:T(8,128)(2,1)} %refs_0_.5), channel_id=1, source_target_pairs={{0,4},{1,5},{2,6},{3,7},{4,0},{5,1},{6,2},{7,3},{8,12},{9,13},{10,... | collective-permute-start | bytes 393224 | tf_op jit(solution)/shard_map/ppermute | solution.py:20
  4.0 6.8 %collective-permute-start = (bf16[8,8192]{1,0:T(8,128)(2,1)}, bf16[8,8192]{1,0:T(8,128)(2,1)S(1)}, u32[]{:S(2)}, u32[]{:S(2)}) collective-permute-start(bf16[8,8192]{1,0:T(8,128)(2,1)} %refs_0_.5), channel_id=1, source_target_pairs={{0,1},{1,0},{2,3},{3,2},{4,5},{5,4},{6,7},{7,6},{8,9},{9,8},{10,11... | collective-permute-start | bytes 393224 | tf_op jit(solution)/shard_map/ppermute | solution.py:20
  5.6 6.5 %collective-permute-start.1 = (bf16[8,8192]{1,0:T(8,128)(2,1)}, bf16[8,8192]{1,0:T(8,128)(2,1)S(1)}, u32[]{:S(2)}, u32[]{:S(2)}) collective-permute-start(bf16[8,8192]{1,0:T(8,128)(2,1)} %refs_0_.5), channel_id=1, source_target_pairs={{0,2},{1,3},{2,0},{3,1},{4,6},{5,7},{6,4},{7,5},{8,10},{9,11},{10,... | collective-permute-start | bytes 393224 | tf_op jit(solution)/shard_map/ppermute | solution.py:20
  12.1 10.1 %collective-permute-start.5 = (bf16[8,8192]{1,0:T(8,128)(2,1)S(1)}, bf16[8,8192]{1,0:T(8,128)(2,1)S(1)}, u32[]{:S(2)}, u32[]{:S(2)}) collective-permute-start(bf16[8,8192]{1,0:T(8,128)(2,1)S(1)} %get-tuple-element.45), channel_id=1, source_target_pairs={{0,2},{1,3},{2,0},{3,1},{4,6},{5,7},{6,4},{7,5},{8,10},{9,11},{10,... | collective-permute-start | bytes 393224 | tf_op jit(solution)/shard_map/ppermute | solution.py:20
  12.4 9.8 %collective-permute-start.6 = (bf16[8,8192]{1,0:T(8,128)(2,1)S(1)}, bf16[8,8192]{1,0:T(8,128)(2,1)S(1)}, u32[]{:S(2)}, u32[]{:S(2)}) collective-permute-start(bf16[8,8192]{1,0:T(8,128)(2,1)S(1)} %get-tuple-element.45), channel_id=1, source_target_pairs={{0,1},{1,0},{2,3},{3,2},{4,5},{5,4},{6,7},{7,6},{8,9},{9,8},{10,11... | collective-permute-start | bytes 393224 | tf_op jit(solution)/shard_map/ppermute | solution.py:20
  13.9 8.3 %collective-permute-start.3 = (bf16[8,8192]{1,0:T(8,128)(2,1)S(1)}, bf16[8,8192]{1,0:T(8,128)(2,1)S(1)}, u32[]{:S(2)}, u32[]{:S(2)}) collective-permute-start(bf16[8,8192]{1,0:T(8,128)(2,1)S(1)} %get-tuple-element.47), channel_id=1, source_target_pairs={{0,6},{1,7},{2,4},{3,5},{4,2},{5,3},{6,0},{7,1},{8,14},{9,15},{10,... | collective-permute-start | bytes 393224 | tf_op jit(solution)/shard_map/ppermute | solution.py:20
  15.8 6.6 %copy-start = (bf16[8,8192]{1,0:T(8,128)(2,1)S(1)}, bf16[8,8192]{1,0:T(8,128)(2,1)}, u32[]{:S(2)}) copy-start(bf16[8,8192]{1,0:T(8,128)(2,1)} %refs_0_.5) | copy-start | bytes 393220
  15.8 9.3 %copy-start.1 = (f32[8192]{0:T(1024)S(1)}, f32[8192]{0:T(1024)}, u32[]{:S(2)}) copy-start(f32[8192]{0:T(1024)} %param.6) | copy-start | bytes 98308
  15.8 6.4 %collective-permute-start.4 = (bf16[8,8192]{1,0:T(8,128)(2,1)S(1)}, bf16[8,8192]{1,0:T(8,128)(2,1)S(1)}, u32[]{:S(2)}, u32[]{:S(2)}) collective-permute-start(bf16[8,8192]{1,0:T(8,128)(2,1)S(1)} %get-tuple-element.46), channel_id=1, source_target_pairs={{0,1},{1,0},{2,3},{3,2},{4,5},{5,4},{6,7},{7,6},{8,9},{9,8},{10,11... | collective-permute-start | bytes 393224 | tf_op jit(solution)/shard_map/ppermute | solution.py:20
  22.2 9.0 %slice-start = ((s8[14680064]{0:T(1024)(128)(4,1)}), s8[4194304]{0:T(1024)(128)(4,1)S(1)}, s32[]{:S(2)}) async-start(s8[14680064]{0:T(1024)(128)(4,1)} %bitcast.1), calls=%async_computation | async-start | bytes 8388608
  22.3 2.7 %collective-permute-start.11 = (bf16[32,8192]{1,0:T(8,128)(2,1)S(1)}, bf16[32,8192]{1,0:T(8,128)(2,1)S(1)}, u32[]{:S(2)}, u32[]{:S(2)}) collective-permute-start(bf16[32,8192]{1,0:T(8,128)(2,1)S(1)} %join.1), channel_id=1, source_target_pairs={{0,8},{8,0},{1,9},{9,1},{2,10},{10,2},{3,11},{11,3},{4,12},{12,4},... | collective-permute-start | bytes 1572872 | tf_op jit(solution)/shard_map/ppermute | solution.py:20
  22.4 2.1 %collective-permute-start.7 = (bf16[8,8192]{1,0:T(8,128)(2,1)S(1)}, bf16[8,8192]{1,0:T(8,128)(2,1)S(1)}, u32[]{:S(2)}, u32[]{:S(2)}) collective-permute-start(bf16[8,8192]{1,0:T(8,128)(2,1)S(1)} %copy-done), channel_id=1, source_target_pairs={{0,8},{8,0},{1,9},{9,1},{2,10},{10,2},{3,11},{11,3},{4,12},{12,4},... | collective-permute-start | bytes 393224 | tf_op jit(solution)/shard_map/ppermute | solution.py:20
  22.9 1.8 %collective-permute-start.10 = (bf16[8,8192]{1,0:T(8,128)(2,1)S(1)}, bf16[8,8192]{1,0:T(8,128)(2,1)S(1)}, u32[]{:S(2)}, u32[]{:S(2)}) collective-permute-start(bf16[8,8192]{1,0:T(8,128)(2,1)S(1)} %collective-permute-done.2.refs_2_.refs_3_), channel_id=1, source_target_pairs={{0,8},{8,0},{1,9},{9,1},{2,10},{10,2},{3,11},{11,3},{4,12},{12,4},... | collective-permute-start | bytes 393224 | tf_op jit(solution)/shard_map/ppermute | solution.py:20
  23.0 1.9 %collective-permute-start.8 = (bf16[8,8192]{1,0:T(8,128)(2,1)S(1)}, bf16[8,8192]{1,0:T(8,128)(2,1)S(1)}, u32[]{:S(2)}, u32[]{:S(2)}) collective-permute-start(bf16[8,8192]{1,0:T(8,128)(2,1)S(1)} %collective-permute-done.refs_1_), channel_id=1, source_target_pairs={{0,8},{8,0},{1,9},{9,1},{2,10},{10,2},{3,11},{11,3},{4,12},{12,4},... | collective-permute-start | bytes 393224 | tf_op jit(solution)/shard_map/ppermute | solution.py:20
  23.4 1.6 %collective-permute-start.9 = (bf16[8,8192]{1,0:T(8,128)(2,1)S(1)}, bf16[8,8192]{1,0:T(8,128)(2,1)S(1)}, u32[]{:S(2)}, u32[]{:S(2)}) collective-permute-start(bf16[8,8192]{1,0:T(8,128)(2,1)S(1)} %collective-permute-done.1.refs_2_), channel_id=1, source_target_pairs={{0,8},{8,0},{1,9},{9,1},{2,10},{10,2},{3,11},{11,3},{4,12},{12,4},... | collective-permute-start | bytes 393224 | tf_op jit(solution)/shard_map/ppermute | solution.py:20
  25.1 6.2 %slice-start.1 = ((s8[14680064]{0:T(1024)(128)(4,1)}), s8[4194304]{0:T(1024)(128)(4,1)S(1)}, s32[]{:S(2)}) async-start(s8[14680064]{0:T(1024)(128)(4,1)} %bitcast.1), calls=%async_computation.1 | async-start | bytes 8388608
  25.1 6.2 %slice-start.2 = ((s8[14680064]{0:T(1024)(128)(4,1)}), s8[4194304]{0:T(1024)(128)(4,1)S(1)}, s32[]{:S(2)}) async-start(s8[14680064]{0:T(1024)(128)(4,1)} %bitcast.1), calls=%async_computation.2 | async-start | bytes 8388608
  25.1 6.2 %slice-start.3 = ((s8[14680064]{0:T(1024)(128)(4,1)}), s8[2097152]{0:T(1024)(128)(4,1)S(1)}, s32[]{:S(2)}) async-start(s8[14680064]{0:T(1024)(128)(4,1)} %bitcast.1), calls=%async_computation.3 | async-start | bytes 4194304
  33.1 2.7 %collective-permute-start.12 = (bf16[64,6144]{1,0:T(8,128)(2,1)S(1)}, bf16[64,6144]{1,0:T(8,128)(2,1)S(1)}, u32[]{:S(2)}, u32[]{:S(2)}) collective-permute-start(bf16[64,6144]{1,0:T(8,128)(2,1)S(1)} %get-tuple-element.33), channel_id=1, source_target_pairs={{0,8},{8,0},{1,9},{9,1},{2,10},{10,2},{3,11},{11,3},{4,12},{12,4},... | collective-permute-start | bytes 2359304 | tf_op jit(solution)/shard_map/ppermute | solution.py:20
  34.1 1.8 %collective-permute-start.13 = (bf16[64,2048]{1,0:T(8,128)(2,1)S(1)}, bf16[64,2048]{1,0:T(8,128)(2,1)S(1)}, u32[]{:S(2)}, u32[]{:S(2)}) collective-permute-start(bf16[64,2048]{1,0:T(8,128)(2,1)S(1)} %get-tuple-element.34), channel_id=1, source_target_pairs={{0,8},{8,0},{1,9},{9,1},{2,10},{10,2},{3,11},{11,3},{4,12},{12,4},... | collective-permute-start | bytes 786440 | tf_op jit(solution)/shard_map/ppermute | solution.py:20
  36.0 6.4 %collective-permute-start.14 = (bf16[8,8192]{1,0:T(8,128)(2,1)S(1)}, bf16[8,8192]{1,0:T(8,128)(2,1)S(1)}, u32[]{:S(2)}, u32[]{:S(2)}) collective-permute-start(bf16[8,8192]{1,0:T(8,128)(2,1)S(1)} %get-tuple-element.37), channel_id=1, source_target_pairs={{0,1},{1,0},{2,3},{3,2},{4,5},{5,4},{6,7},{7,6},{8,9},{9,8},{10,11... | collective-permute-start | bytes 393224 | tf_op jit(solution)/shard_map/ppermute | solution.py:20
  36.9 5.5 %collective-permute-start.15 = (bf16[8,8192]{1,0:T(8,128)(2,1)S(1)}, bf16[8,8192]{1,0:T(8,128)(2,1)S(1)}, u32[]{:S(2)}, u32[]{:S(2)}) collective-permute-start(bf16[8,8192]{1,0:T(8,128)(2,1)S(1)} %get-tuple-element.38), channel_id=1, source_target_pairs={{0,2},{1,3},{2,0},{3,1},{4,6},{5,7},{6,4},{7,5},{8,10},{9,11},{10,... | collective-permute-start | bytes 393224 | tf_op jit(solution)/shard_map/ppermute | solution.py:20
  38.0 6.5 %collective-permute-start.16 = (bf16[8,8192]{1,0:T(8,128)(2,1)S(1)}, bf16[8,8192]{1,0:T(8,128)(2,1)S(1)}, u32[]{:S(2)}, u32[]{:S(2)}) collective-permute-start(bf16[8,8192]{1,0:T(8,128)(2,1)S(1)} %get-tuple-element.40), channel_id=1, source_target_pairs={{0,1},{1,0},{2,3},{3,2},{4,5},{5,4},{6,7},{7,6},{8,9},{9,8},{10,11... | collective-permute-start | bytes 393224 | tf_op jit(solution)/shard_map/ppermute | solution.py:20
  39.2 7.3 %collective-permute-start.19 = (bf16[8,8192]{1,0:T(8,128)(2,1)S(1)}, bf16[8,8192]{1,0:T(8,128)(2,1)S(1)}, u32[]{:S(2)}, u32[]{:S(2)}) collective-permute-start(bf16[8,8192]{1,0:T(8,128)(2,1)S(1)} %get-tuple-element.44), channel_id=1, source_target_pairs={{0,6},{1,7},{2,4},{3,5},{4,2},{5,3},{6,0},{7,1},{8,14},{9,15},{10,... | collective-permute-start | bytes 393224 | tf_op jit(solution)/shard_map/ppermute | solution.py:20
  44.6 8.6 %collective-permute-start.17 = (bf16[8,8192]{1,0:T(8,128)(2,1)S(1)}, bf16[8,8192]{1,0:T(8,128)(2,1)S(1)}, u32[]{:S(2)}, u32[]{:S(2)}) collective-permute-start(bf16[8,8192]{1,0:T(8,128)(2,1)S(1)} %get-tuple-element.41), channel_id=1, source_target_pairs={{0,4},{1,5},{2,6},{3,7},{4,0},{5,1},{6,2},{7,3},{8,12},{9,13},{10,... | collective-permute-start | bytes 393224 | tf_op jit(solution)/shard_map/ppermute | solution.py:20
  46.3 6.9 %collective-permute-start.18 = (bf16[8,8192]{1,0:T(8,128)(2,1)S(1)}, bf16[8,8192]{1,0:T(8,128)(2,1)S(1)}, u32[]{:S(2)}, u32[]{:S(2)}) collective-permute-start(bf16[8,8192]{1,0:T(8,128)(2,1)S(1)} %get-tuple-element.42), channel_id=1, source_target_pairs={{0,2},{1,3},{2,0},{3,1},{4,6},{5,7},{6,4},{7,5},{8,10},{9,11},{10,... | collective-permute-start | bytes 393224 | tf_op jit(solution)/shard_map/ppermute | solution.py:20
  46.5 6.7 %collective-permute-start.20 = (bf16[8,8192]{1,0:T(8,128)(2,1)S(1)}, bf16[8,8192]{1,0:T(8,128)(2,1)S(1)}, u32[]{:S(2)}, u32[]{:S(2)}) collective-permute-start(bf16[8,8192]{1,0:T(8,128)(2,1)S(1)} %add_convert_fusion.1), channel_id=1, source_target_pairs={{0,1},{1,0},{2,3},{3,2},{4,5},{5,4},{6,7},{7,6},{8,9},{9,8},{10,11... | collective-permute-start | bytes 393224 | tf_op jit(solution)/shard_map/ppermute | solution.py:20
